TPU v7x, 32 devices: a whole 2x2x4 slice. The times are simulated.
32 devices in a mesh: dp: 8 (over z, y), row: 2 (over x), col: 2 (over core).
Axes of the slice: x: 2, y: 2, z: 4, core: 2. Of those that a mesh axis runs over, the one named last changes fastest.
Arguments:
- images: bfloat16 [128, 14, 14, 256], P('dp', 'row', 'col'), may hold values from -6 to 6
- cotangent: bfloat16 [128, 14, 14, 256], P('dp', 'row', 'col'), may hold values from -6 to 6
- mix_partner: int32 [128], replicated, may hold values from 0 to 127, as said below
- cut_partner: int32 [128], replicated, may hold values from 0 to 127, as said below
- ratios: float32 [128], P('dp'), may hold values from 0.3 to 0.9
- corners: int32 [128, 4], P('dp'), may hold values from 0 to 13, as said below
- drop_masks: int32 [128, 4], P('dp'), may hold values 0 or 1
- norm_gains: float32 [2, 2, 256], replicated, may hold values from 0.25 to 1.75
- norm_shifts: float32 [2, 2, 256], replicated, may hold values from -2 to 2
- entry_weight: bfloat16 [2, 256, 768], replicated, may hold values from -0.5 to 0.5
- entry_bias: float32 [2, 512], replicated, may hold values from -3 to 3
- position_kernel: float32 [2, 3, 3, 256], replicated, may hold values from -2 to 2
- position_bias: float32 [2, 256], replicated, may hold values from -2 to 2
- exit_weight: bfloat16 [2, 256, 256], replicated, may hold values from -0.5 to 0.5
- exit_bias: float32 [2, 256], replicated, may hold values from -2 to 2
- expand_weight: bfloat16 [2, 256, 1024], replicated, may hold values from -0.375 to 0.375
- expand_bias: float32 [2, 1024], replicated, may hold values from -2 to 2
- shrink_weight: bfloat16 [2, 1024, 256], replicated, may hold values from -0.25 to 0.25
- shrink_bias: float32 [2, 256], replicated, may hold values from -2 to 2
Outputs:
- activations: bfloat16 [128, 14, 14, 256], P('dp', 'row', 'col')
- input_gradient: float32 [128, 14, 14, 256], P('dp', 'row', 'col')
- norm_gains_gradient: float32 [2, 2, 256], replicated
- norm_shifts_gradient: float32 [2, 2, 256], replicated
- entry_weight_gradient: float32 [2, 256, 768], replicated
- entry_bias_gradient: float32 [2, 512], replicated
- position_kernel_gradient: float32 [2, 3, 3, 256], replicated
- position_bias_gradient: float32 [2, 256], replicated
- exit_weight_gradient: float32 [2, 256, 256], replicated
- exit_bias_gradient: float32 [2, 256], replicated
- expand_weight_gradient: float32 [2, 256, 1024], replicated
- expand_bias_gradient: float32 [2, 1024], replicated
- shrink_weight_gradient: float32 [2, 1024, 256], replicated
- shrink_bias_gradient: float32 [2, 256], replicated
Inputs may be any that keep to these rules, and one draw needn't show every extreme that they name: `mix_partner`: of the 32 mixup and cutmix partners of the images of one index of dp, at most 4 lie on any one index of dp, and in every draw some pair of indices reaches 4. `cut_partner`: counted with mix_partner in its bound. `corners`: each box spans 4 to 6 rows and 4 to 6 columns, bottom and right exclusive.
All inputs are finite; a program needn't handle non-finite values. No bound on the sum of `drop_masks` on one device may be relied on, other than what follows from the above.
Results may differ from a plain program's by a relative error of at most 0.017.
Values may be sent and summed in bfloat16 or wider, within the bound.
No kernel may reach another device: no remote copies, remote signals or barrier semaphores. Data moves between devices by JAX's collectives and lax.ppermute only.
A program may use at most 128 MiB of HBM per device.

v0:
```python
import jax
import jax.numpy as jnp
from jax import lax
from jax.sharding import PartitionSpec as P

HEADS = 8
TILE = 7
HEAD_DIM = 32


def norm_rows(values, scale_by, shift_by):
    centre = jnp.mean(values, axis=-1, keepdims=True)
    centered = values - centre
    variance = jnp.mean(centered * centered, axis=-1, keepdims=True)
    return centered * lax.rsqrt(variance + 1e-05) * scale_by + shift_by


def exact_gelu(values):
    return jax.nn.gelu(values, approximate=False)


def head_rows(tensor):
    return tensor.reshape(tensor.shape[0], -1, HEADS // 2, HEAD_DIM)


def stripe_scores(queries, key_full):
    return jnp.einsum(
        "bqhd,bkhd->bhqk",
        head_rows(queries),
        head_rows(key_full),
        preferred_element_type=jnp.float32,
    ) * HEAD_DIM ** (-0.5)


def stripe_attend(queries, key_full, value_full):
    scores = stripe_scores(queries, key_full)
    row_max = jnp.max(scores, axis=-1, keepdims=True)
    lifted = jnp.exp(scores - row_max)
    totals = jnp.sum(lifted, axis=-1, keepdims=True)
    chances = (lifted / totals).astype(jnp.bfloat16)
    output = jnp.einsum(
        "bhqk,bkhd->bqhd", chances, head_rows(value_full), preferred_element_type=jnp.float32
    )
    return (output.reshape(queries.shape), row_max + jnp.log(totals))


def stripe_backward(queries, key_full, value_full, log_total, out_delta):
    chances = jnp.exp(stripe_scores(queries, key_full) - log_total)
    out_rows = head_rows(out_delta)
    chance_delta = jnp.einsum(
        "bqhd,bkhd->bhqk", out_rows, head_rows(value_full), preferred_element_type=jnp.float32
    )
    values_delta = jnp.einsum(
        "bhqk,bqhd->bkhd",
        chances.astype(jnp.bfloat16),
        out_rows,
        preferred_element_type=jnp.float32,
    )
    score_delta = (
        chances * (chance_delta - jnp.sum(chances * chance_delta, axis=-1, keepdims=True))
    ).astype(jnp.bfloat16)
    query_delta = jnp.einsum(
        "bhqk,bkhd->bqhd", score_delta, head_rows(key_full), preferred_element_type=jnp.float32
    ) * HEAD_DIM ** (-0.5)
    keys_delta = jnp.einsum(
        "bhqk,bqhd->bkhd", score_delta, head_rows(queries), preferred_element_type=jnp.float32
    ) * HEAD_DIM ** (-0.5)
    return (
        query_delta.reshape(queries.shape),
        keys_delta.reshape(key_full.shape),
        values_delta.reshape(value_full.shape),
    )


def pad_window(values):
    return jnp.pad(values, ((0, 0), (1, 1), (1, 1), (0, 0)))


def region_take(value_full, start_at, slice_axis):
    return lax.dynamic_slice_in_dim(pad_window(value_full), start_at, TILE + 2, slice_axis)


def region_apply(region, kernel, bias_row):
    height = region.shape[1] - 2
    breadth = region.shape[2] - 2
    result = bias_row
    for row_step in range(3):
        for col_step in range(3):
            result = (
                result
                + kernel[row_step, col_step]
                * region[:, row_step : row_step + height, col_step : col_step + breadth]
            )
    return result


def region_backward(region, kernel, out_delta):
    height = out_delta.shape[1]
    breadth = out_delta.shape[2]
    output_wide = out_delta.astype(jnp.float32)
    region_wide = region.astype(jnp.float32)
    region_delta = jnp.zeros(region.shape, jnp.float32)
    kernel_rows = []
    for row_step in range(3):
        kernel_cols = []
        for col_step in range(3):
            window = region_wide[:, row_step : row_step + height, col_step : col_step + breadth]
            kernel_cols.append(jnp.sum(output_wide * window, axis=(0, 1, 2)))
            region_delta = region_delta + jnp.pad(
                kernel[row_step, col_step] * output_wide,
                ((0, 0), (row_step, 2 - row_step), (col_step, 2 - col_step), (0, 0)),
            )
        kernel_rows.append(jnp.stack(kernel_cols))
    return (jnp.stack(kernel_rows), jnp.sum(output_wide, axis=(0, 1, 2)), region_delta)


def region_return(region_delta, start_at, slice_axis, full_shape):
    padded_shape = (full_shape[0], full_shape[1] + 2, full_shape[2] + 2, full_shape[3])
    placed = lax.dynamic_update_slice_in_dim(
        jnp.zeros(padded_shape, jnp.float32), region_delta, start_at, slice_axis
    )
    return placed[:, 1:-1, 1:-1]


def block_forward(hidden, block_index, weights, scales, row_start, col_start):
    (
        norm_gains,
        norm_shifts,
        entry_weight,
        entry_bias,
        position_kernel,
        position_bias,
        exit_weight,
        exit_bias,
        expand_weight,
        expand_bias,
        shrink_weight,
        shrink_bias,
    ) = weights
    images_here, tokens_here, channels = hidden.shape
    channel_half = channels // 2
    side = TILE
    normed = norm_rows(hidden, norm_gains[block_index, 0], norm_shifts[block_index, 0]).astype(
        jnp.bfloat16
    )
    full_bias = jnp.concatenate(
        [
            entry_bias[block_index, :channels],
            jnp.zeros((channels,), jnp.float32),
            entry_bias[block_index, channels:],
        ]
    )
    triple = (
        jnp.dot(normed, entry_weight[block_index], preferred_element_type=jnp.float32) + full_bias
    ).astype(jnp.bfloat16)
    triple = triple.reshape(images_here, side, side, 3 * channels)
    queries = triple[..., :channels]
    key_local = triple[..., channels : 2 * channels]
    value_local = triple[..., 2 * channels :]
    kernel_here = position_kernel[block_index]
    bias_here = position_bias[block_index]
    across_query = queries[..., :channel_half]
    down_query = queries[..., channel_half:]
    across_keys, across_values = (
        lax.all_gather(key_local[..., :channel_half], "col", axis=2, tiled=True),
        lax.all_gather(value_local[..., :channel_half], "col", axis=2, tiled=True),
    )
    down_keys, down_values = (
        lax.all_gather(key_local[..., channel_half:], "row", axis=1, tiled=True),
        lax.all_gather(value_local[..., channel_half:], "row", axis=1, tiled=True),
    )
    across_out, across_total = stripe_attend(across_query, across_keys, across_values)
    down_out, down_total = stripe_attend(down_query, down_keys, down_values)
    across_out = across_out + region_apply(
        region_take(across_values, col_start, 2),
        kernel_here[:, :, :channel_half],
        bias_here[:channel_half],
    )
    down_out = down_out + region_apply(
        region_take(down_values, row_start, 1),
        kernel_here[:, :, channel_half:],
        bias_here[channel_half:],
    )
    stripe_out = (
        jnp.concatenate([across_out, down_out], axis=-1)
        .reshape(images_here, tokens_here, channels)
        .astype(jnp.bfloat16)
    )
    branch = (
        jnp.dot(stripe_out, exit_weight[block_index], preferred_element_type=jnp.float32)
        + exit_bias[block_index]
    )
    midway = hidden + scales[:, 2 * block_index, None, None] * branch
    inner_normed = norm_rows(
        midway, norm_gains[block_index, 1], norm_shifts[block_index, 1]
    ).astype(jnp.bfloat16)
    pre_act = (
        jnp.dot(inner_normed, expand_weight[block_index], preferred_element_type=jnp.float32)
        + expand_bias[block_index]
    )
    activated = exact_gelu(pre_act).astype(jnp.bfloat16)
    feed_out = (
        jnp.dot(activated, shrink_weight[block_index], preferred_element_type=jnp.float32)
        + shrink_bias[block_index]
    )
    output = midway + scales[:, 2 * block_index + 1, None, None] * feed_out
    stored = (
        hidden,
        normed,
        (across_query, down_query),
        key_local,
        value_local,
        (across_keys, across_values, down_keys, down_values),
        across_total,
        down_total,
        stripe_out,
        midway,
        inner_normed,
        pre_act,
        activated,
    )
    return (output, stored)


def block_backward(gradient, block_index, weights, scales, stored, row_start, col_start):
    (
        norm_gains,
        norm_shifts,
        entry_weight,
        entry_bias,
        position_kernel,
        position_bias,
        exit_weight,
        exit_bias,
        expand_weight,
        expand_bias,
        shrink_weight,
        shrink_bias,
    ) = weights
    (
        hidden,
        normed,
        query_parts,
        key_local,
        value_local,
        gathered,
        across_total,
        down_total,
        stripe_out,
        midway,
        inner_normed,
        pre_act,
        activated,
    ) = stored
    across_keys, across_values, down_keys, down_values = gathered
    images_here, tokens_here, channels = hidden.shape
    channel_half = channels // 2
    side = TILE
    kernel_here = position_kernel[block_index]
    feed_delta = (gradient * scales[:, 2 * block_index + 1, None, None]).astype(jnp.bfloat16)
    shrink_total = jnp.einsum(
        "btf,btd->fd", activated, feed_delta, preferred_element_type=jnp.float32
    )
    shrink_offset = jnp.sum(feed_delta.astype(jnp.float32), axis=(0, 1))
    act_delta = jnp.einsum(
        "btd,fd->btf", feed_delta, shrink_weight[block_index], preferred_element_type=jnp.float32
    )
    _, gelu_back = jax.vjp(exact_gelu, pre_act)
    pre_delta = gelu_back(act_delta)[0].astype(jnp.bfloat16)
    expand_total = jnp.einsum(
        "btd,btf->df", inner_normed, pre_delta, preferred_element_type=jnp.float32
    )
    expand_offset = jnp.sum(pre_delta.astype(jnp.float32), axis=(0, 1))
    inner_delta = jnp.einsum(
        "btf,df->btd", pre_delta, expand_weight[block_index], preferred_element_type=jnp.float32
    )
    _, norm_back = jax.vjp(
        norm_rows, midway, norm_gains[block_index, 1], norm_shifts[block_index, 1]
    )
    midway_part, late_gain, late_shift = norm_back(inner_delta)
    gradient = gradient + midway_part
    branch_delta = (gradient * scales[:, 2 * block_index, None, None]).astype(jnp.bfloat16)
    exit_total = jnp.einsum(
        "btd,bte->de", stripe_out, branch_delta, preferred_element_type=jnp.float32
    )
    exit_offset = jnp.sum(branch_delta.astype(jnp.float32), axis=(0, 1))
    stripe_delta = (
        jnp.einsum(
            "bte,de->btd",
            branch_delta,
            exit_weight[block_index],
            preferred_element_type=jnp.float32,
        )
        .astype(jnp.bfloat16)
        .reshape(images_here, side, side, channels)
    )
    across_delta = stripe_delta[..., :channel_half]
    down_delta = stripe_delta[..., channel_half:]
    query_across, keys_across, values_across = stripe_backward(
        query_parts[0], across_keys, across_values, across_total, across_delta
    )
    query_down, keys_down, values_down = stripe_backward(
        query_parts[1], down_keys, down_values, down_total, down_delta
    )
    kernel_across, bias_across, region_across = region_backward(
        region_take(across_values, col_start, 2), kernel_here[:, :, :channel_half], across_delta
    )
    kernel_down, bias_down, region_down = region_backward(
        region_take(down_values, row_start, 1), kernel_here[:, :, channel_half:], down_delta
    )
    values_across = values_across + region_return(region_across, col_start, 2, across_values.shape)
    values_down = values_down + region_return(region_down, row_start, 1, down_values.shape)
    keys_across, values_across = (
        lax.psum_scatter(
            keys_across.astype(jnp.bfloat16), "col", scatter_dimension=2, tiled=True
        ).astype(jnp.float32),
        lax.psum_scatter(
            values_across.astype(jnp.bfloat16), "col", scatter_dimension=2, tiled=True
        ).astype(jnp.float32),
    )
    keys_down, values_down = (
        lax.psum_scatter(
            keys_down.astype(jnp.bfloat16), "row", scatter_dimension=1, tiled=True
        ).astype(jnp.float32),
        lax.psum_scatter(
            values_down.astype(jnp.bfloat16), "row", scatter_dimension=1, tiled=True
        ).astype(jnp.float32),
    )
    triple_delta = (
        jnp.concatenate(
            [query_across, query_down, keys_across, keys_down, values_across, values_down], axis=-1
        )
        .astype(jnp.bfloat16)
        .reshape(images_here, tokens_here, 3 * channels)
    )
    entry_total = jnp.einsum(
        "btd,bte->de", normed, triple_delta, preferred_element_type=jnp.float32
    )
    triple_sums = jnp.sum(triple_delta.astype(jnp.float32), axis=(0, 1))
    entry_offset = jnp.concatenate([triple_sums[:channels], triple_sums[2 * channels :]])
    normed_delta = jnp.einsum(
        "bte,de->btd", triple_delta, entry_weight[block_index], preferred_element_type=jnp.float32
    )
    _, norm_first = jax.vjp(
        norm_rows, hidden, norm_gains[block_index, 0], norm_shifts[block_index, 0]
    )
    hidden_part, early_gain, early_shift = norm_first(normed_delta)
    gradient = gradient + hidden_part
    pieces = (
        jnp.stack([early_gain, late_gain]),
        jnp.stack([early_shift, late_shift]),
        entry_total,
        entry_offset,
        jnp.concatenate([kernel_across, kernel_down], axis=-1),
        jnp.concatenate([bias_across, bias_down]),
        exit_total,
        exit_offset,
        expand_total,
        expand_offset,
        shrink_total,
        shrink_offset,
    )
    return (gradient, pieces)


def partner_plan(mix_partner, cut_partner, images_here, groups, device):
    requests = jnp.concatenate(
        [mix_partner.reshape(groups, images_here), cut_partner.reshape(groups, images_here)], axis=1
    )
    owners = requests // images_here
    within = requests % images_here
    wanted = 2 * images_here
    before = jnp.arange(wanted)[None, :] < jnp.arange(wanted)[:, None]
    slot_rank = jnp.sum((owners[:, :, None] == owners[:, None, :]) & before[None], axis=2)
    capacity = (wanted + groups - 1) // groups
    slot_ids = jnp.arange(capacity)
    chosen = (
        (owners == device)[:, :, None] & (slot_rank[:, :, None] == slot_ids[None, None, :])
    ).astype(jnp.float32)
    local_hot = (within[:, :, None] == jnp.arange(images_here)[None, None, :]).astype(jnp.float32)
    pick_table = jnp.einsum("gjk,gjb->gkb", chosen, local_hot, precision=lax.Precision.HIGHEST)
    my_owner = lax.dynamic_index_in_dim(owners, device, 0, keepdims=False)
    my_rank = lax.dynamic_index_in_dim(slot_rank, device, 0, keepdims=False)
    take_table = (
        (
            (my_owner[:, None, None] == jnp.arange(groups)[None, :, None])
            & (my_rank[:, None, None] == slot_ids[None, None, :])
        )
        .astype(jnp.float32)
        .reshape(wanted, groups * capacity)
    )
    return (pick_table, take_table, capacity)


def local(
    images,
    cotangent,
    mix_partner,
    cut_partner,
    ratios,
    corners,
    drop_masks,
    norm_gains,
    norm_shifts,
    entry_weight,
    entry_bias,
    position_kernel,
    position_bias,
    exit_weight,
    exit_bias,
    expand_weight,
    expand_bias,
    shrink_weight,
    shrink_bias,
):
    images_here = images.shape[0]
    channels = images.shape[3]
    features = TILE * TILE * channels
    groups = lax.axis_size("dp")
    device = lax.axis_index("dp")
    row_start = lax.axis_index("row") * TILE
    col_start = lax.axis_index("col") * TILE
    pick_table, take_table, capacity = partner_plan(
        mix_partner, cut_partner, images_here, groups, device
    )
    flat_images = images.reshape(images_here, features)
    outgoing = (
        jnp.dot(
            pick_table.reshape(groups * capacity, images_here).astype(jnp.bfloat16),
            flat_images,
            preferred_element_type=jnp.float32,
        )
        .astype(jnp.bfloat16)
        .reshape(groups, capacity, features)
    )
    incoming = lax.all_to_all(outgoing, "dp", split_axis=0, concat_axis=0, tiled=True)
    fetched = jnp.dot(
        take_table.astype(jnp.bfloat16),
        incoming.reshape(groups * capacity, features),
        preferred_element_type=jnp.float32,
    ).reshape(2, images_here, TILE * TILE, channels)
    positions = jnp.arange(TILE)
    row_pos = row_start + positions
    col_pos = col_start + positions
    in_rows = (row_pos[None, :] >= corners[:, 0:1]) & (row_pos[None, :] < corners[:, 1:2])
    in_cols = (col_pos[None, :] >= corners[:, 2:3]) & (col_pos[None, :] < corners[:, 3:4])
    inside = (
        (in_rows[:, :, None] & in_cols[:, None, :])
        .astype(jnp.float32)
        .reshape(images_here, TILE * TILE, 1)
    )
    ratio_here = ratios[:, None, None]
    own_images = images.reshape(images_here, TILE * TILE, channels).astype(jnp.float32)
    mixed_input = inside * fetched[1] + (1.0 - inside) * (
        ratio_here * own_images + (1.0 - ratio_here) * fetched[0]
    )
    scales = drop_masks.astype(jnp.float32) * 1.25
    weights = (
        norm_gains,
        norm_shifts,
        entry_weight,
        entry_bias,
        position_kernel,
        position_bias,
        exit_weight,
        exit_bias,
        expand_weight,
        expand_bias,
        shrink_weight,
        shrink_bias,
    )
    gradient = cotangent.reshape(images_here, TILE * TILE, channels).astype(jnp.float32)
    first_out, first_stored = block_forward(mixed_input, 0, weights, scales, row_start, col_start)
    second_out, second_stored = block_forward(first_out, 1, weights, scales, row_start, col_start)
    rounded_out = second_out.astype(jnp.bfloat16)
    gradient, late_pieces = block_backward(
        gradient, 1, weights, scales, second_stored, row_start, col_start
    )
    gradient, early_pieces = block_backward(
        gradient, 0, weights, scales, first_stored, row_start, col_start
    )
    activations = rounded_out.reshape(images_here, TILE, TILE, channels)
    stacked = [
        jnp.stack([first_piece, second_piece])
        for first_piece, second_piece in zip(early_pieces, late_pieces)
    ]
    (
        gain_sum,
        shift_sum,
        entry_sum,
        entry_offset,
        kernel_sum,
        position_offset,
        exit_sum,
        exit_offset,
        expand_sum,
        expand_offset,
        shrink_sum,
        shrink_offset,
    ) = stacked
    (
        gain_sum,
        shift_sum,
        entry_sum,
        entry_offset,
        kernel_sum,
        position_offset,
        exit_sum,
        exit_offset,
        expand_sum,
        expand_offset,
        shrink_sum,
        shrink_offset,
    ) = lax.psum(
        (
            gain_sum,
            shift_sum,
            entry_sum,
            entry_offset,
            kernel_sum,
            position_offset,
            exit_sum,
            exit_offset,
            expand_sum,
            expand_offset,
            shrink_sum,
            shrink_offset,
        ),
        ("dp", "row", "col"),
    )
    outside_delta = (1.0 - inside) * gradient
    own_delta = ratio_here * outside_delta
    mix_delta = (1.0 - ratio_here) * outside_delta
    cut_delta = inside * gradient
    fetched_delta = jnp.concatenate([mix_delta, cut_delta], axis=0).reshape(
        2 * images_here, features
    )
    slot_delta = jnp.dot(take_table.T, fetched_delta, precision=lax.Precision.HIGHEST).reshape(
        groups, capacity, features
    )
    returned = lax.all_to_all(
        slot_delta.astype(jnp.bfloat16), "dp", split_axis=0, concat_axis=0, tiled=True
    ).astype(slot_delta.dtype)
    input_gradient = own_delta.reshape(images_here, features) + jnp.einsum(
        "gkb,gkf->bf", pick_table, returned, precision=lax.Precision.HIGHEST
    )
    return (
        activations,
        input_gradient.reshape(images_here, TILE, TILE, channels),
        gain_sum,
        shift_sum,
        entry_sum,
        entry_offset,
        kernel_sum,
        position_offset,
        exit_sum,
        exit_offset,
        expand_sum,
        expand_offset,
        shrink_sum,
        shrink_offset,
    )


def solution(mesh):
    return jax.shard_map(
        local,
        mesh=mesh,
        in_specs=(
            P("dp", "row", "col", None),
            P("dp", "row", "col", None),
            P(),
            P(),
            P("dp"),
            P("dp", None),
            P("dp", None),
            P(),
            P(),
            P(),
            P(),
            P(),
            P(),
            P(),
            P(),
            P(),
            P(),
            P(),
            P(),
        ),
        out_specs=(
            P("dp", "row", "col", None),
            P("dp", "row", "col", None),
            P(),
            P(),
            P(),
            P(),
            P(),
            P(),
            P(),
            P(),
            P(),
            P(),
            P(),
            P(),
        ),
        check_vma=False,
    )
```

profile of v0, /device:TPU:0, one launch (start us, length us, event | category | flops | bytes accessed | tf_op | source)
XLA Modules:
  0.0 694.0 jit_solution(16402286723097562728)
XLA Ops:
  13.7 7.3 %all-to-all-start = ((bf16[8,4,12544]{2,1,0:T(4,128)(2,1)}), bf16[8,4,12544]{2,1,0:T(4,128)(2,1)S(1)}, u32[]{:S(2)}, u32[]{:S(2)}) async-start(bf16[8,4,12544]{2,1,0:T(4,128)(2,1)} %reshape.916), calls=%async_computation | async-start | bytes 1605632 | tf_op jit(solution)/shard_map/all_to_all | solution.py:436
  37.1 4.5 all-to-all-done
  88.6 10.8 %all_gather.27 = bf16[16,14,7,128]{3,0,2,1:T(8,128)(2,1)} all-gather(bf16[16,7,7,128]{3,0,2,1:T(8,128)(2,1)} %get-tuple-element.176), channel_id=1, replica_groups=mesh['dp'=8,'row'=2,'col'=2] {'row'}, dimensions={1}, use_global_device_ids=true | all-gather | bytes 602112 | tf_op jit(solution)/shard_map/all_gather | solution.py:169
  107.6 8.0 %all_gather.26 = bf16[16,14,7,128]{3,0,2,1:T(8,128)(2,1)} all-gather(bf16[16,7,7,128]{3,0,2,1:T(8,128)(2,1)S(1)} %get-tuple-element.178), channel_id=1, replica_groups=mesh['dp'=8,'row'=2,'col'=2] {'row'}, dimensions={1}, use_global_device_ids=true | all-gather | bytes 602112 | tf_op jit(solution)/shard_map/all_gather | solution.py:170
  139.6 9.5 %multiply_convert_fusion.1 = (bf16[16,49,1024]{2,1,0:T(8,128)(2,1)S(1)}, f32[16,49,1024]{2,1,0:T(8,128)}) fusion(f32[16,49,1024]{2,1,0:T(8,128)S(1)} %get-tuple-element.303, f32[1024]{0:T(1024)S(1)} %bitcast.672, u16[49,1024]{1,0:T(8,128)(2,1)S(1)} %get-tuple-element.73, u16[49,1024]{1,0:T(8,128)(2,1)S(1)} %get-tuple-element.72), kind=kLoop, calls=%fused_computation.35 | loop fusion | flops 56999936 | bytes 8232960 | tf_op jit(solution)/shard_map/convert_element_type | solution.py:201
  160.9 3.7 all_gather.29
  176.3 3.5 copy.253
  196.4 9.8 %all_gather.31 = bf16[16,14,7,128]{3,0,2,1:T(8,128)(2,1)} all-gather(bf16[16,7,7,128]{3,0,2,1:T(8,128)(2,1)} %get-tuple-element.170), channel_id=1, replica_groups=mesh['dp'=8,'row'=2,'col'=2] {'row'}, dimensions={1}, use_global_device_ids=true | all-gather | bytes 602112 | tf_op jit(solution)/shard_map/all_gather | solution.py:169
  209.5 3.5 copy.256
  217.9 9.7 %all_gather.30 = bf16[16,14,7,128]{3,0,2,1:T(8,128)(2,1)} all-gather(bf16[16,7,7,128]{3,0,2,1:T(8,128)(2,1)} %get-tuple-element.172), channel_id=1, replica_groups=mesh['dp'=8,'row'=2,'col'=2] {'row'}, dimensions={1}, use_global_device_ids=true | all-gather | bytes 602112 | tf_op jit(solution)/shard_map/all_gather | solution.py:170
  252.9 9.6 %multiply_convert_fusion = (bf16[16,49,1024]{2,1,0:T(8,128)(2,1)}, f32[16,49,1024]{2,1,0:T(8,128)S(1)}) fusion(f32[16,49,1024]{2,1,0:T(8,128)S(1)} %get-tuple-element.312, f32[1024]{0:T(1024)S(1)} %bitcast.675, u16[49,1024]{1,0:T(8,128)(2,1)S(1)} %get-tuple-element.71, u16[49,1024]{1,0:T(8,128)(2,1)S(1)} %get-tuple-element.70), kind=kLoop, calls=%fused_computation.22 | loop fusion | flops 56999936 | bytes 8232960 | tf_op jit(solution)/shard_map/convert_element_type | solution.py:201
  300.8 3.9 copy.278
  304.8 3.7 reshape.940
  319.8 4.6 fusion.104
  324.3 3.9 copy.276
  328.3 3.6 reshape.939
  358.7 4.1 convolution_bitcast_fusion.2
  406.8 3.5 convolution_bitcast_fusion.7
  440.9 3.9 copy.297
  444.8 3.6 reshape.944
  493.2 5.0 reduce-scatter.23.cloned.1.call-done
  514.0 5.6 all-to-all-start.1
  520.1 50.0 %all-reduce.44 = (f32[2,2,256]{2,1,0:T(2,128)}, f32[2,2,256]{2,1,0:T(2,128)}, f32[2,512]{1,0:T(2,128)}, f32[2,3,3,256]{3,2,1,0:T(4,128)S(1)}, f32[2,256]{1,0:T(2...) all-reduce(f32[2,2,256]{2,1,0:T(2,128)S(1)} %pad_maximum_fusion.11,, ...), channel_id=1, replica_groups=mesh['dp'=8,'row'=2,'col'=2] {'dp','row','col'}, use_global_device_ids=true, to_apply=%region_41.42 | all-reduce | flops 11264 | bytes 90112 | tf_op jit(solution)/shard_map/psum | solution.py:514
  573.5 105.6 %all-reduce.52.cloned.1.call-done = (f32[2,256,768]{2,1,0:T(8,128)}, f32[2,256,256]{2,1,0:T(8,128)}, f32[2,256,1024]{2,1,0:T(8,128)}, f32[2,1024,256]{2,1,0:T(8,128)}) async-done(((f32[2,256,768]{2,1,0:T(8,128)}, f32[2,256,256]{2,1,0:T(8,128)}, f32[2,256,1024]{2,1,0:T(8,128)}, f32[2,1024,256]{2,1,0:T(8,128)}), (f32[2,256,768]{2,1,0:T(8,128)}, f32[2,256,256]{2,1,0:T(8,128)}, f32[2,256,1024]{2,1,0:T(8,128)}, ...) | async-done | bytes 6291472 | tf_op jit(solution)/shard_map/psum | solution.py:514
  (926 shorter events, 392.9 us)
Async XLA Ops:
  13.7 27.8 %all-to-all-start = ((bf16[8,4,12544]{2,1,0:T(4,128)(2,1)}), bf16[8,4,12544]{2,1,0:T(4,128)(2,1)S(1)}, u32[]{:S(2)}, u32[]{:S(2)}) async-start(bf16[8,4,12544]{2,1,0:T(4,128)(2,1)} %reshape.916), calls=%async_computation | async-start | bytes 1605632 | tf_op jit(solution)/shard_map/all_to_all | solution.py:436
  21.0 352.1 %all-reduce.56.cloned.1.call-start = ((), (), s32[]{:S(2)}) async-start(), calls=%async_computation.12 | async-start | bytes 1605632
  23.3 12.6 %copy-start.100 = (bf16[16,7,7,256]{3,0,2,1:T(8,128)(2,1)S(1)}, bf16[16,7,7,256]{3,0,2,1:T(8,128)(2,1)}, u32[]{:S(2)}) copy-start(bf16[16,7,7,256]{3,0,2,1:T(8,128)(2,1)} %param.19) | copy-start | bytes 1204228
  37.1 230.3 %copy-start.31 = (f32[16,49,256]{2,0,1:T(8,128)}, f32[16,49,256]{2,0,1:T(8,128)S(1)}, u32[]{:S(2)}) copy-start(f32[16,49,256]{2,0,1:T(8,128)S(1)} %bitcast_convert_fusion.1) | copy-start | bytes 2408452
  49.0 86.2 %copy-start.7 = (f32[16,49,256]{2,1,0:T(8,128)}, f32[16,49,256]{2,1,0:T(8,128)S(1)}, u32[]{:S(2)}) copy-start(f32[16,49,256]{2,1,0:T(8,128)S(1)} %get-tuple-element.164) | copy-start | bytes 2408452
  136.7 12.4 %copy-start.11 = (f32[16,49,256]{2,1,0:T(8,128)}, f32[16,49,256]{2,1,0:T(8,128)S(1)}, u32[]{:S(2)}) copy-start(f32[16,49,256]{2,1,0:T(8,128)S(1)} %get-tuple-element.302) | copy-start | bytes 2408452
  250.6 16.0 %copy-start.14 = (f32[16,49,256]{2,1,0:T(8,128)}, f32[16,49,256]{2,1,0:T(8,128)S(1)}, u32[]{:S(2)}) copy-start(f32[16,49,256]{2,1,0:T(8,128)S(1)} %get-tuple-element.311) | copy-start | bytes 2408452
  250.6 16.0 %copy-start.133 = (f32[16,49]{1,0:T(8,128)}, f32[16,49]{1,0:T(8,128)S(1)}, u32[]{:S(2)}) copy-start(f32[16,49]{1,0:T(8,128)S(1)} %broadcast_multiply_fusion.1) | copy-start | bytes 9412
  251.0 15.7 %copy-start.145 = (f32[16,49]{1,0:T(8,128)}, f32[16,49]{1,0:T(8,128)S(1)}, u32[]{:S(2)}) copy-start(f32[16,49]{1,0:T(8,128)S(1)} %fusion.171) | copy-start | bytes 9412
  343.5 32.9 %reduce-scatter.17.cloned.1.call-start = ((), (), s32[]{:S(2)}) async-start(), calls=%async_computation.6 | async-start | bytes 602112 | tf_op jit(solution)/shard_map/reduce_scatter | solution.py:322
  350.6 29.2 %reduce-scatter.19.cloned.1.call-start = ((), (), s32[]{:S(2)}) async-start(), calls=%async_computation.7 | async-start | bytes 602112 | tf_op jit(solution)/shard_map/reduce_scatter | solution.py:325
  364.8 16.7 %copy-start.128 = (f32[16,49]{1,0:T(8,128)S(1)}, f32[16,49]{1,0:T(8,128)}, u32[]{:S(2)}) copy-start(f32[16,49]{1,0:T(8,128)} %copy-done.127) | copy-start | bytes 9412
  364.8 123.1 %all-reduce.54.cloned.1.call-start = ((), (), s32[]{:S(2)}) async-start(), calls=%async_computation.11 | async-start | bytes 1605632
  461.8 28.9 %reduce-scatter.21.cloned.1.call-start = ((), (), s32[]{:S(2)}) async-start(), calls=%async_computation.8 | async-start | bytes 602112 | tf_op jit(solution)/shard_map/reduce_scatter | solution.py:322
  467.7 30.5 %reduce-scatter.23.cloned.1.call-start = ((), (), s32[]{:S(2)}) async-start(), calls=%async_computation.9 | async-start | bytes 602112 | tf_op jit(solution)/shard_map/reduce_scatter | solution.py:325
  486.6 13.3 %copy-start.8 = (f32[16,49,256]{2,1,0:T(8,128)S(1)}, f32[16,49,256]{2,1,0:T(8,128)}, u32[]{:S(2)}) copy-start(f32[16,49,256]{2,1,0:T(8,128)} %copy-done.7) | copy-start | bytes 2408452
  486.6 13.3 %copy-start.113 = (f32[16,49]{1,0:T(8,128)S(1)}, f32[16,49]{1,0:T(8,128)}, u32[]{:S(2)}) copy-start(f32[16,49]{1,0:T(8,128)} %copy-done.112) | copy-start | bytes 9412
  486.6 13.3 %copy-start.141 = (f32[16,49]{1,0:T(8,128)S(1)}, f32[16,49]{1,0:T(8,128)}, u32[]{:S(2)}) copy-start(f32[16,49]{1,0:T(8,128)} %copy-done.140) | copy-start | bytes 9412
  486.6 13.3 %copy-start.167 = (f32[1,1,256]{2,1,0:T(1,128)S(1)}, f32[1,1,256]{2,1,0:T(1,128)}, u32[]{:S(2)}) copy-start(f32[1,1,256]{2,1,0:T(1,128)} %copy-done.166) | copy-start | bytes 3076
  486.6 13.3 %copy-start.246 = (f32[1,1,256]{2,1,0:T(1,128)S(1)}, f32[1,1,256]{2,1,0:T(1,128)}, u32[]{:S(2)}) copy-start(f32[1,1,256]{2,1,0:T(1,128)} %copy-done.245) | copy-start | bytes 3076
  486.6 192.5 %all-reduce.52.cloned.1.call-start = ((), (), s32[]{:S(2)}) async-start(), calls=%async_computation.10 | async-start | bytes 12582912 | tf_op jit(solution)/shard_map/psum | solution.py:514
  512.8 57.9 %copy-start.53 = (f32[16,49,256]{2,1,0:T(8,128)S(1)}, f32[16,49,256]{2,1,0:T(8,128)}, u32[]{:S(2)}) copy-start(f32[16,49,256]{2,1,0:T(8,128)} %get-tuple-element.182) | copy-start | bytes 2408452
  514.0 57.0 %copy-start.295 = (f32[8,4,16]{2,1,0:T(4,128)S(1)}, f32[8,4,16]{2,1,0:T(4,128)}, u32[]{:S(2)}) copy-start(f32[8,4,16]{2,1,0:T(4,128)} %get-tuple-element.296) | copy-start | bytes 6148
  514.0 57.0 %all-to-all-start.1 = ((bf16[8,4,12544]{2,1,0:T(4,128)(2,1)}), bf16[8,4,12544]{2,1,0:T(4,128)(2,1)S(1)}, u32[]{:S(2)}, u32[]{:S(2)}) async-start(bf16[8,4,12544]{2,1,0:T(4,128)(2,1)} %copy.307), calls=%async_computation.5 | async-start | bytes 1605632 | tf_op jit(solution)/shard_map/all_to_all | solution.py:541
  (281 other events, 920.0 us)
Sparse Core Ops, SparseCore 0:
  343.7 17.6 all-reduce.55
  461.9 17.5 all-reduce.53
  504.9 174.2 all-reduce.51
Sparse Core Ops, SparseCore 1:
  350.7 11.4 reduce-scatter.16
  364.9 12.4 reduce-scatter.18
  467.7 11.4 reduce-scatter.20
  486.7 11.4 reduce-scatter.22
where the time goes:
time: 705 us; the launch traced here: 694 us
  local copies, waits for them, and re-layouts  238 us (34%)
  waiting for transfers between devices  115 us (16%)
  other arithmetic  113 us (16%)
  blocking collectives  98.7 us (14%)
  matrix products  96 us (14%)
  between operations  20.2 us (3%)
  starting transfers between devices  13.2 us (2%)
    psum x1, waiting for transfers between devices, local(): lax.psum((gain_sum, shift_sum, entry_sum, entry_offset, kernel_sum, posit...  106 us
    reshape x32, local copies, waits for them, and re-layouts, head_rows(): return tensor.reshape(tensor.shape[0], -1, HEADS // 2, HEAD_DIM)  80.1 us
    psum x1, blocking collectives, local(): lax.psum((gain_sum, shift_sum, entry_sum, entry_offset, kernel_sum, posit...  50 us
    unnamed x620, local copies, waits for them, and re-layouts  44.1 us
    all_gather x2, blocking collectives, block_forward(): lax.all_gather(key_local[..., channel_half:], 'row', axis=1, tiled=True)  20.6 us
    convert_element_type x2, other arithmetic, block_forward(): activated = exact_gelu(pre_act).astype(jnp.bfloat16)  19.1 us
    all_gather x2, blocking collectives, block_forward(): lax.all_gather(value_local[..., channel_half:], 'row', axis=1, tiled=True)  17.6 us
    transpose x4, local copies, waits for them, and re-layouts, stripe_backward(): jnp.einsum('bhqk,bqhd->bkhd', chances.astype(jnp.bfloat16), out_rows, pre...  15.3 us
  transfers between devices with their start and end apart: 9, of which 3 were waited for; matrix products, arithmetic and copies ran while one was open for 13% of the time, Pallas kernels for 0%

commit v1 on v0

v1 whole, which is shorter than its diff:
```python
import functools

import jax
import jax.numpy as jnp
from jax import lax
from jax.experimental import pallas as pl
from jax.experimental.pallas import tpu as pltpu
from jax.sharding import PartitionSpec as P

TILE = 7
PAD = 56
HEAD_DIM = 32
SIDE_HEADS = 4
HALF = 128
WIN = 2 * PAD
LANES = SIDE_HEADS * 128
SCALE = HEAD_DIM ** (-0.5)
EPS = 1e-05
BF = jnp.bfloat16
F32 = jnp.float32
VMEM_BYTES = 60 * 1024 * 1024


def dot_nn(a, b):
    return lax.dot_general(a, b, (((1,), (0,)), ((), ())), preferred_element_type=F32)


def dot_nt(a, b):
    return lax.dot_general(a, b, (((1,), (1,)), ((), ())), preferred_element_type=F32)


def dot_tn(a, b):
    return lax.dot_general(a, b, (((0,), (0,)), ((), ())), preferred_element_type=F32)


def norm_parts(values):
    centered = values - jnp.mean(values, axis=-1, keepdims=True)
    inverse = lax.rsqrt(jnp.mean(centered * centered, axis=-1, keepdims=True) + EPS)
    return centered * inverse, inverse


def norm_back(delta, hat, inverse, gain):
    scaled = delta * gain
    first = jnp.mean(scaled, axis=-1, keepdims=True)
    second = jnp.mean(scaled * hat, axis=-1, keepdims=True)
    return inverse * (scaled - first - hat * second)


def gelu_parts(values):
    size = jnp.abs(values) * (0.5**0.5)
    fall = jnp.exp(-(size * size))
    step = 1.0 / (1.0 + 0.3275911 * size)
    series = step * (
        0.254829592
        + step * (-0.284496736 + step * (1.421413741 + step * (-1.453152027 + step * 1.061405429)))
    )
    tail = 0.5 * series * fall
    chance = jnp.where(values >= 0.0, 1.0 - tail, tail)
    return chance, fall * 0.3989422804014327


def row_sums(values):
    count, width = values.shape
    return jnp.sum(values.reshape(count // 8, 8, width), axis=0)


def scale_rows(scale_ref, column, rows_of):
    return jnp.concatenate(
        [jnp.full((PAD, 1), scale_ref[i, column], F32) for i in range(rows_of)], axis=0
    )


def add_row(acc_ref, row, values):
    acc_ref[row] += values


def spread_heads(values):
    lane = lax.broadcasted_iota(jnp.int32, values.shape, 1) // HEAD_DIM
    empty = jnp.zeros((128 - WIN, HALF), F32)
    blocks = []
    for head in range(SIDE_HEADS):
        blocks.append(jnp.where(lane == head, values, 0.0))
        blocks.append(empty)
    return jnp.concatenate(blocks, axis=0).astype(BF)


def gather_heads(wide):
    picked = jnp.concatenate(
        [
            wide[head * HEAD_DIM : (head + 1) * HEAD_DIM, head * 128 : (head + 1) * 128]
            for head in range(SIDE_HEADS)
        ],
        axis=0,
    )
    return picked.T[:WIN]


def valid_rows(shape):
    return lax.broadcasted_iota(jnp.int32, shape, 0) % 8 != 7


def column_shifts(values, across):
    cube = values.reshape(2 * TILE, 8, HALF)
    if not across:
        return (pltpu.roll(cube, 1, 1), cube, pltpu.roll(cube, 7, 1))
    left, right = cube[:TILE], cube[TILE:]
    column = lax.broadcasted_iota(jnp.int32, left.shape, 1)
    before = jnp.concatenate(
        [
            pltpu.roll(left, 1, 1),
            jnp.where(column == 0, pltpu.roll(left, 2, 1), pltpu.roll(right, 1, 1)),
        ],
        axis=0,
    )
    after = jnp.concatenate(
        [
            jnp.where(column == 6, pltpu.roll(right, 6, 1), pltpu.roll(left, 7, 1)),
            pltpu.roll(right, 7, 1),
        ],
        axis=0,
    )
    return (before, cube, after)


def row_shift(cube, step, across):
    if step == 0:
        return cube
    empty = jnp.zeros((1, 8, HALF), F32)

    def move(part):
        if step < 0:
            return jnp.concatenate([empty, part[:-1]], axis=0)
        return jnp.concatenate([part[1:], empty], axis=0)

    if across:
        return jnp.concatenate([move(cube[:TILE]), move(cube[TILE:])], axis=0)
    return move(cube)


def window_conv(shifts, kernel_at, across):
    total = None
    for i in range(3):
        part = None
        for j in range(3):
            term = kernel_at(i, j) * shifts[j]
            part = term if part is None else part + term
        part = row_shift(part, i - 1, across)
        total = part if total is None else total + part
    return total.reshape(WIN, HALF)


def window_rows(across, window):
    side, image = window // 4, window % 4
    if across:
        first, second = 2 * side, 2 * side + 1
    else:
        first, second = side, 2 + side
    return (
        pl.multiple_of((first * 4 + image) * PAD, 8),
        pl.multiple_of((second * 4 + image) * PAD, 8),
    )


def take_window(ref, at, lane):
    return jnp.concatenate(
        [ref[pl.ds(at[0], PAD), lane : lane + HALF], ref[pl.ds(at[1], PAD), lane : lane + HALF]],
        axis=0,
    )


def put_window(ref, at, lane, values):
    ref[pl.ds(at[0], PAD), lane : lane + HALF] = values[:PAD]
    ref[pl.ds(at[1], PAD), lane : lane + HALF] = values[PAD:]


def round_bf(values):
    return values.astype(BF).astype(F32)


def attention_forward(
    block, hidden_ref, gains, shifts, entry_w, entry_b, conv_k, conv_b, wide, stripe, win_out, chance_out
):
    width = hidden_ref.shape[1]

    @pl.loop(0, 4)
    def _(t):
        rows = pl.ds(pl.multiple_of(t * 4 * PAD, 4 * PAD), 4 * PAD)
        hat, _ = norm_parts(hidden_ref[rows, :])
        normed = (hat * gains[block, 0:1, :] + shifts[block, 0:1, :]).astype(BF)
        for part in range(3):
            out = dot_nn(normed, entry_w[block, :, part * width : (part + 1) * width])
            if part != 1:
                at = 0 if part == 0 else width
                out = out + entry_b[block : block + 1, at : at + width]
            wide[rows, part * width : (part + 1) * width] = round_bf(out)

    for direction in range(2):
        across = direction == 0
        lane = direction * HALF

        @pl.loop(0, 8)
        def _(window, across=across, lane=lane, direction=direction):
            at = window_rows(across, window)
            queries = take_window(wide, at, lane)
            keys = take_window(wide, at, width + lane)
            values = take_window(wide, at, 2 * width + lane)
            keys_bf = keys.astype(BF)
            win_out[direction * 8 + window, :, 0:HALF] = queries.astype(BF)
            win_out[direction * 8 + window, :, HALF : 2 * HALF] = keys_bf
            win_out[direction * 8 + window, :, 2 * HALF : 3 * HALF] = values.astype(BF)
            scores = dot_nt(keys_bf, spread_heads(queries))
            keep = valid_rows(scores.shape)
            scores = jnp.where(keep, scores, -1e30)
            top = jnp.max(scores, axis=0, keepdims=True)
            lifted = jnp.exp((scores - top) * SCALE)
            totals = jnp.sum(lifted, axis=0, keepdims=True)
            chances = (lifted * (1.0 / totals)).astype(BF)
            chance_out[direction * 8 + window] = chances
            attended = gather_heads(dot_nn(values.T.astype(BF), chances))
            clean = jnp.where(valid_rows(values.shape), values, 0.0)
            position = window_conv(
                column_shifts(clean, across),
                lambda i, j: conv_k[block, 3 * i + j : 3 * i + j + 1, lane : lane + HALF],
                across,
            )
            put_window(
                stripe, at, lane, attended + position + conv_b[block : block + 1, lane : lane + HALF]
            )


def attention_backward(
    block,
    win_in,
    chance_in,
    conv_k,
    stripe_delta,
    wide,
    conv_acc,
):
    width = stripe_delta.shape[1]
    for direction in range(2):
        across = direction == 0
        lane = direction * HALF

        @pl.loop(0, 8)
        def _(window, across=across, lane=lane, direction=direction):
            at = window_rows(across, window)
            out_delta = take_window(stripe_delta, at, lane)
            queries = win_in[direction * 8 + window, :, 0:HALF].astype(F32)
            keys = win_in[direction * 8 + window, :, HALF : 2 * HALF].astype(F32)
            values_bf = win_in[direction * 8 + window, :, 2 * HALF : 3 * HALF]
            values = values_bf.astype(F32)
            chances = chance_in[direction * 8 + window]
            delta_spread = spread_heads(out_delta)
            chance_delta = dot_nt(values_bf, delta_spread)
            wide_chances = chances.astype(F32)
            weighted = wide_chances * chance_delta
            score_delta = (
                weighted - wide_chances * jnp.sum(weighted, axis=0, keepdims=True)
            ).astype(BF)
            values_delta = dot_nn(chances, delta_spread)
            keys_delta = dot_nn(score_delta, spread_heads(queries)) * SCALE
            query_delta = gather_heads(dot_nn(keys.T.astype(BF), score_delta)) * SCALE
            keep = valid_rows(values.shape)
            clean = jnp.where(keep, values, 0.0)
            shifts = column_shifts(clean, across)
            cube = out_delta.reshape(2 * TILE, 8, HALF)
            for i in range(3):
                moved = row_shift(cube, 1 - i, across)
                for j in range(3):
                    conv_acc[3 * i + j, :, lane : lane + HALF] += jnp.sum(moved * shifts[j], axis=0)
            back = window_conv(
                column_shifts(out_delta, across),
                lambda i, j: conv_k[block, 8 - 3 * i - j : 9 - 3 * i - j, lane : lane + HALF],
                across,
            )
            values_delta = jnp.where(keep, values_delta + back, 0.0)
            put_window(wide, at, lane, query_delta)
            put_window(wide, at, width + lane, keys_delta)
            put_window(wide, at, 2 * width + lane, values_delta)


def chunk(t):
    return pl.ds(pl.multiple_of(t * 4 * PAD, 4 * PAD), 4 * PAD)


def put_squares(out_ref, at, values, side):
    for part in range(values.shape[1] // side):
        out_ref[at + part * side : at + (part + 1) * side, :] = values[
            :, part * side : (part + 1) * side
        ].astype(BF)


def first_kernel(
    scale_ref,
    mixed_ref,
    cot_ref,
    gains,
    shifts,
    entry_w,
    entry_b,
    conv_k,
    conv_b,
    exit_w,
    exit_b,
    expand_w,
    expand_b,
    shrink_w,
    shrink_b,
    act_out,
    bundle_out,
    vec_out,
    active0_out,
    slope0_out,
    win0_out,
    chance0_out,
    stripe0_out,
    mid0_out,
    win1_out,
    chance1_out,
    stripe1_out,
    hidden1_out,
    grad_out,
    hidden,
    wide,
    stripe,
    active1,
    pre1,
    feed1,
    inner1,
):
    width = hidden.shape[1]
    hidden_units = expand_w.shape[2]
    vec_out[...] = jnp.zeros(vec_out.shape, F32)

    @pl.loop(0, 16)
    def _(n):
        hidden[pl.ds(pl.multiple_of(n * PAD, 8), PAD), :] = mixed_ref[n // 4, n % 4].astype(F32)

    for block in range(2):
        win_out, chance_out, stripe_out = (
            (win0_out, chance0_out, stripe0_out),
            (win1_out, chance1_out, stripe1_out),
        )[block]
        attention_forward(
            block, hidden, gains, shifts, entry_w, entry_b, conv_k, conv_b, wide, stripe, win_out, chance_out
        )

        @pl.loop(0, 4)
        def _(t, block=block, stripe_out=stripe_out):
            rows = chunk(t)
            striped = stripe[rows, :].astype(BF)
            stripe_out[rows, :] = striped
            branch = dot_nn(striped, exit_w[block]) + exit_b[block : block + 1, :]
            midway = hidden[rows, :] + scale_rows(scale_ref, 2 * block, 4) * branch
            if block == 0:
                mid0_out[rows, :] = midway
            hat, inverse = norm_parts(midway)
            normed = (hat * gains[block, 1:2, :] + shifts[block, 1:2, :]).astype(BF)
            feed_scale = scale_rows(scale_ref, 2 * block + 1, 4)
            feed = shrink_b[block : block + 1, :]
            if block == 1:
                inner1[rows, :] = normed
                gradient = jnp.concatenate([cot_ref[t, i] for i in range(4)], axis=0).astype(F32)
                feed_delta = (feed_scale * gradient).astype(BF)
                feed1[rows, :] = feed_delta
                add_row(vec_out, 4, row_sums(feed_delta.astype(F32)))
                inner_delta = jnp.zeros((4 * PAD, width), F32)
            for part in range(hidden_units // width):
                at = slice(part * width, (part + 1) * width)
                pre_act = dot_nn(normed, expand_w[block, :, at]) + expand_b[block : block + 1, at]
                chance, density = gelu_parts(pre_act)
                active = (pre_act * chance).astype(BF)
                slope = chance + pre_act * density
                if block == 0:
                    active0_out[rows, at] = active
                    slope0_out[rows, at] = slope.astype(BF)
                else:
                    active1[rows, at] = active
                    pre_delta = (dot_nt(feed_delta, shrink_w[block, at, :]) * slope).astype(BF)
                    pre1[rows, at] = pre_delta
                    add_row(vec_out, part, row_sums(pre_delta.astype(F32)))
                    inner_delta = inner_delta + dot_nt(pre_delta, expand_w[block, :, at])
                feed = feed + dot_nn(active, shrink_w[block, at, :])
            output = midway + feed_scale * feed
            if block == 0:
                hidden[rows, :] = output
                hidden1_out[rows, :] = output
            else:
                for i in range(4):
                    act_out[t, i] = output[i * PAD : (i + 1) * PAD].astype(BF)
                add_row(vec_out, 5, row_sums(inner_delta * hat))
                add_row(vec_out, 6, row_sums(inner_delta))
                grad_out[rows, :] = gradient + norm_back(
                    inner_delta, hat, inverse, gains[block, 1:2, :]
                )

    put_squares(bundle_out, 0, dot_tn(inner1[...], pre1[...]), width)
    for part in range(hidden_units // width):
        bundle_out[hidden_units + part * width : hidden_units + (part + 1) * width, :] = dot_tn(
            active1[:, part * width : (part + 1) * width], feed1[...]
        ).astype(BF)


def delta_rows(block, scale_ref, exit_w, grad_ref, stripe_delta, branch_delta, vec_out, at):
    @pl.loop(0, 4)
    def _(t):
        rows = chunk(t)
        rounded = (scale_rows(scale_ref, 2 * block, 4) * grad_ref[rows, :]).astype(BF)
        branch_delta[rows, :] = rounded
        add_row(vec_out, at, row_sums(rounded.astype(F32)))
        out = round_bf(dot_nt(rounded, exit_w[block]))
        stripe_delta[rows, :] = out
        add_row(vec_out, at + 1, row_sums(out))


def entry_backward(block, hidden_ref, gains, shifts, entry_w, grad_ref, wide, wide_bf, normed_bf, vec_out, at, emit):
    width = hidden_ref.shape[1]

    @pl.loop(0, 4)
    def _(t):
        rows = chunk(t)
        hat, inverse = norm_parts(hidden_ref[rows, :])
        normed_bf[rows, :] = (hat * gains[block, 0:1, :] + shifts[block, 0:1, :]).astype(BF)
        delta = jnp.zeros((4 * PAD, width), F32)
        for part in range(3):
            lanes = slice(part * width, (part + 1) * width)
            rounded = wide[rows, lanes].astype(BF)
            wide_bf[rows, lanes] = rounded
            if part != 1:
                add_row(vec_out, at + part // 2, row_sums(rounded.astype(F32)))
            delta = delta + dot_nt(rounded, entry_w[block, :, lanes])
        add_row(vec_out, at + 2, row_sums(delta * hat))
        add_row(vec_out, at + 3, row_sums(delta))
        emit(t, rows, grad_ref[rows, :] + norm_back(delta, hat, inverse, gains[block, 0:1, :]))


def second_kernel(
    scale_ref,
    grad_in,
    hidden1,
    stripe1,
    win1,
    chance1,
    mid0,
    active0,
    slope0,
    stripe0,
    gains,
    shifts,
    entry_w,
    conv_k,
    exit_w,
    expand_w,
    shrink_w,
    bundle_out,
    vec_out,
    conv_out,
    grad_out,
    stripe_delta_out,
    grad,
    stripe_delta,
    branch_delta,
    wide,
    wide_bf,
    normed_bf,
    feed0,
    pre0,
):
    width = grad.shape[1]
    hidden_units = expand_w.shape[2]
    vec_out[...] = jnp.zeros(vec_out.shape, F32)
    conv_out[...] = jnp.zeros(conv_out.shape, F32)
    delta_rows(1, scale_ref, exit_w, grad_in, stripe_delta, branch_delta, vec_out, 0)
    attention_backward(1, win1, chance1, conv_k, stripe_delta, wide, conv_out)

    def emit(t, rows, values):
        grad[rows, :] = values

    entry_backward(
        1, hidden1, gains, shifts, entry_w, grad_in, wide, wide_bf, normed_bf, vec_out, 2, emit
    )
    put_squares(bundle_out, 0, dot_tn(normed_bf[...], wide_bf[...]), width)
    bundle_out[3 * width : 4 * width, :] = dot_tn(stripe1[...], branch_delta[...]).astype(BF)

    @pl.loop(0, 4)
    def _(t):
        rows = chunk(t)
        gradient = grad[rows, :]
        hat, inverse = norm_parts(mid0[rows, :])
        normed_bf[rows, :] = (hat * gains[0, 1:2, :] + shifts[0, 1:2, :]).astype(BF)
        feed_delta = (scale_rows(scale_ref, 1, 4) * gradient).astype(BF)
        feed0[rows, :] = feed_delta
        add_row(vec_out, 6, row_sums(feed_delta.astype(F32)))
        inner_delta = jnp.zeros((4 * PAD, width), F32)
        for part in range(hidden_units // width):
            at = slice(part * width, (part + 1) * width)
            pre_delta = (
                dot_nt(feed_delta, shrink_w[0, at, :]) * slope0[rows, at].astype(F32)
            ).astype(BF)
            pre0[rows, at] = pre_delta
            add_row(vec_out, 7 + part, row_sums(pre_delta.astype(F32)))
            inner_delta = inner_delta + dot_nt(pre_delta, expand_w[0, :, at])
        add_row(vec_out, 11, row_sums(inner_delta * hat))
        add_row(vec_out, 12, row_sums(inner_delta))
        grad[rows, :] = gradient + norm_back(inner_delta, hat, inverse, gains[0, 1:2, :])

    grad_out[...] = grad[...]
    put_squares(bundle_out, 4 * width, dot_tn(normed_bf[...], pre0[...]), width)
    for part in range(hidden_units // width):
        base = 8 * width + part * width
        bundle_out[base : base + width, :] = dot_tn(
            active0[:, part * width : (part + 1) * width], feed0[...]
        ).astype(BF)
    delta_rows(0, scale_ref, exit_w, grad, stripe_delta_out, branch_delta, vec_out, 13)
    bundle_out[12 * width : 13 * width, :] = dot_tn(stripe0[...], branch_delta[...]).astype(BF)


def third_kernel(
    grad_in,
    stripe_delta,
    mixed_ref,
    win0,
    chance0,
    gains,
    shifts,
    entry_w,
    conv_k,
    out_ref,
    bundle_out,
    vec_out,
    conv_out,
    hidden,
    wide,
    wide_bf,
    normed_bf,
):
    width = hidden.shape[1]
    vec_out[...] = jnp.zeros(vec_out.shape, F32)
    conv_out[...] = jnp.zeros(conv_out.shape, F32)

    @pl.loop(0, 16)
    def _(n):
        hidden[pl.ds(pl.multiple_of(n * PAD, 8), PAD), :] = mixed_ref[n // 4, n % 4].astype(F32)

    attention_backward(0, win0, chance0, conv_k, stripe_delta, wide, conv_out)

    def emit(t, rows, values):
        for i in range(4):
            out_ref[t, i] = values[i * PAD : (i + 1) * PAD].astype(BF)

    entry_backward(
        0, hidden, gains, shifts, entry_w, grad_in, wide, wide_bf, normed_bf, vec_out, 0, emit
    )
    put_squares(bundle_out, 0, dot_tn(normed_bf[...], wide_bf[...]), width)


def pick_kernel(index_ref, images_ref, out_ref):
    @pl.loop(0, out_ref.shape[0])
    def _(s):
        out_ref[s] = images_ref[jnp.minimum(index_ref[s], images_ref.shape[0] - 1)]


def inside_box(corner_ref, n, start_ref):
    token = lax.broadcasted_iota(jnp.int32, (PAD, 1), 0)
    row = start_ref[0] + token // 8
    col = start_ref[1] + token % 8
    hit = (
        (row >= corner_ref[n, 0])
        & (row < corner_ref[n, 1])
        & (col >= corner_ref[n, 2])
        & (col < corner_ref[n, 3])
    )
    return jnp.where(hit, 1.0, 0.0)


def mix_kernel(take_ref, corner_ref, ratio_ref, start_ref, arrived, images_ref, out_ref):
    count = images_ref.shape[0]

    @pl.loop(0, count)
    def _(n):
        inside = inside_box(corner_ref, n, start_ref)
        ratio = ratio_ref[n]
        own = images_ref[n].astype(F32)
        blend = arrived[take_ref[n]].astype(F32)
        cut = arrived[take_ref[count + n]].astype(F32)
        mixed = inside * cut + (1.0 - inside) * (ratio * own + (1.0 - ratio) * blend)
        out_ref[n] = mixed.astype(BF)


def split_kernel(take_ref, corner_ref, ratio_ref, start_ref, grad_ref, out_ref):
    count = grad_ref.shape[0]
    out_ref[...] = jnp.zeros(out_ref.shape, BF)

    @pl.loop(0, count)
    def _(n):
        inside = inside_box(corner_ref, n, start_ref)
        gradient = grad_ref[n].astype(F32)
        cut = inside * gradient
        out_ref[take_ref[n]] = ((1.0 - ratio_ref[n]) * (gradient - cut)).astype(BF)
        out_ref[take_ref[count + n]] = cut.astype(BF)


def join_kernel(index_ref, corner_ref, ratio_ref, start_ref, grad_ref, back_ref, out_ref, total):
    count = grad_ref.shape[0]

    @pl.loop(0, count)
    def _(n):
        outside = 1.0 - inside_box(corner_ref, n, start_ref)
        total[n] = ratio_ref[n] * outside * grad_ref[n].astype(F32)

    @pl.loop(0, back_ref.shape[0])
    def _(s):
        total[index_ref[s]] += back_ref[s].astype(F32)

    @pl.loop(0, count)
    def _(n):
        out_ref[n] = total[n].reshape(TILE, 8, total.shape[2])[:, :TILE, :]


SMEM = pl.BlockSpec(memory_space=pltpu.SMEM)
VMEM = pl.BlockSpec(memory_space=pltpu.VMEM)


def run(kernel, scalars, arrays, outs, scratch=(), flops=0, name=None):
    out_shape = [jax.ShapeDtypeStruct(shape, dtype) for shape, dtype in outs]
    moved = sum(a.size * a.dtype.itemsize for a in arrays)
    return pl.pallas_call(
        kernel,
        out_shape=out_shape,
        in_specs=[SMEM] * len(scalars) + [VMEM] * len(arrays),
        out_specs=[VMEM] * len(outs),
        scratch_shapes=[pltpu.VMEM(shape, dtype) for shape, dtype in scratch],
        compiler_params=pltpu.CompilerParams(vmem_limit_bytes=VMEM_BYTES),
        cost_estimate=pl.CostEstimate(flops=flops, bytes_accessed=moved, transcendentals=0),
        name=name,
    )(*scalars, *arrays)


def partner_plan(mix_partner, cut_partner, images_here, groups, device):
    requests = jnp.concatenate(
        [mix_partner.reshape(groups, images_here), cut_partner.reshape(groups, images_here)], axis=1
    )
    owners = requests // images_here
    within = requests % images_here
    wanted = 2 * images_here
    before = jnp.arange(wanted)[None, :] < jnp.arange(wanted)[:, None]
    rank = jnp.sum((owners[:, :, None] == owners[:, None, :]) & before[None], axis=2)
    capacity = (wanted + groups - 1) // groups
    chosen = (owners == device)[:, :, None] & (
        rank[:, :, None] == jnp.arange(capacity)[None, None, :]
    )
    index = images_here + jnp.sum(
        jnp.where(chosen, (within - images_here)[:, :, None], 0), axis=1
    ).reshape(groups * capacity)
    take = lax.dynamic_index_in_dim(owners * capacity + rank, device, 0, keepdims=False)
    return index.astype(jnp.int32), take.astype(jnp.int32), capacity


def swap(values, axis):
    return lax.ppermute(values, axis, [(0, 1), (1, 0)])


def halve(values, axis):
    place = lax.axis_index(axis)
    count = values.shape[0] // 2
    away = lax.dynamic_slice_in_dim(values, (1 - place) * count, count, 0)
    mine = lax.dynamic_slice_in_dim(values, place * count, count, 0)
    return (mine.astype(F32) + swap(away, axis).astype(F32)).astype(BF)


def unhalve(values, axis):
    other = swap(values, axis)
    first = lax.axis_index(axis) == 0
    return jnp.concatenate([jnp.where(first, values, other), jnp.where(first, other, values)])


def sum_spread(values, groups):
    part = halve(halve(values, "col"), "row")
    rows = part.shape[0] // groups
    pieces = lax.all_to_all(
        part.reshape(groups, rows, part.shape[1]), "dp", split_axis=0, concat_axis=0, tiled=True
    )
    mine = jnp.sum(pieces.astype(F32), axis=0).astype(BF)
    full = lax.all_to_all(
        jnp.broadcast_to(mine[None], pieces.shape), "dp", split_axis=0, concat_axis=0, tiled=True
    )
    return unhalve(unhalve(full.reshape(part.shape), "row"), "col")


def sum_doubling(values, groups):
    part = halve(halve(values, "col"), "row")
    step = 1
    while step < groups:
        other = lax.ppermute(part, "dp", [(i, i ^ step) for i in range(groups)])
        part = (part.astype(F32) + other.astype(F32)).astype(BF)
        step *= 2
    return unhalve(unhalve(part, "row"), "col")


def local(
    groups,
    images,
    cotangent,
    mix_partner,
    cut_partner,
    ratios,
    corners,
    drop_masks,
    norm_gains,
    norm_shifts,
    entry_weight,
    entry_bias,
    position_kernel,
    position_bias,
    exit_weight,
    exit_bias,
    expand_weight,
    expand_bias,
    shrink_weight,
    shrink_bias,
):
    images_here = images.shape[0]
    width = images.shape[3]
    units = expand_weight.shape[2]
    device = lax.axis_index("dp")
    row, col = lax.axis_index("row"), lax.axis_index("col")
    start = jnp.stack([row * TILE, col * TILE]).astype(jnp.int32)
    share = images_here // 4
    rows = 4 * share * PAD
    index, take, capacity = partner_plan(mix_partner, cut_partner, images_here, groups, device)
    slots = groups * capacity

    def padded(values):
        wide = jnp.pad(values, ((0, 0), (0, 0), (0, 1), (0, 0)))
        return wide.reshape(images_here, PAD, width)

    def regroup(values):
        return lax.all_to_all(values, ("row", "col"), split_axis=0, concat_axis=0, tiled=True)

    own = padded(images)
    (outgoing,) = run(pick_kernel, [index], [own], [((slots, PAD, width), BF)], name="pick")
    arrived = lax.all_to_all(outgoing, "dp", split_axis=0, concat_axis=0, tiled=True)
    cot = regroup(padded(cotangent).reshape(4, share, PAD, width))
    (mixed,) = run(
        mix_kernel,
        [take, corners, ratios, start],
        [arrived, own],
        [((images_here, PAD, width), BF)],
        name="mix",
    )
    mixed = regroup(mixed.reshape(4, share, PAD, width))
    scales = lax.dynamic_slice_in_dim(
        drop_masks.astype(F32) * 1.25, (2 * row + col) * share, share, 0
    )
    conv_k = position_kernel.reshape(2, 9, width)
    tall = (rows, width)
    (
        act,
        bundle1,
        vec1,
        active0,
        slope0,
        win0,
        chance0,
        stripe0,
        mid0,
        win1,
        chance1,
        stripe1,
        hidden1,
        grad1,
    ) = run(
        first_kernel,
        [scales],
        [
            mixed,
            cot,
            norm_gains,
            norm_shifts,
            entry_weight,
            entry_bias,
            conv_k,
            position_bias,
            exit_weight,
            exit_bias,
            expand_weight,
            expand_bias,
            shrink_weight,
            shrink_bias,
        ],
        [
            ((4, share, PAD, width), BF),
            ((2 * units, width), BF),
            ((7, 8, width), F32),
            ((rows, units), BF),
            ((rows, units), BF),
            ((4 * share, WIN, 3 * HALF), BF),
            ((4 * share, WIN, LANES), BF),
            (tall, BF),
            (tall, F32),
            ((4 * share, WIN, 3 * HALF), BF),
            ((4 * share, WIN, LANES), BF),
            (tall, BF),
            (tall, F32),
            (tall, F32),
        ],
        [
            (tall, F32),
            ((rows, 3 * width), F32),
            (tall, F32),
            ((rows, units), BF),
            ((rows, units), BF),
            (tall, BF),
            (tall, BF),
        ],
        flops=10 * rows * width * width * 12,
        name="first",
    )
    sum1 = sum_spread(bundle1, groups)
    act = regroup(act)
    bundle2, vec2, conv2, grad0, delta0 = run(
        second_kernel,
        [scales],
        [
            grad1,
            hidden1,
            stripe1,
            win1,
            chance1,
            mid0,
            active0,
            slope0,
            stripe0,
            norm_gains,
            norm_shifts,
            entry_weight,
            conv_k,
            exit_weight,
            expand_weight,
            shrink_weight,
        ],
        [
            ((13 * width, width), BF),
            ((15, 8, width), F32),
            ((9, 8, width), F32),
            (tall, F32),
            (tall, F32),
        ],
        [
            (tall, F32),
            (tall, F32),
            (tall, BF),
            ((rows, 3 * width), F32),
            ((rows, 3 * width), BF),
            (tall, BF),
            (tall, BF),
            ((rows, units), BF),
        ],
        flops=6 * rows * width * width * 12,
        name="second",
    )
    sum2 = sum_spread(bundle2, groups)
    out_tiles, bundle3, vec3, conv3 = run(
        third_kernel,
        [],
        [grad0, delta0, mixed, win0, chance0, norm_gains, norm_shifts, entry_weight, conv_k],
        [
            ((4, share, PAD, width), BF),
            ((3 * width, width), BF),
            ((4, 8, width), F32),
            ((9, 8, width), F32),
        ],
        [(tall, F32), ((rows, 3 * width), F32), ((rows, 3 * width), BF), (tall, BF)],
        flops=3 * rows * width * width * 12,
        name="third",
    )
    gradient = regroup(out_tiles).reshape(images_here, PAD, width)
    (parted,) = run(
        split_kernel,
        [take, corners, ratios, start],
        [gradient],
        [((slots, PAD, width), BF)],
        name="split",
    )
    back = lax.all_to_all(parted, "dp", split_axis=0, concat_axis=0, tiled=True)
    (input_gradient,) = run(
        join_kernel,
        [index, corners, ratios, start],
        [gradient, back],
        [((images_here, TILE, TILE, width), F32)],
        [((images_here + 1, PAD, width), F32)],
        name="join",
    )
    vectors = jnp.sum(jnp.concatenate([vec1, vec2, conv2, vec3, conv3]), axis=1)
    count = vectors.shape[0]
    filled = jnp.pad(vectors.astype(BF), ((0, 64 - count), (0, 0)))
    sum3 = sum_doubling(jnp.concatenate([bundle3, filled]), groups)

    def flat(values):
        return values.reshape(-1, width, width).transpose(1, 0, 2).reshape(width, -1)

    sum1, sum2, sum3 = sum1.astype(F32), sum2.astype(F32), sum3.astype(F32)
    v = sum3[3 * width : 3 * width + count]
    v1, v2, c2, v3, c3 = v[0:7], v[7:22], v[22:31], v[31:35], v[35:44]
    return (
        act.reshape(images_here, TILE, 8, width)[:, :, :TILE, :],
        input_gradient,
        jnp.stack([jnp.stack([v3[2], v2[11]]), jnp.stack([v2[4], v1[5]])]),
        jnp.stack([jnp.stack([v3[3], v2[12]]), jnp.stack([v2[5], v1[6]])]),
        jnp.stack([flat(sum3[: 3 * width]), flat(sum2[: 3 * width])]),
        jnp.stack([v3[0:2].reshape(-1), v2[2:4].reshape(-1)]),
        jnp.stack([c3, c2]).reshape(2, 3, 3, width),
        jnp.stack([v2[14], v2[1]]),
        jnp.stack([sum2[12 * width :], sum2[3 * width : 4 * width]]),
        jnp.stack([v2[13], v2[0]]),
        jnp.stack([flat(sum2[4 * width : 8 * width]), flat(sum1[:units])]),
        jnp.stack([v2[7:11].reshape(-1), v1[0:4].reshape(-1)]),
        jnp.stack([sum2[8 * width : 12 * width], sum1[units:]]),
        jnp.stack([v2[6], v1[4]]),
    )


def solution(mesh):
    tiles = P("dp", "row", "col", None)
    return jax.shard_map(
        functools.partial(local, mesh.shape["dp"]),
        mesh=mesh,
        in_specs=(tiles, tiles, P(), P(), P("dp"), P("dp", None), P("dp", None)) + (P(),) * 12,
        out_specs=(tiles, tiles) + (P(),) * 12,
        check_vma=False,
    )
```

time: 705 us -> 290 us (0.41); the launches traced: 694 us -> 288 us
  local copies, waits for them, and re-layouts: 238 us -> 31.3 us
  blocking collectives: 98.7 us -> 0 us
  matrix products: 96 us -> 0 us
  Pallas kernels: 0 us -> 88.6 us
  other arithmetic: 113 us -> 24.7 us
  starting transfers between devices: 13.2 us -> 51.4 us
  waiting for transfers between devices: 115 us -> 91 us
  between operations: 20.2 us -> 1.18 us
    psum x1 -> x0, waiting for transfers between devices: 106 us -> none  [local(): lax.psum((gain_sum, shift_sum, entry_sum, entry_offset, kernel_sum, posit...]
    reshape x44 -> x3, local copies, waits for them, and re-layouts: 107 us -> 3.75 us  [the longest x1 2.29 us: flat(): values.reshape(-1, width, width).transpose(1, 0, 2).reshape(width, -1)]
    dot_general x53 -> x0, matrix products: 96 us -> none  [the longest x4 11.6 us: stripe_backward(): jnp.einsum('bhqk,bqhd->bkhd', chances.astype(jnp.bfloat16), out_rows, pre...]
    pallas_call x0 -> x7, Pallas kernels: none -> 88.6 us  [run(): pl.pallas_call(kernel, out_shape=out_shape, in_specs=[SMEM] * len(scalars...]
    psum x1 -> x0, blocking collectives: 50 us -> none  [local(): lax.psum((gain_sum, shift_sum, entry_sum, entry_offset, kernel_sum, posit...]
    all_gather x8 -> x0, blocking collectives: 48.8 us -> none  [the longest x2 20.6 us: block_forward(): lax.all_gather(key_local[..., channel_half:], 'row', axis=1, tiled=True)]
    all_to_all x1 -> x9, waiting for transfers between devices: 0.01 us -> 47.5 us  [the longest x4 21.3 us: regroup(): lax.all_to_all(values, ('row', 'col'), split_axis=0, concat_axis=0, tiled...]
    unnamed x620 -> x48, local copies, waits for them, and re-layouts: 44.1 us -> 13.5 us
  transfers between devices with their start and end apart: 9 -> 25, of which waited for: 3 -> 14; matrix products, arithmetic and copies ran while one was open for 13% -> 9% of each run, Pallas kernels for 0% -> 3%
where the time goes in v1:
time: 290 us; the launch traced here: 288 us
  waiting for transfers between devices  91 us (31%)
  Pallas kernels  88.6 us (31%)
  starting transfers between devices  51.4 us (18%)
  local copies, waits for them, and re-layouts  31.3 us (11%)
  other arithmetic  24.7 us (9%)
    pallas_call x7, Pallas kernels, run(): pl.pallas_call(kernel, out_shape=out_shape, in_specs=[SMEM] * len(scalars...  88.6 us
    ppermute x12, waiting for transfers between devices, swap(): return lax.ppermute(values, axis, [(0, 1), (1, 0)])  22.2 us
    all_to_all x1, waiting for transfers between devices, local(): lax.all_to_all(outgoing, 'dp', split_axis=0, concat_axis=0, tiled=True)  21.4 us
    all_to_all x4, waiting for transfers between devices, regroup(): lax.all_to_all(values, ('row', 'col'), split_axis=0, concat_axis=0, tiled...  21.3 us
    all_to_all x2, waiting for transfers between devices, sum_spread(): lax.all_to_all(jnp.broadcast_to(mine[None], pieces.shape), 'dp', split_ax...  15.7 us
    all_to_all x4, starting transfers between devices, regroup(): lax.all_to_all(values, ('row', 'col'), split_axis=0, concat_axis=0, tiled...  14.2 us
    unnamed x48, local copies, waits for them, and re-layouts  13.5 us
    all_to_all x2, waiting for transfers between devices, sum_spread(): lax.all_to_all(part.reshape(groups, rows, part.shape[1]), 'dp', split_axi...  10.5 us
  transfers between devices with their start and end apart: 25, of which 14 were waited for; matrix products, arithmetic and copies ran while one was open for 9% of the time, Pallas kernels for 3%

profile of v1, /device:TPU:0, one launch (start us, length us, event | category | flops | bytes accessed | tf_op | source)
XLA Modules:
  0.0 288.2 jit_solution(14600022642569906983)
XLA Ops:
  7.7 7.3 %all-to-all-start = ((bf16[32,56,256]{2,1,0:T(8,128)(2,1)}), bf16[32,56,256]{2,1,0:T(8,128)(2,1)S(1)}, u32[]{:S(2)}, u32[]{:S(2)}) async-start(bf16[32,56,256]{2,1,0:T(8,128)(2,1)} %pick.1), calls=%async_computation | async-start | bytes 1835008 | tf_op jit(solution)/shard_map/all_to_all | solution.py:743
  16.7 21.4 %all-to-all-done.arrived = bf16[32,56,256]{2,1,0:T(8,128)(2,1)S(1)} async-done(((bf16[32,56,256]{2,1,0:T(8,128)(2,1)}), bf16[32,56,256]{2,1,0:T(8,128)(2,1)S(1)}, u32[]{:S(2)}, u32[]{:S(2)}) %all-to-all-start) | async-done | bytes 917536 | tf_op jit(solution)/shard_map/all_to_all | solution.py:743
  38.1 3.6 %all-to-all-start.2 = ((bf16[4,4,56,256]{3,2,1,0:T(8,128)(2,1)}), bf16[4,4,56,256]{3,2,1,0:T(8,128)(2,1)S(1)}, u32[]{:S(2)}, u32[]{:S(2)}) async-start(bf16[4,4,56,256]{3,2,1,0:T(8,128)(2,1)} %bitcast.5), calls=%async_computation.2 | async-start | bytes 917504 | tf_op jit(solution)/shard_map/all_to_all | solution.py:739
  45.5 4.3 %all-to-all-done.2.cot_ref = bf16[4,4,56,256]{3,2,1,0:T(8,128)(2,1)S(1)} async-done(((bf16[4,4,56,256]{3,2,1,0:T(8,128)(2,1)}), bf16[4,4,56,256]{3,2,1,0:T(8,128)(2,1)S(1)}, u32[]{:S(2)}, u32[]{:S(2)}) %all-to-all-start.2) | async-done | bytes 458784 | tf_op jit(solution)/shard_map/all_to_all | solution.py:739
  49.8 3.5 %all-to-all-start.1 = ((bf16[4,4,56,256]{3,2,1,0:T(8,128)(2,1)}), bf16[4,4,56,256]{3,2,1,0:T(8,128)(2,1)S(1)}, u32[]{:S(2)}, u32[]{:S(2)}) async-start(bf16[4,4,56,256]{3,2,1,0:T(8,128)(2,1)} %bitcast.75), calls=%async_computation.1 | async-start | bytes 917504 | tf_op jit(solution)/shard_map/all_to_all | solution.py:739
  54.7 6.7 %all-to-all-done.1.mixed_ref = bf16[4,4,56,256]{3,2,1,0:T(8,128)(2,1)S(1)} async-done(((bf16[4,4,56,256]{3,2,1,0:T(8,128)(2,1)}), bf16[4,4,56,256]{3,2,1,0:T(8,128)(2,1)S(1)}, u32[]{:S(2)}, u32[]{:S(2)}) %all-to-all-start.1) | async-done | bytes 458784 | tf_op jit(solution)/shard_map/all_to_all | solution.py:739
  62.1 39.9 %first.1 = (bf16[4,4,56,256]{3,2,1,0:T(8,128)(2,1)}, bf16[2048,256]{1,0:T(8,128)(2,1)}, f32[7,8,256]{2,1,0:T(8,128)}, bf16[896,1024]{1,0:T(8,128)(2,1)}, bf16[89...) custom-call(f32[4,4]{1,0:T(4,128)} %broadcast_multiply_fusion.scale_, ...), custom_call_target="tpu_custom_call" | custom-call | flops 7046430720 | bytes 4108288 | tf_op jit(solution)/shard_map/first/pallas_call | solution.py:628
  102.9 23.6 %second.1 = (bf16[3328,256]{1,0:T(8,128)(2,1)}, f32[15,8,256]{2,1,0:T(8,128)}, f32[9,8,256]{2,1,0:T(8,128)}, f32[896,256]{1,0:T(8,128)}, f32[896,256]{1,0:T(8,128)}) custom-call(f32[4,4]{1,0:T(4,128)} %broadcast_multiply_fusion.scale_ref, f32[896,256]{1,0:T(8,128)} %get-tuple-element.38.grad_in, f32[896,256]{1,0:T(8,128)} %get-tuple-element.39.hidden1, ...), custom_call_target="tpu_custom_call" | custom-call | flops 4227858432 | bytes 13723648 | tf_op jit(solution)/shard_map/second/pallas_call | solution.py:628
  128.2 14.5 %third.1 = (bf16[4,4,56,256]{3,2,1,0:T(8,128)(2,1)}, bf16[768,256]{1,0:T(8,128)(2,1)}, f32[4,8,256]{2,1,0:T(8,128)}, f32[9,8,256]{2,1,0:T(8,128)}) custom-call(f32[896,256]{1,0:T(8,128)} %get-tuple-element.47.grad_in, f32[896,256]{1,0:T(8,128)} %get-tuple-element.48.stripe_delta, bf16[4,4,56,256]{3,2,1,0:T(8,128)(2,1)} %copy-done.10, ...), custom_call_target="tpu_custom_call" | custom-call | flops 2113929216 | bytes 6318080 | tf_op jit(solution)/shard_map/third/pallas_call | solution.py:628
  147.9 4.5 %collective-permute-done.1 = bf16[208,256]{1,0:T(8,128)(2,1)S(1)} collective-permute-done((bf16[208,256]{1,0:T(8,128)(2,1)S(1)}, bf16[208,256]{1,0:T(8,128)(2,1)S(1)}, u32[]{:S(2)}, u32[]{:S(2)}) %collective-permute-start.1) | collective-permute-done | bytes 106528 | tf_op jit(solution)/shard_map/ppermute | solution.py:661
  153.9 3.6 %all-to-all-start.3 = ((bf16[4,4,56,256]{3,2,1,0:T(8,128)(2,1)}), bf16[4,4,56,256]{3,2,1,0:T(8,128)(2,1)S(1)}, u32[]{:S(2)}, u32[]{:S(2)}) async-start(bf16[4,4,56,256]{3,2,1,0:T(8,128)(2,1)} %get-tuple-element.37), calls=%async_computation.3 | async-start | bytes 917504 | tf_op jit(solution)/shard_map/all_to_all | solution.py:739
  161.4 4.6 %all-to-all-done.3 = bf16[4,4,56,256]{3,2,1,0:T(8,128)(2,1)S(1)} async-done(((bf16[4,4,56,256]{3,2,1,0:T(8,128)(2,1)}), bf16[4,4,56,256]{3,2,1,0:T(8,128)(2,1)S(1)}, u32[]{:S(2)}, u32[]{:S(2)}) %all-to-all-start.3) | async-done | bytes 458784 | tf_op jit(solution)/shard_map/all_to_all | solution.py:739
  166.0 3.5 %all-to-all-start.4 = ((bf16[4,4,56,256]{3,2,1,0:T(8,128)(2,1)}), bf16[4,4,56,256]{3,2,1,0:T(8,128)(2,1)S(1)}, u32[]{:S(2)}, u32[]{:S(2)}) async-start(bf16[4,4,56,256]{3,2,1,0:T(8,128)(2,1)} %get-tuple-element.51), calls=%async_computation.4 | async-start | bytes 917504 | tf_op jit(solution)/shard_map/all_to_all | solution.py:739
  172.3 5.7 %all-to-all-done.4 = bf16[4,4,56,256]{3,2,1,0:T(8,128)(2,1)S(1)} async-done(((bf16[4,4,56,256]{3,2,1,0:T(8,128)(2,1)}), bf16[4,4,56,256]{3,2,1,0:T(8,128)(2,1)S(1)}, u32[]{:S(2)}, u32[]{:S(2)}) %all-to-all-start.4) | async-done | bytes 458784 | tf_op jit(solution)/shard_map/all_to_all | solution.py:739
  188.7 4.6 %all-to-all-done.8 = bf16[8,64,256]{2,1,0:T(8,128)(2,1)S(1)} async-done(((bf16[8,64,256]{2,1,0:T(8,128)(2,1)}), bf16[8,64,256]{2,1,0:T(8,128)(2,1)S(1)}, u32[]{:S(2)}, u32[]{:S(2)}) %all-to-all-start.8) | async-done | bytes 262176 | tf_op jit(solution)/shard_map/all_to_all | solution.py:681
  193.3 3.5 %all-to-all-start.6 = ((bf16[8,104,256]{2,1,0:T(8,128)(2,1)}), bf16[8,104,256]{2,1,0:T(8,128)(2,1)S(1)}, u32[]{:S(2)}, u32[]{:S(2)}) async-start(bf16[8,104,256]{2,1,0:T(8,128)(2,1)} %bitcast.16), calls=%async_computation.6 | async-start | bytes 851968 | tf_op jit(solution)/shard_map/all_to_all | solution.py:681
  197.5 4.1 %collective-permute-done.5 = bf16[208,256]{1,0:T(8,128)(2,1)S(1)} collective-permute-done((bf16[208,256]{1,0:T(8,128)(2,1)S(1)}, bf16[208,256]{1,0:T(8,128)(2,1)S(1)}, u32[]{:S(2)}, u32[]{:S(2)}) %collective-permute-start.5) | collective-permute-done | bytes 106528 | tf_op jit(solution)/shard_map/ppermute | solution.py:661
  201.8 5.9 %all-to-all-done.6 = bf16[8,104,256]{2,1,0:T(8,128)(2,1)S(1)} async-done(((bf16[8,104,256]{2,1,0:T(8,128)(2,1)}), bf16[8,104,256]{2,1,0:T(8,128)(2,1)S(1)}, u32[]{:S(2)}, u32[]{:S(2)}) %all-to-all-start.6) | async-done | bytes 426016 | tf_op jit(solution)/shard_map/all_to_all | solution.py:681
  208.4 3.7 %all-to-all-start.9 = ((bf16[8,64,256]{2,1,0:T(8,128)(2,1)}), bf16[8,64,256]{2,1,0:T(8,128)(2,1)S(1)}, u32[]{:S(2)}, u32[]{:S(2)}) async-start(bf16[8,64,256]{2,1,0:T(8,128)(2,1)} %broadcast_in_dim.19), calls=%async_computation.9 | async-start | bytes 524288 | tf_op jit(solution)/shard_map/all_to_all | solution.py:685
  215.6 4.7 %all-to-all-done.9 = bf16[8,64,256]{2,1,0:T(8,128)(2,1)S(1)} async-done(((bf16[8,64,256]{2,1,0:T(8,128)(2,1)}), bf16[8,64,256]{2,1,0:T(8,128)(2,1)S(1)}, u32[]{:S(2)}, u32[]{:S(2)}) %all-to-all-start.9) | async-done | bytes 262176 | tf_op jit(solution)/shard_map/all_to_all | solution.py:685
  225.2 11.0 %all-to-all-done.7 = bf16[8,104,256]{2,1,0:T(8,128)(2,1)S(1)} async-done(((bf16[8,104,256]{2,1,0:T(8,128)(2,1)}), bf16[8,104,256]{2,1,0:T(8,128)(2,1)S(1)}, u32[]{:S(2)}, u32[]{:S(2)}) %all-to-all-start.7) | async-done | bytes 426016 | tf_op jit(solution)/shard_map/all_to_all | solution.py:685
  236.2 3.7 %all-to-all-start.5 = ((bf16[32,56,256]{2,1,0:T(8,128)(2,1)}), bf16[32,56,256]{2,1,0:T(8,128)(2,1)S(1)}, u32[]{:S(2)}, u32[]{:S(2)}) async-start(bf16[32,56,256]{2,1,0:T(8,128)(2,1)} %split.1), calls=%async_computation.5 | async-start | bytes 1835008 | tf_op jit(solution)/shard_map/all_to_all | solution.py:886
  244.5 5.9 %collective-permute-done.13 = bf16[512,256]{1,0:T(8,128)(2,1)S(1)} collective-permute-done((bf16[512,256]{1,0:T(8,128)(2,1)S(1)}, bf16[512,256]{1,0:T(8,128)(2,1)S(1)}, u32[]{:S(2)}, u32[]{:S(2)}) %collective-permute-start.13) | collective-permute-done | bytes 262176 | tf_op jit(solution)/shard_map/ppermute | solution.py:661
  251.3 6.1 %collective-permute-done.9 = bf16[832,256]{1,0:T(8,128)(2,1)S(1)} collective-permute-done((bf16[832,256]{1,0:T(8,128)(2,1)S(1)}, bf16[832,256]{1,0:T(8,128)(2,1)S(1)}, u32[]{:S(2)}, u32[]{:S(2)}) %collective-permute-start.9) | collective-permute-done | bytes 426016 | tf_op jit(solution)/shard_map/ppermute | solution.py:661
  (165 shorter events, 87.2 us)
Async XLA Ops:
  7.7 30.3 %all-to-all-start = ((bf16[32,56,256]{2,1,0:T(8,128)(2,1)}), bf16[32,56,256]{2,1,0:T(8,128)(2,1)S(1)}, u32[]{:S(2)}, u32[]{:S(2)}) async-start(bf16[32,56,256]{2,1,0:T(8,128)(2,1)} %pick.1), calls=%async_computation | async-start | bytes 1835008 | tf_op jit(solution)/shard_map/all_to_all | solution.py:743
  38.1 11.7 %all-to-all-start.2 = ((bf16[4,4,56,256]{3,2,1,0:T(8,128)(2,1)}), bf16[4,4,56,256]{3,2,1,0:T(8,128)(2,1)S(1)}, u32[]{:S(2)}, u32[]{:S(2)}) async-start(bf16[4,4,56,256]{3,2,1,0:T(8,128)(2,1)} %bitcast.5), calls=%async_computation.2 | async-start | bytes 917504 | tf_op jit(solution)/shard_map/all_to_all | solution.py:739
  49.8 11.6 %all-to-all-start.1 = ((bf16[4,4,56,256]{3,2,1,0:T(8,128)(2,1)}), bf16[4,4,56,256]{3,2,1,0:T(8,128)(2,1)S(1)}, u32[]{:S(2)}, u32[]{:S(2)}) async-start(bf16[4,4,56,256]{3,2,1,0:T(8,128)(2,1)} %bitcast.75), calls=%async_computation.1 | async-start | bytes 917504 | tf_op jit(solution)/shard_map/all_to_all | solution.py:739
  146.8 12.9 %collective-permute-start.7 = (bf16[1664,256]{1,0:T(8,128)(2,1)}, bf16[1664,256]{1,0:T(8,128)(2,1)}, u32[]{:S(2)}, u32[]{:S(2)}) collective-permute-start(bf16[1664,256]{1,0:T(8,128)(2,1)} %constant_dynamic-slice_fusion.3), channel_id=1, source_target_pairs={{0,1},{1,0},{2,3},{3,2},{4,5},{5,4},{6,7},{7,6},{8,9},{9,8},{10,11... | collective-permute-start | bytes 2555912 | tf_op jit(solution)/shard_map/ppermute | solution.py:661
  147.4 5.1 %collective-permute-start.1 = (bf16[208,256]{1,0:T(8,128)(2,1)S(1)}, bf16[208,256]{1,0:T(8,128)(2,1)S(1)}, u32[]{:S(2)}, u32[]{:S(2)}) collective-permute-start(bf16[208,256]{1,0:T(8,128)(2,1)S(1)} %constant_dynamic-slice_fusion.4), channel_id=1, source_target_pairs={{0,2},{2,0},{1,3},{3,1},{4,6},{6,4},{5,7},{7,5},{8,10},{10,8},{9,1... | collective-permute-start | bytes 319496 | tf_op jit(solution)/shard_map/ppermute | solution.py:661
  147.9 9.8 %collective-permute-start.11 = (bf16[1024,256]{1,0:T(8,128)(2,1)S(1)}, bf16[1024,256]{1,0:T(8,128)(2,1)S(1)}, u32[]{:S(2)}, u32[]{:S(2)}) collective-permute-start(bf16[1024,256]{1,0:T(8,128)(2,1)S(1)} %constant_dynamic-slice_fusion.1), channel_id=1, source_target_pairs={{0,1},{1,0},{2,3},{3,2},{4,5},{5,4},{6,7},{7,6},{8,9},{9,8},{10,11... | collective-permute-start | bytes 1572872 | tf_op jit(solution)/shard_map/ppermute | solution.py:661
  152.5 5.1 %collective-permute-start.2 = (bf16[208,256]{1,0:T(8,128)(2,1)S(1)}, bf16[208,256]{1,0:T(8,128)(2,1)S(1)}, u32[]{:S(2)}, u32[]{:S(2)}) collective-permute-start(bf16[208,256]{1,0:T(8,128)(2,1)S(1)} %add_convert_fusion.8), channel_id=1, source_target_pairs={{0,4},{4,0},{8,12},{12,8},{16,20},{20,16},{24,28},{28,24},{1,5},{5... | collective-permute-start | bytes 319496 | tf_op jit(solution)/shard_map/ppermute | solution.py:695
  153.9 12.1 %all-to-all-start.3 = ((bf16[4,4,56,256]{3,2,1,0:T(8,128)(2,1)}), bf16[4,4,56,256]{3,2,1,0:T(8,128)(2,1)S(1)}, u32[]{:S(2)}, u32[]{:S(2)}) async-start(bf16[4,4,56,256]{3,2,1,0:T(8,128)(2,1)} %get-tuple-element.37), calls=%async_computation.3 | async-start | bytes 917504 | tf_op jit(solution)/shard_map/all_to_all | solution.py:739
  157.6 23.8 %collective-permute-start.3 = (bf16[208,256]{1,0:T(8,128)(2,1)S(1)}, bf16[208,256]{1,0:T(8,128)(2,1)}, u32[]{:S(2)}, u32[]{:S(2)}) collective-permute-start(bf16[208,256]{1,0:T(8,128)(2,1)S(1)} %add_convert_fusion.7), channel_id=1, source_target_pairs={{0,8},{4,12},{8,0},{12,4},{16,24},{20,28},{24,16},{28,20},{1,9},{5... | collective-permute-start | bytes 319496 | tf_op jit(solution)/shard_map/ppermute | solution.py:695
  157.9 13.6 %collective-permute-start.12 = (bf16[512,256]{1,0:T(8,128)(2,1)S(1)}, bf16[512,256]{1,0:T(8,128)(2,1)S(1)}, u32[]{:S(2)}, u32[]{:S(2)}) collective-permute-start(bf16[512,256]{1,0:T(8,128)(2,1)S(1)} %constant_dynamic-slice_fusion), channel_id=1, source_target_pairs={{0,2},{2,0},{1,3},{3,1},{4,6},{6,4},{5,7},{7,5},{8,10},{10,8},{9,1... | collective-permute-start | bytes 786440 | tf_op jit(solution)/shard_map/ppermute | solution.py:661
  166.0 12.1 %all-to-all-start.4 = ((bf16[4,4,56,256]{3,2,1,0:T(8,128)(2,1)}), bf16[4,4,56,256]{3,2,1,0:T(8,128)(2,1)S(1)}, u32[]{:S(2)}, u32[]{:S(2)}) async-start(bf16[4,4,56,256]{3,2,1,0:T(8,128)(2,1)} %get-tuple-element.51), calls=%async_computation.4 | async-start | bytes 917504 | tf_op jit(solution)/shard_map/all_to_all | solution.py:739
  169.5 17.3 %collective-permute-start.8 = (bf16[832,256]{1,0:T(8,128)(2,1)S(1)}, bf16[832,256]{1,0:T(8,128)(2,1)}, u32[]{:S(2)}, u32[]{:S(2)}) collective-permute-start(bf16[832,256]{1,0:T(8,128)(2,1)S(1)} %constant_dynamic-slice_fusion.2), channel_id=1, source_target_pairs={{0,2},{2,0},{1,3},{3,1},{4,6},{6,4},{5,7},{7,5},{8,10},{10,8},{9,1... | collective-permute-start | bytes 1277960 | tf_op jit(solution)/shard_map/ppermute | solution.py:661
  178.0 15.2 %all-to-all-start.8 = ((bf16[8,64,256]{2,1,0:T(8,128)(2,1)}), bf16[8,64,256]{2,1,0:T(8,128)(2,1)S(1)}, u32[]{:S(2)}, u32[]{:S(2)}) async-start(bf16[8,64,256]{2,1,0:T(8,128)(2,1)} %bitcast.25), calls=%async_computation.8 | async-start | bytes 524288 | tf_op jit(solution)/shard_map/all_to_all | solution.py:681
  182.4 14.4 %collective-permute-start.4 = (bf16[208,256]{1,0:T(8,128)(2,1)S(1)}, bf16[208,256]{1,0:T(8,128)(2,1)S(1)}, u32[]{:S(2)}, u32[]{:S(2)}) collective-permute-start(bf16[208,256]{1,0:T(8,128)(2,1)S(1)} %add_convert_fusion.6), channel_id=1, source_target_pairs={{0,16},{4,20},{8,24},{12,28},{16,0},{20,4},{24,8},{28,12},{1,17},{... | collective-permute-start | bytes 319496 | tf_op jit(solution)/shard_map/ppermute | solution.py:695
  193.3 14.4 %all-to-all-start.6 = ((bf16[8,104,256]{2,1,0:T(8,128)(2,1)}), bf16[8,104,256]{2,1,0:T(8,128)(2,1)S(1)}, u32[]{:S(2)}, u32[]{:S(2)}) async-start(bf16[8,104,256]{2,1,0:T(8,128)(2,1)} %bitcast.16), calls=%async_computation.6 | async-start | bytes 851968 | tf_op jit(solution)/shard_map/all_to_all | solution.py:681
  196.8 4.8 %collective-permute-start.5 = (bf16[208,256]{1,0:T(8,128)(2,1)S(1)}, bf16[208,256]{1,0:T(8,128)(2,1)S(1)}, u32[]{:S(2)}, u32[]{:S(2)}) collective-permute-start(bf16[208,256]{1,0:T(8,128)(2,1)S(1)} %add_convert_fusion.5), channel_id=1, source_target_pairs={{0,2},{2,0},{1,3},{3,1},{4,6},{6,4},{5,7},{7,5},{8,10},{10,8},{9,1... | collective-permute-start | bytes 319496 | tf_op jit(solution)/shard_map/ppermute | solution.py:661
  201.6 13.8 %collective-permute-start.6 = (bf16[416,256]{1,0:T(8,128)(2,1)S(1)}, bf16[416,256]{1,0:T(8,128)(2,1)S(1)}, u32[]{:S(2)}, u32[]{:S(2)}) collective-permute-start(bf16[416,256]{1,0:T(8,128)(2,1)S(1)} %pad_maximum_fusion.6), channel_id=1, source_target_pairs={{0,1},{1,0},{2,3},{3,2},{4,5},{5,4},{6,7},{7,6},{8,9},{9,8},{10,11... | collective-permute-start | bytes 638984 | tf_op jit(solution)/shard_map/ppermute | solution.py:661
  208.4 11.9 %all-to-all-start.9 = ((bf16[8,64,256]{2,1,0:T(8,128)(2,1)}), bf16[8,64,256]{2,1,0:T(8,128)(2,1)S(1)}, u32[]{:S(2)}, u32[]{:S(2)}) async-start(bf16[8,64,256]{2,1,0:T(8,128)(2,1)} %broadcast_in_dim.19), calls=%async_computation.9 | async-start | bytes 524288 | tf_op jit(solution)/shard_map/all_to_all | solution.py:685
  221.1 15.2 %all-to-all-start.7 = ((bf16[8,104,256]{2,1,0:T(8,128)(2,1)}), bf16[8,104,256]{2,1,0:T(8,128)(2,1)S(1)}, u32[]{:S(2)}, u32[]{:S(2)}) async-start(bf16[8,104,256]{2,1,0:T(8,128)(2,1)} %broadcast_in_dim.18), calls=%async_computation.7 | async-start | bytes 851968 | tf_op jit(solution)/shard_map/all_to_all | solution.py:685
  236.2 26.7 %all-to-all-start.5 = ((bf16[32,56,256]{2,1,0:T(8,128)(2,1)}), bf16[32,56,256]{2,1,0:T(8,128)(2,1)S(1)}, u32[]{:S(2)}, u32[]{:S(2)}) async-start(bf16[32,56,256]{2,1,0:T(8,128)(2,1)} %split.1), calls=%async_computation.5 | async-start | bytes 1835008 | tf_op jit(solution)/shard_map/all_to_all | solution.py:886
  241.2 9.2 %collective-permute-start.13 = (bf16[512,256]{1,0:T(8,128)(2,1)S(1)}, bf16[512,256]{1,0:T(8,128)(2,1)S(1)}, u32[]{:S(2)}, u32[]{:S(2)}) collective-permute-start(bf16[512,256]{1,0:T(8,128)(2,1)S(1)} %bitcast.77), channel_id=1, source_target_pairs={{0,2},{2,0},{1,3},{3,1},{4,6},{6,4},{5,7},{7,5},{8,10},{10,8},{9,1... | collective-permute-start | bytes 786440 | tf_op jit(solution)/shard_map/ppermute | solution.py:661
  243.2 14.3 %collective-permute-start.9 = (bf16[832,256]{1,0:T(8,128)(2,1)S(1)}, bf16[832,256]{1,0:T(8,128)(2,1)S(1)}, u32[]{:S(2)}, u32[]{:S(2)}) collective-permute-start(bf16[832,256]{1,0:T(8,128)(2,1)S(1)} %bitcast.76), channel_id=1, source_target_pairs={{0,2},{2,0},{1,3},{3,1},{4,6},{6,4},{5,7},{7,5},{8,10},{10,8},{9,1... | collective-permute-start | bytes 1277960 | tf_op jit(solution)/shard_map/ppermute | solution.py:661
  251.3 18.0 %collective-permute-start.14 = (bf16[1024,256]{1,0:T(8,128)(2,1)}, bf16[1024,256]{1,0:T(8,128)(2,1)S(1)}, u32[]{:S(2)}, u32[]{:S(2)}) collective-permute-start(bf16[1024,256]{1,0:T(8,128)(2,1)} %pad_maximum_fusion.5), channel_id=1, source_target_pairs={{0,1},{1,0},{2,3},{3,2},{4,5},{5,4},{6,7},{7,6},{8,9},{9,8},{10,11... | collective-permute-start | bytes 1572872 | tf_op jit(solution)/shard_map/ppermute | solution.py:661
  258.5 13.5 %collective-permute-start.10 = (bf16[1664,256]{1,0:T(8,128)(2,1)}, bf16[1664,256]{1,0:T(8,128)(2,1)}, u32[]{:S(2)}, u32[]{:S(2)}) collective-permute-start(bf16[1664,256]{1,0:T(8,128)(2,1)} %pad_maximum_fusion.3), channel_id=1, source_target_pairs={{0,1},{1,0},{2,3},{3,2},{4,5},{5,4},{6,7},{7,6},{8,9},{9,8},{10,11... | collective-permute-start | bytes 2555912 | tf_op jit(solution)/shard_map/ppermute | solution.py:661
  (17 other events, 118.4 us)

commit v2 on v1

--- a/solution.py
+++ b/solution.py
@@ -64,10 +64,11 @@
     return jnp.sum(values.reshape(count // 8, 8, width), axis=0)
 
 
-def scale_rows(scale_ref, column, rows_of):
-    return jnp.concatenate(
-        [jnp.full((PAD, 1), scale_ref[i, column], F32) for i in range(rows_of)], axis=0
-    )
+def scale_rows(place_ref, mask_ref, column):
+    scales = [
+        mask_ref[column, 4 * place_ref[3] + i].astype(F32) * 1.25 for i in range(4)
+    ]
+    return jnp.concatenate([jnp.full((PAD, 1), scale, F32) for scale in scales], axis=0)
 
 
 def add_row(acc_ref, row, values):
@@ -220,7 +221,7 @@
             clean = jnp.where(valid_rows(values.shape), values, 0.0)
             position = window_conv(
                 column_shifts(clean, across),
-                lambda i, j: conv_k[block, 3 * i + j : 3 * i + j + 1, lane : lane + HALF],
+                lambda i, j: conv_k[i, j, block : block + 1, lane : lane + HALF],
                 across,
             )
             put_window(
@@ -271,7 +272,7 @@
                     conv_acc[3 * i + j, :, lane : lane + HALF] += jnp.sum(moved * shifts[j], axis=0)
             back = window_conv(
                 column_shifts(out_delta, across),
-                lambda i, j: conv_k[block, 8 - 3 * i - j : 9 - 3 * i - j, lane : lane + HALF],
+                lambda i, j: conv_k[2 - i, 2 - j, block : block + 1, lane : lane + HALF],
                 across,
             )
             values_delta = jnp.where(keep, values_delta + back, 0.0)
@@ -284,17 +285,57 @@
     return pl.ds(pl.multiple_of(t * 4 * PAD, 4 * PAD), 4 * PAD)
 
 
-def put_squares(out_ref, at, values, side):
+def put_rows(bundle, at, values):
+    place_ref, keep, away = bundle
+    values = values.astype(BF)
+    half = keep.shape[0]
+    count = values.shape[0]
+    cuts = [at, at + count] if at >= half or at + count <= half else [at, half, at + count]
+    for first, last in zip(cuts[:-1], cuts[1:]):
+        number = first // half
+        piece = values[first - at : last - at]
+        place = slice(first - number * half, last - number * half)
+
+        @pl.when(place_ref[2] == number)
+        def _(piece=piece, place=place):
+            keep[place, :] = piece
+
+        @pl.when(place_ref[2] != number)
+        def _(piece=piece, place=place):
+            away[place, :] = piece
+
+
+def put_squares(bundle, at, values, side):
     for part in range(values.shape[1] // side):
-        out_ref[at + part * side : at + (part + 1) * side, :] = values[
-            :, part * side : (part + 1) * side
-        ].astype(BF)
+        put_rows(bundle, at + part * side, values[:, part * side : (part + 1) * side])
+
+
+def load_tiles(place_ref, tiles, hidden):
+    for d, tile in enumerate(tiles):
+        rows = chunk(jnp.bitwise_xor(place_ref[3], d))
+        hidden[rows, :] = tile[...].astype(F32).reshape(4 * PAD, hidden.shape[1])
+
+
+def store_tile(place_ref, tiles, t, values):
+    values = values.reshape(tiles[0].shape).astype(BF)
+    for d, tile in enumerate(tiles):
+
+        @pl.when(jnp.bitwise_xor(place_ref[3], d) == t)
+        def _(tile=tile):
+            tile[...] = values
 
 
 def first_kernel(
-    scale_ref,
-    mixed_ref,
-    cot_ref,
+    place_ref,
+    mask_ref,
+    mixed_a,
+    mixed_b,
+    mixed_c,
+    mixed_d,
+    cot_a,
+    cot_b,
+    cot_c,
+    cot_d,
     gains,
     shifts,
     entry_w,
@@ -307,8 +348,12 @@
     expand_b,
     shrink_w,
     shrink_b,
-    act_out,
-    bundle_out,
+    act_a,
+    act_b,
+    act_c,
+    act_d,
+    keep_out,
+    away_out,
     vec_out,
     active0_out,
     slope0_out,
@@ -331,11 +376,10 @@
 ):
     width = hidden.shape[1]
     hidden_units = expand_w.shape[2]
+    bundle = (place_ref, keep_out, away_out)
     vec_out[...] = jnp.zeros(vec_out.shape, F32)
-
-    @pl.loop(0, 16)
-    def _(n):
-        hidden[pl.ds(pl.multiple_of(n * PAD, 8), PAD), :] = mixed_ref[n // 4, n % 4].astype(F32)
+    load_tiles(place_ref, (mixed_a, mixed_b, mixed_c, mixed_d), hidden)
+    load_tiles(place_ref, (cot_a, cot_b, cot_c, cot_d), grad_out)
 
     for block in range(2):
         win_out, chance_out, stripe_out = (
@@ -352,16 +396,16 @@
             striped = stripe[rows, :].astype(BF)
             stripe_out[rows, :] = striped
             branch = dot_nn(striped, exit_w[block]) + exit_b[block : block + 1, :]
-            midway = hidden[rows, :] + scale_rows(scale_ref, 2 * block, 4) * branch
+            midway = hidden[rows, :] + scale_rows(place_ref, mask_ref, 2 * block) * branch
             if block == 0:
                 mid0_out[rows, :] = midway
             hat, inverse = norm_parts(midway)
             normed = (hat * gains[block, 1:2, :] + shifts[block, 1:2, :]).astype(BF)
-            feed_scale = scale_rows(scale_ref, 2 * block + 1, 4)
+            feed_scale = scale_rows(place_ref, mask_ref, 2 * block + 1)
             feed = shrink_b[block : block + 1, :]
             if block == 1:
                 inner1[rows, :] = normed
-                gradient = jnp.concatenate([cot_ref[t, i] for i in range(4)], axis=0).astype(F32)
+                gradient = grad_out[rows, :]
                 feed_delta = (feed_scale * gradient).astype(BF)
                 feed1[rows, :] = feed_delta
                 add_row(vec_out, 4, row_sums(feed_delta.astype(F32)))
@@ -387,26 +431,27 @@
                 hidden[rows, :] = output
                 hidden1_out[rows, :] = output
             else:
-                for i in range(4):
-                    act_out[t, i] = output[i * PAD : (i + 1) * PAD].astype(BF)
+                store_tile(place_ref, (act_a, act_b, act_c, act_d), t, output)
                 add_row(vec_out, 5, row_sums(inner_delta * hat))
                 add_row(vec_out, 6, row_sums(inner_delta))
                 grad_out[rows, :] = gradient + norm_back(
                     inner_delta, hat, inverse, gains[block, 1:2, :]
                 )
 
-    put_squares(bundle_out, 0, dot_tn(inner1[...], pre1[...]), width)
+    put_squares(bundle, 0, dot_tn(inner1[...], pre1[...]), width)
     for part in range(hidden_units // width):
-        bundle_out[hidden_units + part * width : hidden_units + (part + 1) * width, :] = dot_tn(
-            active1[:, part * width : (part + 1) * width], feed1[...]
-        ).astype(BF)
-
-
-def delta_rows(block, scale_ref, exit_w, grad_ref, stripe_delta, branch_delta, vec_out, at):
+        put_rows(
+            bundle,
+            hidden_units + part * width,
+            dot_tn(active1[:, part * width : (part + 1) * width], feed1[...]),
+        )
+
+
+def delta_rows(block, place_ref, mask_ref, exit_w, grad_ref, stripe_delta, branch_delta, vec_out, at):
     @pl.loop(0, 4)
     def _(t):
         rows = chunk(t)
-        rounded = (scale_rows(scale_ref, 2 * block, 4) * grad_ref[rows, :]).astype(BF)
+        rounded = (scale_rows(place_ref, mask_ref, 2 * block) * grad_ref[rows, :]).astype(BF)
         branch_delta[rows, :] = rounded
         add_row(vec_out, at, row_sums(rounded.astype(F32)))
         out = round_bf(dot_nt(rounded, exit_w[block]))
@@ -436,7 +481,8 @@
 
 
 def second_kernel(
-    scale_ref,
+    place_ref,
+    mask_ref,
     grad_in,
     hidden1,
     stripe1,
@@ -453,7 +499,8 @@
     exit_w,
     expand_w,
     shrink_w,
-    bundle_out,
+    keep_out,
+    away_out,
     vec_out,
     conv_out,
     grad_out,
@@ -469,9 +516,10 @@
 ):
     width = grad.shape[1]
     hidden_units = expand_w.shape[2]
+    bundle = (place_ref, keep_out, away_out)
     vec_out[...] = jnp.zeros(vec_out.shape, F32)
     conv_out[...] = jnp.zeros(conv_out.shape, F32)
-    delta_rows(1, scale_ref, exit_w, grad_in, stripe_delta, branch_delta, vec_out, 0)
+    delta_rows(1, place_ref, mask_ref, exit_w, grad_in, stripe_delta, branch_delta, vec_out, 0)
     attention_backward(1, win1, chance1, conv_k, stripe_delta, wide, conv_out)
 
     def emit(t, rows, values):
@@ -480,8 +528,8 @@
     entry_backward(
         1, hidden1, gains, shifts, entry_w, grad_in, wide, wide_bf, normed_bf, vec_out, 2, emit
     )
-    put_squares(bundle_out, 0, dot_tn(normed_bf[...], wide_bf[...]), width)
-    bundle_out[3 * width : 4 * width, :] = dot_tn(stripe1[...], branch_delta[...]).astype(BF)
+    put_squares(bundle, 0, dot_tn(normed_bf[...], wide_bf[...]), width)
+    put_rows(bundle, 3 * width, dot_tn(stripe1[...], branch_delta[...]))
 
     @pl.loop(0, 4)
     def _(t):
@@ -489,7 +537,7 @@
         gradient = grad[rows, :]
         hat, inverse = norm_parts(mid0[rows, :])
         normed_bf[rows, :] = (hat * gains[0, 1:2, :] + shifts[0, 1:2, :]).astype(BF)
-        feed_delta = (scale_rows(scale_ref, 1, 4) * gradient).astype(BF)
+        feed_delta = (scale_rows(place_ref, mask_ref, 1) * gradient).astype(BF)
         feed0[rows, :] = feed_delta
         add_row(vec_out, 6, row_sums(feed_delta.astype(F32)))
         inner_delta = jnp.zeros((4 * PAD, width), F32)
@@ -506,196 +554,493 @@
         grad[rows, :] = gradient + norm_back(inner_delta, hat, inverse, gains[0, 1:2, :])
 
     grad_out[...] = grad[...]
-    put_squares(bundle_out, 4 * width, dot_tn(normed_bf[...], pre0[...]), width)
+    put_squares(bundle, 4 * width, dot_tn(normed_bf[...], pre0[...]), width)
     for part in range(hidden_units // width):
-        base = 8 * width + part * width
-        bundle_out[base : base + width, :] = dot_tn(
-            active0[:, part * width : (part + 1) * width], feed0[...]
-        ).astype(BF)
-    delta_rows(0, scale_ref, exit_w, grad, stripe_delta_out, branch_delta, vec_out, 13)
-    bundle_out[12 * width : 13 * width, :] = dot_tn(stripe0[...], branch_delta[...]).astype(BF)
+        put_rows(
+            bundle,
+            (8 + part) * width,
+            dot_tn(active0[:, part * width : (part + 1) * width], feed0[...]),
+        )
+    delta_rows(0, place_ref, mask_ref, exit_w, grad, stripe_delta_out, branch_delta, vec_out, 13)
+    put_rows(bundle, 12 * width, dot_tn(stripe0[...], branch_delta[...]))
 
 
 def third_kernel(
+    place_ref,
     grad_in,
     stripe_delta,
-    mixed_ref,
+    mixed_a,
+    mixed_b,
+    mixed_c,
+    mixed_d,
     win0,
     chance0,
     gains,
     shifts,
     entry_w,
     conv_k,
-    out_ref,
-    bundle_out,
-    vec_out,
-    conv_out,
+    vec1,
+    vec2,
+    conv2,
+    out_a,
+    out_b,
+    out_c,
+    out_d,
+    keep_out,
+    away_out,
     hidden,
     wide,
     wide_bf,
     normed_bf,
+    vec3,
+    conv3,
+    flat,
 ):
     width = hidden.shape[1]
-    vec_out[...] = jnp.zeros(vec_out.shape, F32)
-    conv_out[...] = jnp.zeros(conv_out.shape, F32)
-
-    @pl.loop(0, 16)
-    def _(n):
-        hidden[pl.ds(pl.multiple_of(n * PAD, 8), PAD), :] = mixed_ref[n // 4, n % 4].astype(F32)
-
-    attention_backward(0, win0, chance0, conv_k, stripe_delta, wide, conv_out)
+    bundle = (place_ref, keep_out, away_out)
+    vec3[...] = jnp.zeros(vec3.shape, F32)
+    conv3[...] = jnp.zeros(conv3.shape, F32)
+    load_tiles(place_ref, (mixed_a, mixed_b, mixed_c, mixed_d), hidden)
+    attention_backward(0, win0, chance0, conv_k, stripe_delta, wide, conv3)
 
     def emit(t, rows, values):
-        for i in range(4):
-            out_ref[t, i] = values[i * PAD : (i + 1) * PAD].astype(BF)
+        store_tile(place_ref, (out_a, out_b, out_c, out_d), t, values)
 
     entry_backward(
-        0, hidden, gains, shifts, entry_w, grad_in, wide, wide_bf, normed_bf, vec_out, 0, emit
-    )
-    put_squares(bundle_out, 0, dot_tn(normed_bf[...], wide_bf[...]), width)
-
-
-def pick_kernel(index_ref, images_ref, out_ref):
-    @pl.loop(0, out_ref.shape[0])
-    def _(s):
-        out_ref[s] = images_ref[jnp.minimum(index_ref[s], images_ref.shape[0] - 1)]
-
-
-def inside_box(corner_ref, n, start_ref):
-    token = lax.broadcasted_iota(jnp.int32, (PAD, 1), 0)
-    row = start_ref[0] + token // 8
-    col = start_ref[1] + token % 8
-    hit = (
-        (row >= corner_ref[n, 0])
-        & (row < corner_ref[n, 1])
-        & (col >= corner_ref[n, 2])
-        & (col < corner_ref[n, 3])
-    )
-    return jnp.where(hit, 1.0, 0.0)
-
-
-def mix_kernel(take_ref, corner_ref, ratio_ref, start_ref, arrived, images_ref, out_ref):
-    count = images_ref.shape[0]
+        0, hidden, gains, shifts, entry_w, grad_in, wide, wide_bf, normed_bf, vec3, 0, emit
+    )
+    flat[...] = jnp.zeros(flat.shape, F32)
+    at = 0
+    for ref in (vec1, vec2, conv2, vec3, conv3):
+        flat[at : at + ref.shape[0], :] = jnp.sum(ref[...], axis=1)
+        at += ref.shape[0]
+    spread = dot_tn(normed_bf[...], wide_bf[...])
+    half = keep_out.shape[0]
+    middle = width // 2
+    lots = flat.shape[0] // 2
+    put_rows(bundle, 0, spread[:, :width])
+    put_rows(bundle, width, spread[:middle, width : 2 * width])
+    put_rows(bundle, width + middle, flat[:lots, :])
+    put_rows(bundle, half, spread[middle:, width : 2 * width])
+    put_rows(bundle, half + middle, spread[:, 2 * width :])
+    put_rows(bundle, half + middle + width, flat[lots:, :])
+
+
+def untangle(source, flat, target):
+    count, width = source.shape[2:]
+    lanes = flat.shape[0]
+    for row in range(TILE):
+        flat[:, pl.ds(row * 8 + 7, count, stride=PAD), :] = jnp.zeros((lanes, count, 128), F32)
+        for col in range(TILE):
+            token = source[row, col].astype(F32)
+            for lane in range(lanes):
+                flat[lane, pl.ds(row * 8 + col, count, stride=PAD), :] = token[
+                    :, lane * 128 : (lane + 1) * 128
+                ]
 
     @pl.loop(0, count)
     def _(n):
-        inside = inside_box(corner_ref, n, start_ref)
-        ratio = ratio_ref[n]
-        own = images_ref[n].astype(F32)
-        blend = arrived[take_ref[n]].astype(F32)
-        cut = arrived[take_ref[count + n]].astype(F32)
-        mixed = inside * cut + (1.0 - inside) * (ratio * own + (1.0 - ratio) * blend)
-        out_ref[n] = mixed.astype(BF)
-
-
-def split_kernel(take_ref, corner_ref, ratio_ref, start_ref, grad_ref, out_ref):
-    count = grad_ref.shape[0]
-    out_ref[...] = jnp.zeros(out_ref.shape, BF)
-
-    @pl.loop(0, count)
-    def _(n):
-        inside = inside_box(corner_ref, n, start_ref)
-        gradient = grad_ref[n].astype(F32)
-        cut = inside * gradient
-        out_ref[take_ref[n]] = ((1.0 - ratio_ref[n]) * (gradient - cut)).astype(BF)
-        out_ref[take_ref[count + n]] = cut.astype(BF)
-
-
-def join_kernel(index_ref, corner_ref, ratio_ref, start_ref, grad_ref, back_ref, out_ref, total):
-    count = grad_ref.shape[0]
-
-    @pl.loop(0, count)
-    def _(n):
-        outside = 1.0 - inside_box(corner_ref, n, start_ref)
-        total[n] = ratio_ref[n] * outside * grad_ref[n].astype(F32)
+        rows = pl.ds(pl.multiple_of(n * PAD, 8), PAD)
+        tile = jnp.concatenate([flat[lane, rows, :] for lane in range(lanes)], axis=1)
+        target(n, tile.reshape(TILE, 8, width).astype(BF))
+
+
+def owner_of(wanted, count):
+    if count & (count - 1) == 0:
+        return lax.shift_right_logical(wanted, count.bit_length() - 1)
+    return lax.div(wanted, count)
+
+
+def pick_kernel(
+    place_ref, mix_ref, cut_ref, images_ref, index_out, take_out, sent_out, own_out, flat, counts
+):
+    count = images_ref.shape[2]
+    slots = sent_out.shape[0]
+    capacity = slots // counts.shape[0]
+    me = place_ref[0]
+
+    def put(n, tile):
+        own_out[n] = tile
+
+    untangle(images_ref, flat, put)
+
+    @pl.loop(0, slots, unroll=8)
+    def _(s):
+        index_out[s] = count
+
+    @pl.loop(0, counts.shape[0])
+    def _(g):
+        counts[g] = 0
+        rank = g * capacity
+        for ref in (mix_ref, cut_ref):
+            for j in range(count):
+                wanted = ref[g * count + j]
+                owner = owner_of(wanted, count)
+                hit = owner == me
+                index_out[jnp.where(hit, rank, slots)] = wanted - owner * count
+                rank = rank + hit.astype(jnp.int32)
+
+    @pl.loop(0, slots)
+    def _(s):
+        sent_out[s] = own_out[jnp.minimum(index_out[s], count - 1)]
+
+    for part, ref in enumerate((mix_ref, cut_ref)):
+
+        @pl.loop(0, count)
+        def _(j, part=part, ref=ref):
+            owner = owner_of(ref[me * count + j], count)
+            rank = counts[owner]
+            take_out[part * count + j] = owner * capacity + rank
+            counts[owner] = rank + 1
+
+
+def deal_kernel(place_ref, source, out_a, out_b, out_c, out_d, flat):
+    outs = (out_a, out_b, out_c, out_d)
+    share = out_a.shape[0]
+
+    def put(n, tile):
+        for d, out in enumerate(outs):
+
+            @pl.when(jnp.bitwise_xor(place_ref[3], d) == n // share)
+            def _(out=out):
+                out[n % share] = tile
+
+    untangle(source, flat, put)
+
+
+def inside_box(corner_ref, n, place_ref):
+    shape = (TILE, 8, 1)
+    row = place_ref[1] * TILE + lax.broadcasted_iota(jnp.int32, shape, 0)
+    col = place_ref[2] * TILE + lax.broadcasted_iota(jnp.int32, shape, 1)
+    hit = (
+        (row >= corner_ref[0, n])
+        & (row < corner_ref[1, n])
+        & (col >= corner_ref[2, n])
+        & (col < corner_ref[3, n])
+    )
+    return jnp.where(hit, 1.0, 0.0)
+
+
+def mix_kernel(
+    place_ref, take_ref, corner_ref, ratio_ref, arrived, own_ref, out_a, out_b, out_c, out_d
+):
+    count = own_ref.shape[0]
+    share = out_a.shape[0]
+    for d, out in enumerate((out_a, out_b, out_c, out_d)):
+
+        @pl.loop(0, share)
+        def _(i, d=d, out=out):
+            n = jnp.bitwise_xor(place_ref[3], d) * share + i
+            inside = inside_box(corner_ref, n, place_ref)
+            ratio = ratio_ref[n]
+            own = own_ref[n].astype(F32)
+            blend = arrived[take_ref[n]].astype(F32)
+            cut = arrived[take_ref[count + n]].astype(F32)
+            mixed = inside * cut + (1.0 - inside) * (ratio * own + (1.0 - ratio) * blend)
+            out[i] = mixed.astype(BF)
+
+
+def split_kernel(
+    place_ref, take_ref, corner_ref, ratio_ref, grad_a, grad_b, grad_c, grad_d, out_ref
+):
+    share = grad_a.shape[0]
+    count = 4 * share
+    if out_ref.shape[0] > 2 * count:
+        out_ref[...] = jnp.zeros(out_ref.shape, BF)
+    for d, grad_ref in enumerate((grad_a, grad_b, grad_c, grad_d)):
+
+        @pl.loop(0, share)
+        def _(i, d=d, grad_ref=grad_ref):
+            n = jnp.bitwise_xor(place_ref[3], d) * share + i
+            inside = inside_box(corner_ref, n, place_ref)
+            gradient = grad_ref[i].astype(F32)
+            cut = inside * gradient
+            out_ref[take_ref[n]] = ((1.0 - ratio_ref[n]) * (gradient - cut)).astype(BF)
+            out_ref[take_ref[count + n]] = cut.astype(BF)
+
+
+def join_kernel(
+    place_ref,
+    index_ref,
+    corner_ref,
+    ratio_ref,
+    grad_a,
+    grad_b,
+    grad_c,
+    grad_d,
+    back_ref,
+    out_ref,
+    total,
+):
+    count, width = out_ref.shape[2:]
+    share = grad_a.shape[0]
+
+    def tile_rows(n):
+        return pl.ds(pl.multiple_of(n * PAD, 8), PAD)
+
+    for d, grad_ref in enumerate((grad_a, grad_b, grad_c, grad_d)):
+
+        @pl.loop(0, share)
+        def _(i, d=d, grad_ref=grad_ref):
+            n = jnp.bitwise_xor(place_ref[3], d) * share + i
+            outside = 1.0 - inside_box(corner_ref, n, place_ref)
+            kept = ratio_ref[n] * outside * grad_ref[i].astype(F32)
+            kept = kept.reshape(PAD, width)
+            for lane in range(total.shape[0]):
+                total[lane, tile_rows(n), :] = kept[:, lane * 128 : (lane + 1) * 128]
 
     @pl.loop(0, back_ref.shape[0])
     def _(s):
-        total[index_ref[s]] += back_ref[s].astype(F32)
-
-    @pl.loop(0, count)
-    def _(n):
-        out_ref[n] = total[n].reshape(TILE, 8, total.shape[2])[:, :TILE, :]
+        piece = back_ref[s].astype(F32).reshape(PAD, width)
+        for lane in range(total.shape[0]):
+            total[lane, tile_rows(index_ref[s]), :] += piece[:, lane * 128 : (lane + 1) * 128]
+
+    for row in range(TILE):
+        for col in range(TILE):
+            out_ref[row, col] = jnp.concatenate(
+                [
+                    total[lane, pl.ds(row * 8 + col, count, stride=PAD), :]
+                    for lane in range(total.shape[0])
+                ],
+                axis=1,
+            )
+
+
+def lay_kernel(place_ref, act_a, act_b, act_c, act_d, out_ref, flat):
+    count, width = out_ref.shape[2:]
+    share = act_a.shape[0]
+    for d, act_ref in enumerate((act_a, act_b, act_c, act_d)):
+
+        @pl.loop(0, share)
+        def _(i, d=d, act_ref=act_ref):
+            n = jnp.bitwise_xor(place_ref[3], d) * share + i
+            tile = act_ref[i].astype(F32).reshape(PAD, width)
+            for lane in range(flat.shape[0]):
+                flat[lane, pl.ds(pl.multiple_of(n * PAD, 8), PAD), :] = tile[
+                    :, lane * 128 : (lane + 1) * 128
+                ]
+
+    for row in range(TILE):
+        for col in range(TILE):
+            out_ref[row, col] = jnp.concatenate(
+                [
+                    flat[lane, pl.ds(row * 8 + col, count, stride=PAD), :]
+                    for lane in range(flat.shape[0])
+                ],
+                axis=1,
+            ).astype(BF)
+
+
+def unpack_kernel(
+    place_ref,
+    mine1,
+    other1,
+    mine2,
+    other2,
+    gain_out,
+    shift_out,
+    entry_out,
+    entry_b_out,
+    conv_out,
+    conv_b_out,
+    exit_out,
+    exit_b_out,
+    expand_out,
+    expand_b_out,
+    shrink_out,
+    shrink_b_out,
+    vectors,
+):
+    width = exit_out.shape[1]
+    units = expand_out.shape[2]
+    upper = place_ref[2] == 1
+    middle = width // 2
+
+    def squares(out_ref, block, count):
+        return [(out_ref, block, 0, part * width, width) for part in range(count)]
+
+    def tall(out_ref, block, count):
+        return [(out_ref, block, part * width, 0, width) for part in range(count)]
+
+    plans = (
+        squares(expand_out, 1, units // width) + tall(shrink_out, 1, units // width),
+        squares(entry_out, 1, 3)
+        + tall(exit_out, 1, 1)
+        + squares(expand_out, 0, units // width)
+        + tall(shrink_out, 0, units // width)
+        + tall(exit_out, 0, 1),
+        [
+            (entry_out, 0, 0, 0, width),
+            (entry_out, 0, 0, width, middle),
+            (vectors, None, 0, 0, middle),
+            (entry_out, 0, middle, width, middle),
+            (entry_out, 0, 0, 2 * width, width),
+        ],
+    )
+    total = sum(plan[4] for plan in plans[1])
+    ranks = mine2.shape[0]
+    cut = total // 2 // ranks
+    for number, mine, other, base, count in (
+        (0, mine1, other1, 0, mine1.shape[1]),
+        (1, mine2, other2, 0, cut),
+        (2, mine2, other2, cut, mine2.shape[1] - cut),
+    ):
+        pieces = []
+        at = 0
+        for out_ref, block, first_row, lane, length in plans[number]:
+            done = 0
+            while done < length:
+                step = min(length - done, count - at % count)
+                pieces.append((at, step, out_ref, block, first_row + done, lane))
+                at += step
+                done += step
+        for at, step, out_ref, block, first_row, lane in pieces:
+            shard, start = at // count, at % count
+            half, shard = shard // ranks, shard % ranks
+            if number > 0:
+                shard = jnp.bitwise_xor(place_ref[4], shard)
+            here = upper if half == 1 else jnp.logical_not(upper)
+            rows = slice(base + start, base + start + step)
+            values = jnp.where(
+                here, mine[shard, rows, :].astype(F32), other[shard, rows, :].astype(F32)
+            )
+            place = slice(first_row, first_row + step)
+            if block is None:
+                out_ref[place, :] = values
+            else:
+                out_ref[block, place, lane : lane + width] = values
+
+    def line(n):
+        return vectors[n : n + 1, :]
+
+    gain_out[0] = jnp.concatenate([line(33), line(18)], axis=0)
+    gain_out[1] = jnp.concatenate([line(11), line(5)], axis=0)
+    shift_out[0] = jnp.concatenate([line(34), line(19)], axis=0)
+    shift_out[1] = jnp.concatenate([line(12), line(6)], axis=0)
+    for part in range(2):
+        lanes = slice(part * width, (part + 1) * width)
+        entry_b_out[:, lanes] = jnp.concatenate([line(31 + part), line(9 + part)], axis=0)
+    for i in range(3):
+        for j in range(3):
+            conv_out[i, j] = jnp.concatenate(
+                [line(35 + 3 * i + j), line(22 + 3 * i + j)], axis=0
+            )
+    conv_b_out[...] = jnp.concatenate([line(21), line(8)], axis=0)
+    exit_b_out[...] = jnp.concatenate([line(20), line(7)], axis=0)
+    for part in range(units // width):
+        lanes = slice(part * width, (part + 1) * width)
+        expand_b_out[:, lanes] = jnp.concatenate([line(14 + part), line(part)], axis=0)
+    shrink_b_out[...] = jnp.concatenate([line(13), line(4)], axis=0)
 
 
 SMEM = pl.BlockSpec(memory_space=pltpu.SMEM)
 VMEM = pl.BlockSpec(memory_space=pltpu.VMEM)
 
 
-def run(kernel, scalars, arrays, outs, scratch=(), flops=0, name=None):
-    out_shape = [jax.ShapeDtypeStruct(shape, dtype) for shape, dtype in outs]
+ANYWHERE = pl.BlockSpec(memory_space=pl.ANY)
+
+
+def run(kernel, scalars, arrays, outs, scratch=(), flops=0, name=None, after=(), scalar_outs=()):
+    given = len(scalars) + len(arrays)
+
+    def body(*refs):
+        kernel(*refs[:given], *refs[given + len(after) :])
+
+    out_shape = [jax.ShapeDtypeStruct(shape, dtype) for shape, dtype in scalar_outs + tuple(outs)]
     moved = sum(a.size * a.dtype.itemsize for a in arrays)
     return pl.pallas_call(
-        kernel,
+        body,
         out_shape=out_shape,
-        in_specs=[SMEM] * len(scalars) + [VMEM] * len(arrays),
-        out_specs=[VMEM] * len(outs),
-        scratch_shapes=[pltpu.VMEM(shape, dtype) for shape, dtype in scratch],
+        in_specs=[SMEM] * len(scalars) + [VMEM] * len(arrays) + [ANYWHERE] * len(after),
+        out_specs=[SMEM] * len(scalar_outs) + [VMEM] * len(outs),
+        scratch_shapes=[
+            kind if dtype is None else pltpu.VMEM(kind, dtype) for kind, dtype in scratch
+        ],
         compiler_params=pltpu.CompilerParams(vmem_limit_bytes=VMEM_BYTES),
         cost_estimate=pl.CostEstimate(flops=flops, bytes_accessed=moved, transcendentals=0),
         name=name,
-    )(*scalars, *arrays)
-
-
-def partner_plan(mix_partner, cut_partner, images_here, groups, device):
-    requests = jnp.concatenate(
-        [mix_partner.reshape(groups, images_here), cut_partner.reshape(groups, images_here)], axis=1
-    )
-    owners = requests // images_here
-    within = requests % images_here
-    wanted = 2 * images_here
-    before = jnp.arange(wanted)[None, :] < jnp.arange(wanted)[:, None]
-    rank = jnp.sum((owners[:, :, None] == owners[:, None, :]) & before[None], axis=2)
-    capacity = (wanted + groups - 1) // groups
-    chosen = (owners == device)[:, :, None] & (
-        rank[:, :, None] == jnp.arange(capacity)[None, None, :]
-    )
-    index = images_here + jnp.sum(
-        jnp.where(chosen, (within - images_here)[:, :, None], 0), axis=1
-    ).reshape(groups * capacity)
-    take = lax.dynamic_index_in_dim(owners * capacity + rank, device, 0, keepdims=False)
-    return index.astype(jnp.int32), take.astype(jnp.int32), capacity
+    )(*scalars, *arrays, *after)
+
+
+def gate(values, after):
+    values, after = list(values), list(after)
+
+    def body(*refs):
+        del refs
+
+    return pl.pallas_call(
+        body,
+        out_shape=[jax.ShapeDtypeStruct(v.shape, v.dtype) for v in values],
+        in_specs=[ANYWHERE] * (len(values) + len(after)),
+        out_specs=[ANYWHERE] * len(values),
+        input_output_aliases={i: i for i in range(len(values))},
+        name="gate",
+    )(*values, *after)
 
 
 def swap(values, axis):
     return lax.ppermute(values, axis, [(0, 1), (1, 0)])
 
 
-def halve(values, axis):
-    place = lax.axis_index(axis)
-    count = values.shape[0] // 2
-    away = lax.dynamic_slice_in_dim(values, (1 - place) * count, count, 0)
-    mine = lax.dynamic_slice_in_dim(values, place * count, count, 0)
-    return (mine.astype(F32) + swap(away, axis).astype(F32)).astype(BF)
-
-
-def unhalve(values, axis):
-    other = swap(values, axis)
-    first = lax.axis_index(axis) == 0
-    return jnp.concatenate([jnp.where(first, values, other), jnp.where(first, other, values)])
-
-
-def sum_spread(values, groups):
-    part = halve(halve(values, "col"), "row")
-    rows = part.shape[0] // groups
-    pieces = lax.all_to_all(
-        part.reshape(groups, rows, part.shape[1]), "dp", split_axis=0, concat_axis=0, tiled=True
-    )
+def added(values, others):
+    return (values.astype(F32) + others.astype(F32)).astype(BF)
+
+
+def shards(values, ranks):
+    return values.reshape(ranks, values.shape[0] // ranks, values.shape[1])
+
+
+def spread_sum(pieces):
     mine = jnp.sum(pieces.astype(F32), axis=0).astype(BF)
-    full = lax.all_to_all(
-        jnp.broadcast_to(mine[None], pieces.shape), "dp", split_axis=0, concat_axis=0, tiled=True
-    )
-    return unhalve(unhalve(full.reshape(part.shape), "row"), "col")
-
-
-def sum_doubling(values, groups):
-    part = halve(halve(values, "col"), "row")
-    step = 1
-    while step < groups:
-        other = lax.ppermute(part, "dp", [(i, i ^ step) for i in range(groups)])
-        part = (part.astype(F32) + other.astype(F32)).astype(BF)
-        step *= 2
-    return unhalve(unhalve(part, "row"), "col")
+    return jnp.broadcast_to(mine[None], pieces.shape)
+
+
+def across(values, axes, size, mask):
+    return lax.ppermute(values, axes, [(i, i ^ mask) for i in range(size)])
+
+
+def deal(parts):
+    return [parts[0]] + [across(parts[d], ("row", "col"), 4, d) for d in (1, 2, 3)]
+
+
+RANKS = ("dp", "row")
+
+
+def stages(ranks):
+    bits = ranks.bit_length() - 1
+    return [(bit, min(2, bits - bit)) for bit in range(0, bits, 2)]
+
+
+def scatter_send(values, ranks, stage):
+    bit, count = stage
+    size = 1 << count
+    me = (lax.axis_index(RANKS) >> bit) & (size - 1)
+    cut = values.reshape(size, values.shape[0] // size, values.shape[1])
+    return [lax.dynamic_index_in_dim(cut, me ^ d, 0, keepdims=False) for d in range(size)]
+
+
+def scatter_move(parts, ranks, stage):
+    return [parts[0]] + [
+        across(parts[d], RANKS, ranks, d << stage[0]) for d in range(1, len(parts))
+    ]
+
+
+def scatter_sum(parts):
+    return sum(part.astype(F32) for part in parts).astype(BF)
+
+
+def gather(values, ranks, stage):
+    return jnp.stack(
+        [values]
+        + [across(values, RANKS, ranks, d << stage[0]) for d in range(1, 1 << stage[1])]
+    )
+
+
+def rank_order(rank, ranks):
+    order = 0
+    for bit, count in stages(ranks):
+        order = order * (1 << count) + ((rank >> bit) & ((1 << count) - 1))
+    return order
 
 
 def local(
@@ -723,41 +1068,50 @@
     images_here = images.shape[0]
     width = images.shape[3]
     units = expand_weight.shape[2]
-    device = lax.axis_index("dp")
     row, col = lax.axis_index("row"), lax.axis_index("col")
-    start = jnp.stack([row * TILE, col * TILE]).astype(jnp.int32)
     share = images_here // 4
     rows = 4 * share * PAD
-    index, take, capacity = partner_plan(mix_partner, cut_partner, images_here, groups, device)
+    ranks = 2 * groups
+    capacity = (2 * images_here + groups - 1) // groups
     slots = groups * capacity
-
-    def padded(values):
-        wide = jnp.pad(values, ((0, 0), (0, 0), (0, 1), (0, 0)))
-        return wide.reshape(images_here, PAD, width)
-
-    def regroup(values):
-        return lax.all_to_all(values, ("row", "col"), split_axis=0, concat_axis=0, tiled=True)
-
-    own = padded(images)
-    (outgoing,) = run(pick_kernel, [index], [own], [((slots, PAD, width), BF)], name="pick")
+    order = rank_order(lax.axis_index(RANKS), ranks)
+    place = jnp.stack([lax.axis_index("dp"), row, col, 2 * row + col, order]).astype(jnp.int32)
+    quad = ((share, TILE, 8, width), BF)
+    corners = corners.T
+    masks = drop_masks.T
+    flat = ((width // 128, images_here * PAD, 128), F32)
+    index, take, outgoing, own = run(
+        pick_kernel,
+        [place, mix_partner, cut_partner],
+        [images.transpose(1, 2, 0, 3)],
+        [((slots, TILE, 8, width), BF), ((images_here, TILE, 8, width), BF)],
+        [flat, (pltpu.SMEM((groups,), jnp.int32), None)],
+        name="pick",
+        scalar_outs=(((slots + 8,), jnp.int32), ((2 * images_here,), jnp.int32)),
+    )
     arrived = lax.all_to_all(outgoing, "dp", split_axis=0, concat_axis=0, tiled=True)
-    cot = regroup(padded(cotangent).reshape(4, share, PAD, width))
-    (mixed,) = run(
-        mix_kernel,
-        [take, corners, ratios, start],
-        [arrived, own],
-        [((images_here, PAD, width), BF)],
-        name="mix",
-    )
-    mixed = regroup(mixed.reshape(4, share, PAD, width))
-    scales = lax.dynamic_slice_in_dim(
-        drop_masks.astype(F32) * 1.25, (2 * row + col) * share, share, 0
-    )
-    conv_k = position_kernel.reshape(2, 9, width)
+    cot = deal(
+        run(deal_kernel, [place], [cotangent.transpose(1, 2, 0, 3)], [quad] * 4, [flat], name="deal")
+    )
+    mixed = deal(
+        run(
+            mix_kernel,
+            [place, take, corners, ratios],
+            [arrived, own],
+            [quad] * 4,
+            name="mix",
+            after=cot,
+        )
+    )
+    conv_k = position_kernel.transpose(1, 2, 0, 3)
     tall = (rows, width)
     (
-        act,
-        bundle1,
+        act_a,
+        act_b,
+        act_c,
+        act_d,
+        keep1,
+        away1,
         vec1,
         active0,
         slope0,
@@ -772,10 +1126,10 @@
         grad1,
     ) = run(
         first_kernel,
-        [scales],
+        [place, masks],
         [
-            mixed,
-            cot,
+            *mixed,
+            *cot,
             norm_gains,
             norm_shifts,
             entry_weight,
@@ -790,8 +1144,9 @@
             shrink_bias,
         ],
         [
-            ((4, share, PAD, width), BF),
-            ((2 * units, width), BF),
+            *([quad] * 4),
+            ((units, width), BF),
+            ((units, width), BF),
             ((7, 8, width), F32),
             ((rows, units), BF),
             ((rows, units), BF),
@@ -814,14 +1169,15 @@
             (tall, BF),
             (tall, BF),
         ],
-        flops=10 * rows * width * width * 12,
+        flops=10 * rows * width * width * 120,
         name="first",
     )
-    sum1 = sum_spread(bundle1, groups)
-    act = regroup(act)
-    bundle2, vec2, conv2, grad0, delta0 = run(
+    sent1 = shards(added(keep1, swap(away1, "col")), ranks)
+    pieces1 = lax.all_to_all(sent1, RANKS, split_axis=0, concat_axis=0, tiled=True)
+    act = deal([act_a, act_b, act_c, act_d])
+    keep2, away2, vec2, conv2, grad0, delta0 = run(
         second_kernel,
-        [scales],
+        [place, masks],
         [
             grad1,
             hidden1,
@@ -841,7 +1197,8 @@
             shrink_weight,
         ],
         [
-            ((13 * width, width), BF),
+            ((13 * width // 2, width), BF),
+            ((13 * width // 2, width), BF),
             ((15, 8, width), F32),
             ((9, 8, width), F32),
             (tall, F32),
@@ -857,67 +1214,125 @@
             (tall, BF),
             ((rows, units), BF),
         ],
-        flops=6 * rows * width * width * 12,
+        flops=6 * rows * width * width * 120,
         name="second",
-    )
-    sum2 = sum_spread(bundle2, groups)
-    out_tiles, bundle3, vec3, conv3 = run(
+        after=[sent1],
+    )
+    keep2, away2, grad0, delta0 = gate([keep2, away2, grad0, delta0], [pieces1, *act])
+    spread1 = spread_sum(pieces1)
+    steps = stages(ranks)
+    parts2 = scatter_send(added(keep2, swap(away2, "col")), ranks, steps[0])
+    moved2 = scatter_move(parts2, ranks, steps[0])
+    *out_tiles, keep3, away3 = run(
         third_kernel,
-        [],
-        [grad0, delta0, mixed, win0, chance0, norm_gains, norm_shifts, entry_weight, conv_k],
+        [place],
         [
-            ((4, share, PAD, width), BF),
-            ((3 * width, width), BF),
+            grad0,
+            delta0,
+            *mixed,
+            win0,
+            chance0,
+            norm_gains,
+            norm_shifts,
+            entry_weight,
+            conv_k,
+            vec1,
+            vec2,
+            conv2,
+        ],
+        [quad] * 4 + [((2 * width, width), BF), ((2 * width, width), BF)],
+        [
+            (tall, F32),
+            ((rows, 3 * width), F32),
+            ((rows, 3 * width), BF),
+            (tall, BF),
             ((4, 8, width), F32),
             ((9, 8, width), F32),
-        ],
-        [(tall, F32), ((rows, 3 * width), F32), ((rows, 3 * width), BF), (tall, BF)],
-        flops=3 * rows * width * width * 12,
+            ((width, width), F32),
+        ],
+        flops=3 * rows * width * width * 120,
         name="third",
-    )
-    gradient = regroup(out_tiles).reshape(images_here, PAD, width)
+        after=parts2,
+    )
+    *held, keep3, away3 = gate([*moved2, keep3, away3], [])
+    moved2 = held
+    gradient = deal(out_tiles)
     (parted,) = run(
         split_kernel,
-        [take, corners, ratios, start],
-        [gradient],
-        [((slots, PAD, width), BF)],
+        [place, take, corners, ratios],
+        gradient,
+        [((slots, TILE, 8, width), BF)],
         name="split",
     )
     back = lax.all_to_all(parted, "dp", split_axis=0, concat_axis=0, tiled=True)
     (input_gradient,) = run(
         join_kernel,
-        [index, corners, ratios, start],
-        [gradient, back],
-        [((images_here, TILE, TILE, width), F32)],
-        [((images_here + 1, PAD, width), F32)],
+        [place, index, corners, ratios],
+        [*gradient, back],
+        [((TILE, TILE, images_here, width), F32)],
+        [((width // 128, (images_here + 1) * PAD, 128), F32)],
         name="join",
     )
-    vectors = jnp.sum(jnp.concatenate([vec1, vec2, conv2, vec3, conv3]), axis=1)
-    count = vectors.shape[0]
-    filled = jnp.pad(vectors.astype(BF), ((0, 64 - count), (0, 0)))
-    sum3 = sum_doubling(jnp.concatenate([bundle3, filled]), groups)
-
-    def flat(values):
-        return values.reshape(-1, width, width).transpose(1, 0, 2).reshape(width, -1)
-
-    sum1, sum2, sum3 = sum1.astype(F32), sum2.astype(F32), sum3.astype(F32)
-    v = sum3[3 * width : 3 * width + count]
-    v1, v2, c2, v3, c3 = v[0:7], v[7:22], v[22:31], v[31:35], v[35:44]
+    full1 = lax.all_to_all(spread1, RANKS, split_axis=0, concat_axis=0, tiled=True)
+    mine2 = scatter_sum(moved2)
+    moved3 = scatter_move(
+        scatter_send(added(keep3, swap(away3, "col")), ranks, steps[0]), ranks, steps[0]
+    )
+    mine3 = scatter_sum(moved3)
+    cut = mine2.shape[0] * 4 // ranks
+    lot = mine3.shape[0] * 4 // ranks
+    joint = jnp.concatenate(
+        [
+            mine2.reshape(ranks // 4, cut, width),
+            mine3.reshape(ranks // 4, lot, width),
+        ],
+        axis=1,
+    ).reshape(-1, width)
+    for step in steps[1:]:
+        joint = scatter_sum(scatter_move(scatter_send(joint, ranks, step), ranks, step))
+    for step in reversed(steps):
+        joint = gather(joint, ranks, step).reshape(-1, width)
+    joint = shards(joint, ranks)
+    full = [full1, swap(full1, "col"), joint, swap(joint, "col")]
+    (activations,) = run(
+        lay_kernel, [place], act, [((TILE, TILE, images_here, width), BF)], [flat], name="lay"
+    )
+    gains, shifts, entry, entry_b, conv, conv_b, exit_, exit_b, expand, expand_b, shrink, shrink_b = run(
+        unpack_kernel,
+        [place],
+        full,
+        [
+            ((2, 2, width), F32),
+            ((2, 2, width), F32),
+            ((2, width, 3 * width), F32),
+            ((2, 2 * width), F32),
+            ((3, 3, 2, width), F32),
+            ((2, width), F32),
+            ((2, width, width), F32),
+            ((2, width), F32),
+            ((2, width, units), F32),
+            ((2, units), F32),
+            ((2, units, width), F32),
+            ((2, width), F32),
+        ],
+        [((width // 2, width), F32)],
+        name="unpack",
+    )
     return (
-        act.reshape(images_here, TILE, 8, width)[:, :, :TILE, :],
-        input_gradient,
-        jnp.stack([jnp.stack([v3[2], v2[11]]), jnp.stack([v2[4], v1[5]])]),
-        jnp.stack([jnp.stack([v3[3], v2[12]]), jnp.stack([v2[5], v1[6]])]),
-        jnp.stack([flat(sum3[: 3 * width]), flat(sum2[: 3 * width])]),
-        jnp.stack([v3[0:2].reshape(-1), v2[2:4].reshape(-1)]),
-        jnp.stack([c3, c2]).reshape(2, 3, 3, width),
-        jnp.stack([v2[14], v2[1]]),
-        jnp.stack([sum2[12 * width :], sum2[3 * width : 4 * width]]),
-        jnp.stack([v2[13], v2[0]]),
-        jnp.stack([flat(sum2[4 * width : 8 * width]), flat(sum1[:units])]),
-        jnp.stack([v2[7:11].reshape(-1), v1[0:4].reshape(-1)]),
-        jnp.stack([sum2[8 * width : 12 * width], sum1[units:]]),
-        jnp.stack([v2[6], v1[4]]),
+        activations.transpose(2, 0, 1, 3),
+        input_gradient.transpose(2, 0, 1, 3),
+        gains,
+        shifts,
+        entry,
+        entry_b,
+        conv.transpose(2, 0, 1, 3),
+        conv_b,
+        exit_,
+        exit_b,
+        expand,
+        expand_b,
+        shrink,
+        shrink_b,
     )
 
 

time: 290 us -> 229 us (0.79)
  waiting for transfers between devices: 91 us -> 56.7 us
  local copies, waits for them, and re-layouts: 31.3 us -> 8.27 us
  other arithmetic: 24.7 us -> 3.88 us
  Pallas kernels: 88.6 us -> 108 us
    all_to_all x8 -> x2, waiting for transfers between devices: 47.5 us -> 0.01 us  [the longest x1 0.01 us: local(): lax.all_to_all(sent1, RANKS, split_axis=0, concat_axis=0, tiled=True)]
    ppermute x3 -> x27, waiting for transfers between devices: 0.01 us -> 41.8 us  [across(): return lax.ppermute(values, axes, [(i, i ^ mask) for i in range(size)])]
    ppermute x3 -> x27, starting transfers between devices: 4.39 us -> 26.9 us  [across(): return lax.ppermute(values, axes, [(i, i ^ mask) for i in range(size)])]
    ppermute x12 -> x5, waiting for transfers between devices: 22.2 us -> 2.35 us  [swap(): return lax.ppermute(values, axis, [(0, 1), (1, 0)])]
    pallas_call x7 -> x12, Pallas kernels: 88.6 us -> 108 us  [the longest x10 108 us: run(): pl.pallas_call(body, out_shape=out_shape, in_specs=[SMEM] * len(scalars)...]
    all_to_all x8 -> x2, starting transfers between devices: 28.2 us -> 11.4 us  [the longest x1 6.9 us: local(): lax.all_to_all(spread1, RANKS, split_axis=0, concat_axis=0, tiled=True)]
    another operation x16 -> x2, other arithmetic: 12.4 us -> 0.18 us  [gather(): jnp.stack([values] + [across(values, RANKS, ranks, d << stage[0]) for d i...]
    all_to_all x1, waiting for transfers between devices: 21.4 us -> 12.5 us  [local(): lax.all_to_all(outgoing, 'dp', split_axis=0, concat_axis=0, tiled=True)]
  transfers between devices with their start and end apart: 25 -> 36, of which waited for: 14 -> 13; matrix products, arithmetic and copies ran while one was open for 9% -> 1% of each run, Pallas kernels for 3% -> 23%
where the time goes in v2:
time: 229 us
  Pallas kernels  108 us (47%)
  waiting for transfers between devices  56.7 us (25%)
  starting transfers between devices  50.4 us (22%)
  local copies, waits for them, and re-layouts  8.27 us (4%)
  other arithmetic  3.88 us (2%)
    pallas_call x10, Pallas kernels, run(): pl.pallas_call(body, out_shape=out_shape, in_specs=[SMEM] * len(scalars)...  108 us
    ppermute x27, waiting for transfers between devices, across(): return lax.ppermute(values, axes, [(i, i ^ mask) for i in range(size)])  41.8 us
    ppermute x27, starting transfers between devices, across(): return lax.ppermute(values, axes, [(i, i ^ mask) for i in range(size)])  26.9 us
    all_to_all x1, waiting for transfers between devices, local(): lax.all_to_all(outgoing, 'dp', split_axis=0, concat_axis=0, tiled=True)  12.5 us
    all_to_all x1, starting transfers between devices, local(): lax.all_to_all(outgoing, 'dp', split_axis=0, concat_axis=0, tiled=True)  7.29 us
    all_to_all x1, starting transfers between devices, local(): lax.all_to_all(spread1, RANKS, split_axis=0, concat_axis=0, tiled=True)  6.9 us
    unnamed x66, local copies, waits for them, and re-layouts  6.02 us
  transfers between devices with their start and end apart: 36, of which 13 were waited for; matrix products, arithmetic and copies ran while one was open for 1% of the time, Pallas kernels for 23%

profile of v2, /device:TPU:0, one launch (start us, length us, event | category | flops | bytes accessed | tf_op | source)
XLA Modules:
  0.0 228.6 jit_solution(9027375520362323406)
XLA Ops:
  1.3 3.9 %pick.1 = (s32[40]{0:T(128)}, s32[32]{0:T(128)}, bf16[32,7,8,256]{3,2,1,0:T(8,128)(2,1)}, bf16[16,7,8,256]{3,2,1,0:T(8,128)(2,1)}) custom-call(s32[5]{0:T(128)} %stack.50.refs_0_, s32[128]{0:T(128)} %refs_1_.1, s32[128]{0:T(128)} %refs_2_.1, bf16[7,7,16,256]{3,2,1,0:T(8,128)(2,1)} %bitcast.70), custom_call_target="tpu_custom_call" | custom-call | bytes 401408 | tf_op jit(solution)/shard_map/pick/pallas_call | solution.py:951
  5.2 7.3 %all-to-all-start = ((bf16[32,7,8,256]{3,2,1,0:T(8,128)(2,1)}), bf16[32,7,8,256]{3,2,1,0:T(8,128)(2,1)S(1)}, u32[]{:S(2)}, u32[]{:S(2)}) async-start(bf16[32,7,8,256]{3,2,1,0:T(8,128)(2,1)} %get-tuple-element.79), calls=%async_computation | async-start | bytes 1835008 | tf_op jit(solution)/shard_map/all_to_all | solution.py:1092
  12.5 2.7 %deal.1 = (bf16[4,7,8,256]{3,2,1,0:T(8,128)(2,1)}, bf16[4,7,8,256]{3,2,1,0:T(8,128)(2,1)}, bf16[4,7,8,256]{3,2,1,0:T(8,128)(2,1)}, bf16[4,7,8,256]{3,2,1,0:T(8,128)(2,1)}) custom-call(s32[5]{0:T(128)} %stack.50.refs_0_, bf16[7,7,16,256]{3,2,1,0:T(8,128)(2,1)} %bitcast.71), custom_call_target="tpu_custom_call" | custom-call | bytes 401408 | tf_op jit(solution)/shard_map/deal/pallas_call | solution.py:951
  17.0 4.3 %collective-permute-done.1.refs_8_ = bf16[4,7,8,256]{3,2,1,0:T(8,128)(2,1)S(1)} collective-permute-done((bf16[4,7,8,256]{3,2,1,0:T(8,128)(2,1)}, bf16[4,7,8,256]{3,2,1,0:T(8,128)(2,1)S(1)}, u32[]{:S(2)}, u32[]{:S(2)}) %collective-permute-start.1) | collective-permute-done | bytes 114720 | tf_op jit(solution)/shard_map/ppermute | solution.py:999
  23.0 12.5 %all-to-all-done.refs_4_ = bf16[32,7,8,256]{3,2,1,0:T(8,128)(2,1)S(1)} async-done(((bf16[32,7,8,256]{3,2,1,0:T(8,128)(2,1)}), bf16[32,7,8,256]{3,2,1,0:T(8,128)(2,1)S(1)}, u32[]{:S(2)}, u32[]{:S(2)}) %all-to-all-start) | async-done | bytes 917536 | tf_op jit(solution)/shard_map/all_to_all | solution.py:1092
  36.4 2.7 %mix.1 = (bf16[4,7,8,256]{3,2,1,0:T(8,128)(2,1)}, bf16[4,7,8,256]{3,2,1,0:T(8,128)(2,1)}, bf16[4,7,8,256]{3,2,1,0:T(8,128)(2,1)}, bf16[4,7,8,256]{3,2,1,0:T(8,128)(2,1)}) custom-call(s32[5]{0:T(128)} %stack.50.refs_0_, s32[32]{0:T(128)} %get-tuple-element.78.refs_1_, s32[4,16]{1,0:T(4,128)} %bitcast.80, f32[16]{0:T(128)} %refs_3_.5, ...), custom_call_target="tpu_custom_call" | custom-call | bytes 1376256 | tf_op jit(solution)/shard_map/mix/pallas_call | solution.py:951
  40.9 4.3 %collective-permute-done.4.refs_4_.refs_5_ = bf16[4,7,8,256]{3,2,1,0:T(8,128)(2,1)S(1)} collective-permute-done((bf16[4,7,8,256]{3,2,1,0:T(8,128)(2,1)}, bf16[4,7,8,256]{3,2,1,0:T(8,128)(2,1)S(1)}, u32[]{:S(2)}, u32[]{:S(2)}) %collective-permute-start.4) | collective-permute-done | bytes 114720 | tf_op jit(solution)/shard_map/ppermute | solution.py:999
  47.5 44.8 %first.1 = (bf16[4,7,8,256]{3,2,1,0:T(8,128)(2,1)}, bf16[4,7,8,256]{3,2,1,0:T(8,128)(2,1)}, bf16[4,7,8,256]{3,2,1,0:T(8,128)(2,1)}, bf16[4,7,8,256]{3,2,1,0:T(8,...) custom-call(s32[5]{0:T(128)} %stack.50.refs_0_, ...), custom_call_target="tpu_custom_call" | custom-call | flops 70464307200 | bytes 4108288 | tf_op jit(solution)/shard_map/first/pallas_call | solution.py:951
  96.5 4.5 %all-to-all-start.1 = ((bf16[16,64,256]{2,1,0:T(8,128)(2,1)}), bf16[16,64,256]{2,1,0:T(8,128)(2,1)S(1)}, u32[]{:S(2)}, u32[]{:S(2)}) async-start(bf16[16,64,256]{2,1,0:T(8,128)(2,1)} %bitcast.11.refs_18_), calls=%async_computation.1 | async-start | bytes 1048576 | tf_op jit(solution)/shard_map/all_to_all | solution.py:1176
  101.0 26.4 %second.1 = (bf16[1664,256]{1,0:T(8,128)(2,1)}, bf16[1664,256]{1,0:T(8,128)(2,1)}, f32[15,8,256]{2,1,0:T(8,128)}, f32[9,8,256]{2,1,0:T(8,128)}, f32[896,256]{1,0:T(8,128)}, /*index=5*/f32[896,256]{1,0:T(8,128)}) custom-call(s32[5]{0:T(128)} %stack.50.refs_0_, s32[4,16]{1,0:T(4,128)} %bitcast.88, f32[896,256]{1,0:T(8,128)} %get-tuple-element.94.refs_2_, ...), custom_call_target="tpu_custom_call" | custom-call | flops 42278584320 | bytes 13723648 | tf_op jit(solution)/shard_map/second/pallas_call | solution.py:951
  128.6 2.3 %collective-permute-done.10 = bf16[1664,256]{1,0:T(8,128)(2,1)S(1)} collective-permute-done((bf16[1664,256]{1,0:T(8,128)(2,1)}, bf16[1664,256]{1,0:T(8,128)(2,1)S(1)}, u32[]{:S(2)}, u32[]{:S(2)}) %collective-permute-start.10) | collective-permute-done | bytes 852000 | tf_op jit(solution)/shard_map/ppermute | solution.py:982
  136.5 14.8 %third.1 = (bf16[4,7,8,256]{3,2,1,0:T(8,128)(2,1)}, bf16[4,7,8,256]{3,2,1,0:T(8,128)(2,1)}, bf16[4,7,8,256]{3,2,1,0:T(8,128)(2,1)}, bf16[4,7,8,256]{3,2,1,0:T(8,...) custom-call(s32[5]{0:T(128)} %stack.50.refs_0_, f32[896,256]{1,0:T(8,128)} %get-tuple-element.109.refs_1_, ...), custom_call_target="tpu_custom_call" | custom-call | flops 21139292160 | bytes 6572032 | tf_op jit(solution)/shard_map/third/pallas_call | solution.py:951
  153.6 6.9 %all-to-all-start.3 = ((bf16[16,64,256]{2,1,0:T(8,128)(2,1)}), bf16[16,64,256]{2,1,0:T(8,128)(2,1)S(1)}, u32[]{:S(2)}, u32[]{:S(2)}) async-start(bf16[16,64,256]{2,1,0:T(8,128)(2,1)} %broadcast_in_dim.2), calls=%async_computation.3 | async-start | bytes 1048576 | tf_op jit(solution)/shard_map/all_to_all | solution.py:1276
  164.3 2.4 %collective-permute-done.19 = bf16[128,256]{1,0:T(8,128)(2,1)S(1)} collective-permute-done((bf16[128,256]{1,0:T(8,128)(2,1)S(1)}, bf16[128,256]{1,0:T(8,128)(2,1)S(1)}, u32[]{:S(2)}, u32[]{:S(2)}) %collective-permute-start.19) | collective-permute-done | bytes 65568 | tf_op jit(solution)/shard_map/ppermute | solution.py:999
  166.7 2.8 %collective-permute-done.20 = bf16[128,256]{1,0:T(8,128)(2,1)S(1)} collective-permute-done((bf16[128,256]{1,0:T(8,128)(2,1)S(1)}, bf16[128,256]{1,0:T(8,128)(2,1)S(1)}, u32[]{:S(2)}, u32[]{:S(2)}) %collective-permute-start.20) | collective-permute-done | bytes 65568 | tf_op jit(solution)/shard_map/ppermute | solution.py:999
  172.1 2.7 %collective-permute-start.23 = (bf16[136,256]{1,0:T(8,128)(2,1)S(1)}, bf16[136,256]{1,0:T(8,128)(2,1)S(1)}, u32[]{:S(2)}, u32[]{:S(2)}) collective-permute-start(bf16[136,256]{1,0:T(8,128)(2,1)S(1)} %get-tuple-element.147), channel_id=1, source_target_pairs={{0,16},{2,18},{4,20},{6,22},{8,24},{10,26},{12,28},{14,30},{16,0},... | collective-permute-start | bytes 208904 | tf_op jit(solution)/shard_map/ppermute | solution.py:999
  177.2 2.5 %collective-permute-done.23 = bf16[136,256]{1,0:T(8,128)(2,1)S(1)} collective-permute-done((bf16[136,256]{1,0:T(8,128)(2,1)S(1)}, bf16[136,256]{1,0:T(8,128)(2,1)S(1)}, u32[]{:S(2)}, u32[]{:S(2)}) %collective-permute-start.23) | collective-permute-done | bytes 69664 | tf_op jit(solution)/shard_map/ppermute | solution.py:999
  186.2 2.5 %split.1 = bf16[32,7,8,256]{3,2,1,0:T(8,128)(2,1)} custom-call(s32[5]{0:T(128)} %stack.50.refs_0_, s32[32]{0:T(128)} %get-tuple-element.78.refs_1_, s32[4,16]{1,0:T(4,128)} %bitcast.81, f32[16]{0:T(128)} %refs_3_.5, bf16[4,7,8,256]{3,2,1,0:T(8,128)(2,1)} %get-tuple-element.118.refs_4_, bf16[4,7,8,256]{3,2,1,0:T(8,128)(2,1)} %copy-done.18, ...), custom_call_target="tpu_custom_call" | custom-call | bytes 458752 | tf_op jit(solution)/shard_map/split/pallas_call | solution.py:951
  188.7 3.6 %all-to-all-start.2 = ((bf16[32,7,8,256]{3,2,1,0:T(8,128)(2,1)}), bf16[32,7,8,256]{3,2,1,0:T(8,128)(2,1)S(1)}, u32[]{:S(2)}, u32[]{:S(2)}) async-start(bf16[32,7,8,256]{3,2,1,0:T(8,128)(2,1)} %split.1), calls=%async_computation.2 | async-start | bytes 1835008 | tf_op jit(solution)/shard_map/all_to_all | solution.py:1267
  195.9 6.1 %collective-permute-done.28 = bf16[544,256]{1,0:T(8,128)(2,1)S(1)} collective-permute-done((bf16[544,256]{1,0:T(8,128)(2,1)S(1)}, bf16[544,256]{1,0:T(8,128)(2,1)S(1)}, u32[]{:S(2)}, u32[]{:S(2)}) %collective-permute-start.28) | collective-permute-done | bytes 278560 | tf_op jit(solution)/shard_map/ppermute | solution.py:999
  202.0 13.5 %collective-permute-done.29 = bf16[544,256]{1,0:T(8,128)(2,1)S(1)} collective-permute-done((bf16[544,256]{1,0:T(8,128)(2,1)S(1)}, bf16[544,256]{1,0:T(8,128)(2,1)S(1)}, u32[]{:S(2)}, u32[]{:S(2)}) %collective-permute-start.29) | collective-permute-done | bytes 278560 | tf_op jit(solution)/shard_map/ppermute | solution.py:999
  216.2 2.1 lay.1
  219.2 3.2 %join.1 = f32[7,7,16,256]{3,2,1,0:T(8,128)} custom-call(s32[5]{0:T(128)} %stack.50.refs_0_, s32[40]{0:T(128)} %get-tuple-element.93.refs_1_, s32[4,16]{1,0:T(4,128)} %bitcast.82, f32[16]{0:T(128)} %refs_3_.5, bf16[4,7,8,256]{3,2,1,0:T(8,128)(2,1)} %get-tuple-element.118.refs_4_, bf16[4,7,8,256]{3,2,1,0:T(8,128)(2,1)} %copy-done.18, ...), custom_call_target="tpu_custom_call" | custom-call | bytes 1376256 | tf_op jit(solution)/shard_map/join/pallas_call | solution.py:951
  223.2 5.2 %unpack.1 = (f32[2,2,256]{2,1,0:T(2,128)}, f32[2,2,256]{2,1,0:T(2,128)}, f32[2,256,768]{2,1,0:T(8,128)}, f32[2,512]{1,0:T(2,128)}, f32[3,3,2,256]{3,2,1,0:T(2,12...) custom-call(s32[5]{0:T(128)} %stack.50.refs_0_, ...), custom_call_target="tpu_custom_call" | custom-call | bytes 3276800 | tf_op jit(solution)/shard_map/unpack/pallas_call | solution.py:951
  (140 shorter events, 43.4 us)
Async XLA Ops:
  5.2 30.3 %all-to-all-start = ((bf16[32,7,8,256]{3,2,1,0:T(8,128)(2,1)}), bf16[32,7,8,256]{3,2,1,0:T(8,128)(2,1)S(1)}, u32[]{:S(2)}, u32[]{:S(2)}) async-start(bf16[32,7,8,256]{3,2,1,0:T(8,128)(2,1)} %get-tuple-element.79), calls=%async_computation | async-start | bytes 1835008 | tf_op jit(solution)/shard_map/all_to_all | solution.py:1092
  92.7 34.8 %collective-permute-start.6 = (bf16[4,7,8,256]{3,2,1,0:T(8,128)(2,1)}, bf16[4,7,8,256]{3,2,1,0:T(8,128)(2,1)S(1)}, u32[]{:S(2)}, u32[]{:S(2)}) collective-permute-start(bf16[4,7,8,256]{3,2,1,0:T(8,128)(2,1)} %get-tuple-element.90), channel_id=1, source_target_pairs={{0,1},{1,0},{2,3},{3,2},{4,5},{5,4},{6,7},{7,6},{8,9},{9,8},{10,11... | collective-permute-start | bytes 344072 | tf_op jit(solution)/shard_map/ppermute | solution.py:999
  92.9 34.5 %collective-permute-start.7 = (bf16[4,7,8,256]{3,2,1,0:T(8,128)(2,1)}, bf16[4,7,8,256]{3,2,1,0:T(8,128)(2,1)S(1)}, u32[]{:S(2)}, u32[]{:S(2)}) collective-permute-start(bf16[4,7,8,256]{3,2,1,0:T(8,128)(2,1)} %get-tuple-element.91), channel_id=1, source_target_pairs={{0,2},{1,3},{2,0},{3,1},{4,6},{5,7},{6,4},{7,5},{8,10},{9,11},{10,... | collective-permute-start | bytes 344072 | tf_op jit(solution)/shard_map/ppermute | solution.py:999
  94.4 33.0 %collective-permute-start.8 = (bf16[4,7,8,256]{3,2,1,0:T(8,128)(2,1)}, bf16[4,7,8,256]{3,2,1,0:T(8,128)(2,1)S(1)}, u32[]{:S(2)}, u32[]{:S(2)}) collective-permute-start(bf16[4,7,8,256]{3,2,1,0:T(8,128)(2,1)} %get-tuple-element.92), channel_id=1, source_target_pairs={{0,3},{1,2},{2,1},{3,0},{4,7},{5,6},{6,5},{7,4},{8,11},{9,10},{10,... | collective-permute-start | bytes 344072 | tf_op jit(solution)/shard_map/ppermute | solution.py:999
  96.5 31.0 %all-to-all-start.1 = ((bf16[16,64,256]{2,1,0:T(8,128)(2,1)}), bf16[16,64,256]{2,1,0:T(8,128)(2,1)S(1)}, u32[]{:S(2)}, u32[]{:S(2)}) async-start(bf16[16,64,256]{2,1,0:T(8,128)(2,1)} %bitcast.11.refs_18_), calls=%async_computation.1 | async-start | bytes 1048576 | tf_op jit(solution)/shard_map/all_to_all | solution.py:1176
  133.0 18.3 %collective-permute-start.15 = (bf16[416,256]{1,0:T(8,128)(2,1)S(1)}, bf16[416,256]{1,0:T(8,128)(2,1)S(1)}, u32[]{:S(2)}, u32[]{:S(2)}) collective-permute-start(bf16[416,256]{1,0:T(8,128)(2,1)S(1)} %get-tuple-element.144.refs_17_), channel_id=1, source_target_pairs={{0,2},{2,0},{4,6},{6,4},{8,10},{10,8},{12,14},{14,12},{16,18},{18,... | collective-permute-start | bytes 638984 | tf_op jit(solution)/shard_map/ppermute | solution.py:999
  134.9 16.4 %collective-permute-start.16 = (bf16[416,256]{1,0:T(8,128)(2,1)S(1)}, bf16[416,256]{1,0:T(8,128)(2,1)S(1)}, u32[]{:S(2)}, u32[]{:S(2)}) collective-permute-start(bf16[416,256]{1,0:T(8,128)(2,1)S(1)} %get-tuple-element.143.refs_18_), channel_id=1, source_target_pairs={{0,4},{2,6},{4,0},{6,2},{8,12},{10,14},{12,8},{14,10},{16,20},{18,... | collective-permute-start | bytes 638984 | tf_op jit(solution)/shard_map/ppermute | solution.py:999
  136.4 15.0 %collective-permute-start.17 = (bf16[416,256]{1,0:T(8,128)(2,1)S(1)}, bf16[416,256]{1,0:T(8,128)(2,1)S(1)}, u32[]{:S(2)}, u32[]{:S(2)}) collective-permute-start(bf16[416,256]{1,0:T(8,128)(2,1)S(1)} %get-tuple-element.142.refs_19_), channel_id=1, source_target_pairs={{0,6},{2,4},{4,2},{6,0},{8,14},{10,12},{12,10},{14,8},{16,22},{18,... | collective-permute-start | bytes 638984 | tf_op jit(solution)/shard_map/ppermute | solution.py:999
  152.2 8.3 %collective-permute-start.18 = (bf16[512,256]{1,0:T(8,128)(2,1)}, bf16[512,256]{1,0:T(8,128)(2,1)S(1)}, u32[]{:S(2)}, u32[]{:S(2)}) collective-permute-start(bf16[512,256]{1,0:T(8,128)(2,1)} %get-tuple-element.129), channel_id=1, source_target_pairs={{0,1},{1,0},{2,3},{3,2},{4,5},{5,4},{6,7},{7,6},{8,9},{9,8},{10,11... | collective-permute-start | bytes 786440 | tf_op jit(solution)/shard_map/ppermute | solution.py:982
  153.6 35.1 %all-to-all-start.3 = ((bf16[16,64,256]{2,1,0:T(8,128)(2,1)}), bf16[16,64,256]{2,1,0:T(8,128)(2,1)S(1)}, u32[]{:S(2)}, u32[]{:S(2)}) async-start(bf16[16,64,256]{2,1,0:T(8,128)(2,1)} %broadcast_in_dim.2), calls=%async_computation.3 | async-start | bytes 1048576 | tf_op jit(solution)/shard_map/all_to_all | solution.py:1276
  162.6 6.9 %collective-permute-start.20 = (bf16[128,256]{1,0:T(8,128)(2,1)S(1)}, bf16[128,256]{1,0:T(8,128)(2,1)S(1)}, u32[]{:S(2)}, u32[]{:S(2)}) collective-permute-start(bf16[128,256]{1,0:T(8,128)(2,1)S(1)} %get-tuple-element.151), channel_id=1, source_target_pairs={{0,4},{2,6},{4,0},{6,2},{8,12},{10,14},{12,8},{14,10},{16,20},{18,... | collective-permute-start | bytes 196616 | tf_op jit(solution)/shard_map/ppermute | solution.py:999
  172.1 7.6 %collective-permute-start.23 = (bf16[136,256]{1,0:T(8,128)(2,1)S(1)}, bf16[136,256]{1,0:T(8,128)(2,1)S(1)}, u32[]{:S(2)}, u32[]{:S(2)}) collective-permute-start(bf16[136,256]{1,0:T(8,128)(2,1)S(1)} %get-tuple-element.147), channel_id=1, source_target_pairs={{0,16},{2,18},{4,20},{6,22},{8,24},{10,26},{12,28},{14,30},{16,0},... | collective-permute-start | bytes 208904 | tf_op jit(solution)/shard_map/ppermute | solution.py:999
  175.3 8.2 %collective-permute-start.11 = (bf16[4,7,8,256]{3,2,1,0:T(8,128)(2,1)S(1)}, bf16[4,7,8,256]{3,2,1,0:T(8,128)(2,1)S(1)}, u32[]{:S(2)}, u32[]{:S(2)}) collective-permute-start(bf16[4,7,8,256]{3,2,1,0:T(8,128)(2,1)S(1)} %copy-done.29), channel_id=1, source_target_pairs={{0,1},{1,0},{2,3},{3,2},{4,5},{5,4},{6,7},{7,6},{8,9},{9,8},{10,11... | collective-permute-start | bytes 344072 | tf_op jit(solution)/shard_map/ppermute | solution.py:999
  175.3 10.2 %collective-permute-start.12 = (bf16[4,7,8,256]{3,2,1,0:T(8,128)(2,1)S(1)}, bf16[4,7,8,256]{3,2,1,0:T(8,128)(2,1)S(1)}, u32[]{:S(2)}, u32[]{:S(2)}) collective-permute-start(bf16[4,7,8,256]{3,2,1,0:T(8,128)(2,1)S(1)} %copy-done.28), channel_id=1, source_target_pairs={{0,2},{1,3},{2,0},{3,1},{4,6},{5,7},{6,4},{7,5},{8,10},{9,11},{10,... | collective-permute-start | bytes 344072 | tf_op jit(solution)/shard_map/ppermute | solution.py:999
  176.0 9.5 %collective-permute-start.13 = (bf16[4,7,8,256]{3,2,1,0:T(8,128)(2,1)S(1)}, bf16[4,7,8,256]{3,2,1,0:T(8,128)(2,1)S(1)}, u32[]{:S(2)}, u32[]{:S(2)}) collective-permute-start(bf16[4,7,8,256]{3,2,1,0:T(8,128)(2,1)S(1)} %copy-done.27), channel_id=1, source_target_pairs={{0,3},{1,2},{2,1},{3,0},{4,7},{5,6},{6,5},{7,4},{8,11},{9,10},{10,... | collective-permute-start | bytes 344072 | tf_op jit(solution)/shard_map/ppermute | solution.py:999
  181.1 11.2 %collective-permute-start.25 = (bf16[136,256]{1,0:T(8,128)(2,1)S(1)}, bf16[136,256]{1,0:T(8,128)(2,1)S(1)}, u32[]{:S(2)}, u32[]{:S(2)}) collective-permute-start(bf16[136,256]{1,0:T(8,128)(2,1)S(1)} %fusion.2), channel_id=1, source_target_pairs={{0,8},{2,10},{4,12},{6,14},{8,0},{10,2},{12,4},{14,6},{16,24},{18,... | collective-permute-start | bytes 208904 | tf_op jit(solution)/shard_map/ppermute | solution.py:999
  181.9 10.4 %collective-permute-start.26 = (bf16[136,256]{1,0:T(8,128)(2,1)S(1)}, bf16[136,256]{1,0:T(8,128)(2,1)S(1)}, u32[]{:S(2)}, u32[]{:S(2)}) collective-permute-start(bf16[136,256]{1,0:T(8,128)(2,1)S(1)} %fusion.2), channel_id=1, source_target_pairs={{0,16},{2,18},{4,20},{6,22},{8,24},{10,26},{12,28},{14,30},{16,0},... | collective-permute-start | bytes 208904 | tf_op jit(solution)/shard_map/ppermute | solution.py:999
  183.5 8.8 %collective-permute-start.27 = (bf16[136,256]{1,0:T(8,128)(2,1)S(1)}, bf16[136,256]{1,0:T(8,128)(2,1)S(1)}, u32[]{:S(2)}, u32[]{:S(2)}) collective-permute-start(bf16[136,256]{1,0:T(8,128)(2,1)S(1)} %fusion.2), channel_id=1, source_target_pairs={{0,24},{2,26},{4,28},{6,30},{8,16},{10,18},{12,20},{14,22},{16,8},... | collective-permute-start | bytes 208904 | tf_op jit(solution)/shard_map/ppermute | solution.py:999
  188.7 29.6 %all-to-all-start.2 = ((bf16[32,7,8,256]{3,2,1,0:T(8,128)(2,1)}), bf16[32,7,8,256]{3,2,1,0:T(8,128)(2,1)S(1)}, u32[]{:S(2)}, u32[]{:S(2)}) async-start(bf16[32,7,8,256]{3,2,1,0:T(8,128)(2,1)} %split.1), calls=%async_computation.2 | async-start | bytes 1835008 | tf_op jit(solution)/shard_map/all_to_all | solution.py:1267
  192.3 9.7 %collective-permute-start.28 = (bf16[544,256]{1,0:T(8,128)(2,1)S(1)}, bf16[544,256]{1,0:T(8,128)(2,1)S(1)}, u32[]{:S(2)}, u32[]{:S(2)}) collective-permute-start(bf16[544,256]{1,0:T(8,128)(2,1)S(1)} %bitcast.61), channel_id=1, source_target_pairs={{0,2},{2,0},{4,6},{6,4},{8,10},{10,8},{12,14},{14,12},{16,18},{18,... | collective-permute-start | bytes 835592 | tf_op jit(solution)/shard_map/ppermute | solution.py:999
  193.4 22.0 %collective-permute-start.29 = (bf16[544,256]{1,0:T(8,128)(2,1)S(1)}, bf16[544,256]{1,0:T(8,128)(2,1)S(1)}, u32[]{:S(2)}, u32[]{:S(2)}) collective-permute-start(bf16[544,256]{1,0:T(8,128)(2,1)S(1)} %bitcast.62), channel_id=1, source_target_pairs={{0,4},{2,6},{4,0},{6,2},{8,12},{10,14},{12,8},{14,10},{16,20},{18,... | collective-permute-start | bytes 835592 | tf_op jit(solution)/shard_map/ppermute | solution.py:999
  195.3 20.1 %collective-permute-start.30 = (bf16[544,256]{1,0:T(8,128)(2,1)S(1)}, bf16[544,256]{1,0:T(8,128)(2,1)S(1)}, u32[]{:S(2)}, u32[]{:S(2)}) collective-permute-start(bf16[544,256]{1,0:T(8,128)(2,1)S(1)} %bitcast.63), channel_id=1, source_target_pairs={{0,6},{2,4},{4,2},{6,0},{8,14},{10,12},{12,10},{14,8},{16,22},{18,... | collective-permute-start | bytes 835592 | tf_op jit(solution)/shard_map/ppermute | solution.py:999
  215.6 6.9 %collective-permute-start.31 = (bf16[16,136,256]{2,1,0:T(8,128)(2,1)S(1)}, bf16[16,136,256]{2,1,0:T(8,128)(2,1)}, u32[]{:S(2)}, u32[]{:S(2)}) collective-permute-start(bf16[16,136,256]{2,1,0:T(8,128)(2,1)S(1)} %bitcast.56), channel_id=1, source_target_pairs={{0,1},{1,0},{2,3},{3,2},{4,5},{5,4},{6,7},{7,6},{8,9},{9,8},{10,11... | collective-permute-start | bytes 3342344 | tf_op jit(solution)/shard_map/ppermute | solution.py:982
  215.7 6.8 %collective-permute-start.14 = (bf16[16,64,256]{2,1,0:T(8,128)(2,1)S(1)}, bf16[16,64,256]{2,1,0:T(8,128)(2,1)S(1)}, u32[]{:S(2)}, u32[]{:S(2)}) collective-permute-start(bf16[16,64,256]{2,1,0:T(8,128)(2,1)S(1)} %all-to-all-done.3.refs_1_), channel_id=1, source_target_pairs={{0,1},{1,0},{2,3},{3,2},{4,5},{5,4},{6,7},{7,6},{8,9},{9,8},{10,11... | collective-permute-start | bytes 1572872 | tf_op jit(solution)/shard_map/ppermute | solution.py:982
  (45 other events, 267.1 us)

commit v3 on v2

--- a/solution.py
+++ b/solution.py
@@ -13,8 +13,10 @@
 SIDE_HEADS = 4
 HALF = 128
 WIN = 2 * PAD
+CHUNK = 8 * PAD
 LANES = SIDE_HEADS * 128
 SCALE = HEAD_DIM ** (-0.5)
+LOG2E = 1.4426950408889634
 EPS = 1e-05
 BF = jnp.bfloat16
 F32 = jnp.float32
@@ -68,7 +70,8 @@
     scales = [
         mask_ref[column, 4 * place_ref[3] + i].astype(F32) * 1.25 for i in range(4)
     ]
-    return jnp.concatenate([jnp.full((PAD, 1), scale, F32) for scale in scales], axis=0)
+    columns = [jnp.full((PAD, 1), scale, F32) for scale in scales]
+    return jnp.concatenate(columns * (CHUNK // (4 * PAD)), axis=0)
 
 
 def add_row(acc_ref, row, values):
@@ -94,6 +97,19 @@
         axis=0,
     )
     return picked.T[:WIN]
+
+
+def turned(values):
+    return jnp.concatenate([values, jnp.zeros((128 - WIN, HALF), F32)], axis=0).T.astype(BF)
+
+
+def fill_rows(values):
+    empty = jnp.zeros((128 - WIN, values.shape[1]), values.dtype)
+    return jnp.concatenate([values, empty], axis=0)
+
+
+def valid_column(shape):
+    return lax.broadcasted_iota(jnp.int32, shape, 1) != 7
 
 
 def valid_rows(shape):
@@ -183,9 +199,9 @@
 ):
     width = hidden_ref.shape[1]
 
-    @pl.loop(0, 4)
+    @pl.loop(0, 2)
     def _(t):
-        rows = pl.ds(pl.multiple_of(t * 4 * PAD, 4 * PAD), 4 * PAD)
+        rows = chunk(t)
         hat, _ = norm_parts(hidden_ref[rows, :])
         normed = (hat * gains[block, 0:1, :] + shifts[block, 0:1, :]).astype(BF)
         for part in range(3):
@@ -199,7 +215,7 @@
         across = direction == 0
         lane = direction * HALF
 
-        @pl.loop(0, 8)
+        @pl.loop(0, 8, unroll=4)
         def _(window, across=across, lane=lane, direction=direction):
             at = window_rows(across, window)
             queries = take_window(wide, at, lane)
@@ -209,15 +225,14 @@
             win_out[direction * 8 + window, :, 0:HALF] = queries.astype(BF)
             win_out[direction * 8 + window, :, HALF : 2 * HALF] = keys_bf
             win_out[direction * 8 + window, :, 2 * HALF : 3 * HALF] = values.astype(BF)
-            scores = dot_nt(keys_bf, spread_heads(queries))
-            keep = valid_rows(scores.shape)
-            scores = jnp.where(keep, scores, -1e30)
-            top = jnp.max(scores, axis=0, keepdims=True)
-            lifted = jnp.exp((scores - top) * SCALE)
-            totals = jnp.sum(lifted, axis=0, keepdims=True)
-            chances = (lifted * (1.0 / totals)).astype(BF)
+            scores = dot_nt(keys_bf, spread_heads(queries)).reshape(2 * TILE, 8, LANES)
+            scores = jnp.where(valid_column((1, 8, LANES)), scores, -1e30)
+            top = jnp.max(jnp.max(scores, axis=0), axis=0, keepdims=True)
+            lifted = jnp.exp2((scores - top) * (SCALE * LOG2E))
+            totals = jnp.sum(jnp.sum(lifted, axis=0), axis=0, keepdims=True)
+            chances = (lifted * (1.0 / totals)).reshape(WIN, LANES).astype(BF)
             chance_out[direction * 8 + window] = chances
-            attended = gather_heads(dot_nn(values.T.astype(BF), chances))
+            attended = gather_heads(dot_nn(turned(values), fill_rows(chances)))
             clean = jnp.where(valid_rows(values.shape), values, 0.0)
             position = window_conv(
                 column_shifts(clean, across),
@@ -243,7 +258,7 @@
         across = direction == 0
         lane = direction * HALF
 
-        @pl.loop(0, 8)
+        @pl.loop(0, 8, unroll=4)
         def _(window, across=across, lane=lane, direction=direction):
             at = window_rows(across, window)
             out_delta = take_window(stripe_delta, at, lane)
@@ -254,14 +269,14 @@
             chances = chance_in[direction * 8 + window]
             delta_spread = spread_heads(out_delta)
             chance_delta = dot_nt(values_bf, delta_spread)
-            wide_chances = chances.astype(F32)
-            weighted = wide_chances * chance_delta
-            score_delta = (
-                weighted - wide_chances * jnp.sum(weighted, axis=0, keepdims=True)
-            ).astype(BF)
+            cubes = (2 * TILE, 8, LANES)
+            wide_chances = chances.astype(F32).reshape(cubes)
+            weighted = wide_chances * chance_delta.reshape(cubes)
+            common = jnp.sum(jnp.sum(weighted, axis=0), axis=0, keepdims=True)
+            score_delta = (weighted - wide_chances * common).reshape(WIN, LANES).astype(BF)
             values_delta = dot_nn(chances, delta_spread)
             keys_delta = dot_nn(score_delta, spread_heads(queries)) * SCALE
-            query_delta = gather_heads(dot_nn(keys.T.astype(BF), score_delta)) * SCALE
+            query_delta = gather_heads(dot_nn(turned(keys), fill_rows(score_delta))) * SCALE
             keep = valid_rows(values.shape)
             clean = jnp.where(keep, values, 0.0)
             shifts = column_shifts(clean, across)
@@ -282,79 +297,95 @@
 
 
 def chunk(t):
-    return pl.ds(pl.multiple_of(t * 4 * PAD, 4 * PAD), 4 * PAD)
-
-
-def put_rows(bundle, at, values):
-    place_ref, keep, away = bundle
-    values = values.astype(BF)
-    half = keep.shape[0]
-    count = values.shape[0]
-    cuts = [at, at + count] if at >= half or at + count <= half else [at, half, at + count]
-    for first, last in zip(cuts[:-1], cuts[1:]):
-        number = first // half
-        piece = values[first - at : last - at]
-        place = slice(first - number * half, last - number * half)
-
-        @pl.when(place_ref[2] == number)
-        def _(piece=piece, place=place):
-            keep[place, :] = piece
-
-        @pl.when(place_ref[2] != number)
-        def _(piece=piece, place=place):
-            away[place, :] = piece
+    return pl.ds(pl.multiple_of(t * CHUNK, CHUNK), CHUNK)
+
+
+class Bundle:
+    def __init__(self, place_ref, keep, away, chunks=1, spot=lambda chunk: chunk):
+        self.place_ref, self.keep, self.away = place_ref, keep, away
+        self.step, self.spot = keep.shape[0] // chunks, spot
+
+    def put(self, at, values):
+        values = values.astype(BF)
+        half, step = self.keep.shape[0], self.step
+        last = at + values.shape[0]
+        first = at
+        while first < last:
+            stop = min(last, (first // step + 1) * step)
+            number = first // half
+            start = self.spot(first % half // step) * step
+            inner, count = first % step, stop - first
+            if not isinstance(start, int):
+                start = pl.multiple_of(start, step)
+            rows = pl.ds(start + inner, count)
+            piece = values[first - at : stop - at]
+
+            @pl.when(self.place_ref[2] == number)
+            def _(piece=piece, rows=rows):
+                self.keep[rows, :] = piece
+
+            @pl.when(self.place_ref[2] != number)
+            def _(piece=piece, rows=rows):
+                self.away[rows, :] = piece
+
+            first = stop
 
 
 def put_squares(bundle, at, values, side):
     for part in range(values.shape[1] // side):
-        put_rows(bundle, at + part * side, values[:, part * side : (part + 1) * side])
+        bundle.put(at + part * side, values[:, part * side : (part + 1) * side])
 
 
 def load_tiles(place_ref, tiles, hidden):
     for d, tile in enumerate(tiles):
-        rows = chunk(jnp.bitwise_xor(place_ref[3], d))
+        at = jnp.bitwise_xor(place_ref[3], d) * (4 * PAD)
+        rows = pl.ds(pl.multiple_of(at, 4 * PAD), 4 * PAD)
         hidden[rows, :] = tile[...].astype(F32).reshape(4 * PAD, hidden.shape[1])
 
 
 def store_tile(place_ref, tiles, t, values):
-    values = values.reshape(tiles[0].shape).astype(BF)
-    for d, tile in enumerate(tiles):
-
-        @pl.when(jnp.bitwise_xor(place_ref[3], d) == t)
-        def _(tile=tile):
-            tile[...] = values
+    count = CHUNK // (4 * PAD)
+    values = values.reshape((count,) + tiles[0].shape).astype(BF)
+    for part in range(count):
+        for d, tile in enumerate(tiles):
+
+            @pl.when(jnp.bitwise_xor(place_ref[3], d) == count * t + part)
+            def _(tile=tile, part=part):
+                tile[...] = values[part]
 
 
 def first_kernel(
+    spots,
+    moves,
     place_ref,
     mask_ref,
     mixed_a,
     mixed_b,
     mixed_c,
     mixed_d,
+    gains,
+    shifts,
+    entry_b,
+    conv_k,
+    conv_b,
+    exit_b,
+    expand_b,
+    shrink_b,
+    entry_w,
+    exit_w,
+    expand_w,
+    shrink_w,
     cot_a,
     cot_b,
     cot_c,
     cot_d,
-    gains,
-    shifts,
-    entry_w,
-    entry_b,
-    conv_k,
-    conv_b,
-    exit_w,
-    exit_b,
-    expand_w,
-    expand_b,
-    shrink_w,
-    shrink_b,
+    vec_out,
     act_a,
     act_b,
     act_c,
     act_d,
     keep_out,
     away_out,
-    vec_out,
     active0_out,
     slope0_out,
     win0_out,
@@ -376,10 +407,10 @@
 ):
     width = hidden.shape[1]
     hidden_units = expand_w.shape[2]
-    bundle = (place_ref, keep_out, away_out)
+    bundle = Bundle(place_ref, keep_out, away_out, len(spots), lambda chunk: spots[chunk])
     vec_out[...] = jnp.zeros(vec_out.shape, F32)
     load_tiles(place_ref, (mixed_a, mixed_b, mixed_c, mixed_d), hidden)
-    load_tiles(place_ref, (cot_a, cot_b, cot_c, cot_d), grad_out)
+    moves.need(entry_w)
 
     for block in range(2):
         win_out, chance_out, stripe_out = (
@@ -389,8 +420,13 @@
         attention_forward(
             block, hidden, gains, shifts, entry_w, entry_b, conv_k, conv_b, wide, stripe, win_out, chance_out
         )
-
-        @pl.loop(0, 4)
+        moves.send(win_out, chance_out)
+        moves.need(exit_w, expand_w, shrink_w)
+        if block == 1:
+            moves.need(cot_a, cot_b, cot_c, cot_d)
+            load_tiles(place_ref, (cot_a, cot_b, cot_c, cot_d), grad_out)
+
+        @pl.loop(0, 2)
         def _(t, block=block, stripe_out=stripe_out):
             rows = chunk(t)
             striped = stripe[rows, :].astype(BF)
@@ -409,7 +445,7 @@
                 feed_delta = (feed_scale * gradient).astype(BF)
                 feed1[rows, :] = feed_delta
                 add_row(vec_out, 4, row_sums(feed_delta.astype(F32)))
-                inner_delta = jnp.zeros((4 * PAD, width), F32)
+                inner_delta = jnp.zeros((CHUNK, width), F32)
             for part in range(hidden_units // width):
                 at = slice(part * width, (part + 1) * width)
                 pre_act = dot_nn(normed, expand_w[block, :, at]) + expand_b[block : block + 1, at]
@@ -438,17 +474,22 @@
                     inner_delta, hat, inverse, gains[block, 1:2, :]
                 )
 
+        moves.send(stripe_out)
+        if block == 0:
+            moves.send(mid0_out, active0_out, slope0_out, hidden1_out)
+        else:
+            moves.send(act_a, act_b, act_c, act_d, grad_out)
+
     put_squares(bundle, 0, dot_tn(inner1[...], pre1[...]), width)
     for part in range(hidden_units // width):
-        put_rows(
-            bundle,
+        bundle.put(
             hidden_units + part * width,
             dot_tn(active1[:, part * width : (part + 1) * width], feed1[...]),
         )
 
 
 def delta_rows(block, place_ref, mask_ref, exit_w, grad_ref, stripe_delta, branch_delta, vec_out, at):
-    @pl.loop(0, 4)
+    @pl.loop(0, 2)
     def _(t):
         rows = chunk(t)
         rounded = (scale_rows(place_ref, mask_ref, 2 * block) * grad_ref[rows, :]).astype(BF)
@@ -462,12 +503,12 @@
 def entry_backward(block, hidden_ref, gains, shifts, entry_w, grad_ref, wide, wide_bf, normed_bf, vec_out, at, emit):
     width = hidden_ref.shape[1]
 
-    @pl.loop(0, 4)
+    @pl.loop(0, 2)
     def _(t):
         rows = chunk(t)
         hat, inverse = norm_parts(hidden_ref[rows, :])
         normed_bf[rows, :] = (hat * gains[block, 0:1, :] + shifts[block, 0:1, :]).astype(BF)
-        delta = jnp.zeros((4 * PAD, width), F32)
+        delta = jnp.zeros((CHUNK, width), F32)
         for part in range(3):
             lanes = slice(part * width, (part + 1) * width)
             rounded = wide[rows, lanes].astype(BF)
@@ -481,31 +522,31 @@
 
 
 def second_kernel(
+    moves,
     place_ref,
     mask_ref,
+    gains,
+    shifts,
+    conv_k,
     grad_in,
-    hidden1,
-    stripe1,
+    exit_w,
     win1,
     chance1,
+    hidden1,
+    entry_w,
+    stripe1,
     mid0,
+    shrink_w,
+    slope0,
+    expand_w,
     active0,
-    slope0,
     stripe0,
-    gains,
-    shifts,
-    entry_w,
-    conv_k,
-    exit_w,
-    expand_w,
-    shrink_w,
-    keep_out,
-    away_out,
     vec_out,
     conv_out,
     grad_out,
     stripe_delta_out,
-    grad,
+    keep_out,
+    away_out,
     stripe_delta,
     branch_delta,
     wide,
@@ -514,24 +555,32 @@
     feed0,
     pre0,
 ):
+    grad = grad_out
     width = grad.shape[1]
     hidden_units = expand_w.shape[2]
-    bundle = (place_ref, keep_out, away_out)
+    bundle = Bundle(
+        place_ref, keep_out, away_out, 4, lambda chunk: jnp.bitwise_xor(place_ref[5], chunk)
+    )
     vec_out[...] = jnp.zeros(vec_out.shape, F32)
     conv_out[...] = jnp.zeros(conv_out.shape, F32)
+    moves.need(grad_in, exit_w)
     delta_rows(1, place_ref, mask_ref, exit_w, grad_in, stripe_delta, branch_delta, vec_out, 0)
+    moves.need(win1, chance1)
     attention_backward(1, win1, chance1, conv_k, stripe_delta, wide, conv_out)
 
     def emit(t, rows, values):
         grad[rows, :] = values
 
+    moves.need(hidden1, entry_w)
     entry_backward(
         1, hidden1, gains, shifts, entry_w, grad_in, wide, wide_bf, normed_bf, vec_out, 2, emit
     )
     put_squares(bundle, 0, dot_tn(normed_bf[...], wide_bf[...]), width)
-    put_rows(bundle, 3 * width, dot_tn(stripe1[...], branch_delta[...]))
-
-    @pl.loop(0, 4)
+    moves.need(stripe1)
+    bundle.put(3 * width, dot_tn(stripe1[...], branch_delta[...]))
+    moves.need(mid0, shrink_w, slope0, expand_w)
+
+    @pl.loop(0, 2)
     def _(t):
         rows = chunk(t)
         gradient = grad[rows, :]
@@ -540,7 +589,7 @@
         feed_delta = (scale_rows(place_ref, mask_ref, 1) * gradient).astype(BF)
         feed0[rows, :] = feed_delta
         add_row(vec_out, 6, row_sums(feed_delta.astype(F32)))
-        inner_delta = jnp.zeros((4 * PAD, width), F32)
+        inner_delta = jnp.zeros((CHUNK, width), F32)
         for part in range(hidden_units // width):
             at = slice(part * width, (part + 1) * width)
             pre_delta = (
@@ -553,35 +602,36 @@
         add_row(vec_out, 12, row_sums(inner_delta))
         grad[rows, :] = gradient + norm_back(inner_delta, hat, inverse, gains[0, 1:2, :])
 
-    grad_out[...] = grad[...]
+    delta_rows(0, place_ref, mask_ref, exit_w, grad, stripe_delta_out, branch_delta, vec_out, 13)
+    moves.send(grad_out, stripe_delta_out)
+    moves.need(active0, stripe0)
     put_squares(bundle, 4 * width, dot_tn(normed_bf[...], pre0[...]), width)
     for part in range(hidden_units // width):
-        put_rows(
-            bundle,
+        bundle.put(
             (8 + part) * width,
             dot_tn(active0[:, part * width : (part + 1) * width], feed0[...]),
         )
-    delta_rows(0, place_ref, mask_ref, exit_w, grad, stripe_delta_out, branch_delta, vec_out, 13)
-    put_rows(bundle, 12 * width, dot_tn(stripe0[...], branch_delta[...]))
+    bundle.put(12 * width, dot_tn(stripe0[...], branch_delta[...]))
 
 
 def third_kernel(
+    moves,
     place_ref,
-    grad_in,
+    gains,
+    shifts,
+    conv_k,
+    vec1,
+    vec2,
+    conv2,
     stripe_delta,
+    win0,
+    chance0,
     mixed_a,
     mixed_b,
     mixed_c,
     mixed_d,
-    win0,
-    chance0,
-    gains,
-    shifts,
     entry_w,
-    conv_k,
-    vec1,
-    vec2,
-    conv2,
+    grad_in,
     out_a,
     out_b,
     out_c,
@@ -597,18 +647,23 @@
     flat,
 ):
     width = hidden.shape[1]
-    bundle = (place_ref, keep_out, away_out)
+    bundle = Bundle(
+        place_ref, keep_out, away_out, 4, lambda chunk: jnp.bitwise_xor(place_ref[5], chunk)
+    )
     vec3[...] = jnp.zeros(vec3.shape, F32)
     conv3[...] = jnp.zeros(conv3.shape, F32)
-    load_tiles(place_ref, (mixed_a, mixed_b, mixed_c, mixed_d), hidden)
+    moves.need(stripe_delta, win0, chance0)
     attention_backward(0, win0, chance0, conv_k, stripe_delta, wide, conv3)
 
     def emit(t, rows, values):
         store_tile(place_ref, (out_a, out_b, out_c, out_d), t, values)
 
+    moves.need(mixed_a, mixed_b, mixed_c, mixed_d, entry_w, grad_in)
+    load_tiles(place_ref, (mixed_a, mixed_b, mixed_c, mixed_d), hidden)
     entry_backward(
         0, hidden, gains, shifts, entry_w, grad_in, wide, wide_bf, normed_bf, vec3, 0, emit
     )
+    moves.send(out_a, out_b, out_c, out_d)
     flat[...] = jnp.zeros(flat.shape, F32)
     at = 0
     for ref in (vec1, vec2, conv2, vec3, conv3):
@@ -618,12 +673,12 @@
     half = keep_out.shape[0]
     middle = width // 2
     lots = flat.shape[0] // 2
-    put_rows(bundle, 0, spread[:, :width])
-    put_rows(bundle, width, spread[:middle, width : 2 * width])
-    put_rows(bundle, width + middle, flat[:lots, :])
-    put_rows(bundle, half, spread[middle:, width : 2 * width])
-    put_rows(bundle, half + middle, spread[:, 2 * width :])
-    put_rows(bundle, half + middle + width, flat[lots:, :])
+    bundle.put(0, spread[:, :width])
+    bundle.put(width, spread[:middle, width : 2 * width])
+    bundle.put(width + middle, flat[:lots, :])
+    bundle.put(half, spread[middle:, width : 2 * width])
+    bundle.put(half + middle, spread[:, 2 * width :])
+    bundle.put(half + middle + width, flat[lots:, :])
 
 
 def untangle(source, flat, target):
@@ -832,28 +887,35 @@
 
 
 def unpack_kernel(
+    ranks,
+    counts,
     place_ref,
-    mine1,
-    other1,
-    mine2,
-    other2,
-    gain_out,
-    shift_out,
-    entry_out,
-    entry_b_out,
-    conv_out,
-    conv_b_out,
-    exit_out,
-    exit_b_out,
-    expand_out,
-    expand_b_out,
-    shrink_out,
-    shrink_b_out,
-    vectors,
+    *refs,
 ):
+    pieces, refs = refs[:8], refs[8:]
+    outs, (vectors, held, fetch_sem, *buffers, send_sem) = refs[:12], refs[12:]
+    copies = [
+        pltpu.make_async_copy(piece, held.at[i], fetch_sem.at[i])
+        for i, piece in enumerate(pieces)
+    ]
+    for copy in copies:
+        copy.start()
+    (
+        gain_out,
+        shift_out,
+        entry_out,
+        entry_b_out,
+        conv_out,
+        conv_b_out,
+        exit_out,
+        exit_b_out,
+        expand_out,
+        expand_b_out,
+        shrink_out,
+        shrink_b_out,
+    ) = buffers
     width = exit_out.shape[1]
     units = expand_out.shape[2]
-    upper = place_ref[2] == 1
     middle = width // 2
 
     def squares(out_ref, block, count):
@@ -864,11 +926,6 @@
 
     plans = (
         squares(expand_out, 1, units // width) + tall(shrink_out, 1, units // width),
-        squares(entry_out, 1, 3)
-        + tall(exit_out, 1, 1)
-        + squares(expand_out, 0, units // width)
-        + tall(shrink_out, 0, units // width)
-        + tall(exit_out, 0, 1),
         [
             (entry_out, 0, 0, 0, width),
             (entry_out, 0, 0, width, middle),
@@ -876,39 +933,48 @@
             (entry_out, 0, middle, width, middle),
             (entry_out, 0, 0, 2 * width, width),
         ],
-    )
-    total = sum(plan[4] for plan in plans[1])
-    ranks = mine2.shape[0]
-    cut = total // 2 // ranks
-    for number, mine, other, base, count in (
-        (0, mine1, other1, 0, mine1.shape[1]),
-        (1, mine2, other2, 0, cut),
-        (2, mine2, other2, cut, mine2.shape[1] - cut),
-    ):
-        pieces = []
+        squares(entry_out, 1, 3)
+        + tall(exit_out, 1, 1)
+        + squares(expand_out, 0, units // width)
+        + tall(shrink_out, 0, units // width)
+        + tall(exit_out, 0, 1),
+    )
+    for copy in copies:
+        copy.wait()
+    inner_ranks = ranks // 4
+    moves = []
+    base = 0
+    for plan, count in zip(plans, counts):
         at = 0
-        for out_ref, block, first_row, lane, length in plans[number]:
+        for out_ref, block, first_row, lane, length in plan:
             done = 0
             while done < length:
                 step = min(length - done, count - at % count)
-                pieces.append((at, step, out_ref, block, first_row + done, lane))
+                moves.append((out_ref, block, first_row + done, lane, base, count, at, step))
                 at += step
                 done += step
-        for at, step, out_ref, block, first_row, lane in pieces:
-            shard, start = at // count, at % count
+        base += count
+    sent = []
+    for target in (expand_out, shrink_out, entry_out, exit_out, vectors):
+        for out_ref, block, first_row, lane, base, count, at, step in moves:
+            if out_ref is not target:
+                continue
+            shard, start = at // count, base + at % count
             half, shard = shard // ranks, shard % ranks
-            if number > 0:
-                shard = jnp.bitwise_xor(place_ref[4], shard)
-            here = upper if half == 1 else jnp.logical_not(upper)
-            rows = slice(base + start, base + start + step)
-            values = jnp.where(
-                here, mine[shard, rows, :].astype(F32), other[shard, rows, :].astype(F32)
-            )
+            first, inner = shard // inner_ranks, shard % inner_ranks
+            piece = 4 * jnp.bitwise_xor(place_ref[2], half) + jnp.bitwise_xor(place_ref[5], first)
+            inner = jnp.bitwise_xor(place_ref[6], inner)
+            values = held[piece, inner, start : start + step, :].astype(F32)
             place = slice(first_row, first_row + step)
             if block is None:
                 out_ref[place, :] = values
             else:
                 out_ref[block, place, lane : lane + width] = values
+        if target is not vectors:
+            i = [j for j, ref in enumerate(buffers) if ref is target][0]
+            copy = pltpu.make_async_copy(target, outs[i], send_sem.at[i])
+            copy.start()
+            sent.append(i)
 
     def line(n):
         return vectors[n : n + 1, :]
@@ -931,6 +997,11 @@
         lanes = slice(part * width, (part + 1) * width)
         expand_b_out[:, lanes] = jnp.concatenate([line(14 + part), line(part)], axis=0)
     shrink_b_out[...] = jnp.concatenate([line(13), line(4)], axis=0)
+    for i, (buffer, out) in enumerate(zip(buffers, outs)):
+        if i not in sent:
+            pltpu.make_async_copy(buffer, out, send_sem.at[i]).start()
+    for i, (buffer, out) in enumerate(zip(buffers, outs)):
+        pltpu.make_async_copy(buffer, out, send_sem.at[i]).wait()
 
 
 SMEM = pl.BlockSpec(memory_space=pltpu.SMEM)
@@ -940,42 +1011,104 @@
 ANYWHERE = pl.BlockSpec(memory_space=pl.ANY)
 
 
-def run(kernel, scalars, arrays, outs, scratch=(), flops=0, name=None, after=(), scalar_outs=()):
-    given = len(scalars) + len(arrays)
+class Moves:
+    def __init__(self, fetched, sent):
+        self.fetched, self.sent = dict(fetched), dict(sent)
+        self.waited, self.started = [], []
+        for copy in self.fetched.values():
+            copy.start()
+
+    def need(self, *refs):
+        for ref in refs:
+            if id(ref) in self.fetched and id(ref) not in self.waited:
+                self.fetched[id(ref)].wait()
+                self.waited.append(id(ref))
+
+    def send(self, *refs):
+        for ref in refs:
+            self.sent[id(ref)].start()
+            self.started.append(id(ref))
+
+    def finish(self):
+        for key, copy in self.fetched.items():
+            if key not in self.waited:
+                copy.wait()
+        for key, copy in self.sent.items():
+            if key not in self.started:
+                copy.start()
+        for copy in self.sent.values():
+            copy.wait()
+
+
+def run(
+    kernel,
+    scalars,
+    arrays,
+    outs,
+    scratch=(),
+    flops=0,
+    name=None,
+    after=(),
+    scalar_outs=(),
+    lazy=None,
+):
+    outs = list(outs)
+    first_in, first_out = (len(arrays), len(outs)) if lazy is None else lazy
+    eager, late = list(arrays[:first_in]), list(arrays[first_in:])
+    n_in = len(scalars) + len(eager)
+    scratch_shapes = [
+        kind if dtype is None else pltpu.VMEM(kind, dtype) for kind, dtype in scratch
+    ]
+    n_own = len(scratch_shapes)
+    n_late, n_sent = len(late), len(outs) - first_out
+    if lazy is not None:
+        scratch_shapes += [pltpu.VMEM(a.shape, a.dtype) for a in late]
+        scratch_shapes += [pltpu.VMEM(*out) for out in outs[first_out:]]
+        scratch_shapes += [pltpu.SemaphoreType.DMA((n_late,)), pltpu.SemaphoreType.DMA((n_sent,))]
 
     def body(*refs):
-        kernel(*refs[:given], *refs[given + len(after) :])
-
-    out_shape = [jax.ShapeDtypeStruct(shape, dtype) for shape, dtype in scalar_outs + tuple(outs)]
+        given, refs = refs[:n_in], refs[n_in:]
+        sources, refs = refs[:n_late], refs[n_late + len(after) :]
+        results, refs = refs[: len(scalar_outs) + first_out], refs[len(scalar_outs) + first_out :]
+        targets, refs = refs[:n_sent], refs[n_sent:]
+        own, refs = refs[:n_own], refs[n_own:]
+        if lazy is None:
+            kernel(*given, *results, *own)
+            return
+        buffers, leaving = refs[:n_late], refs[n_late : n_late + n_sent]
+        fetch_sem, send_sem = refs[n_late + n_sent :]
+        moves = Moves(
+            [
+                (id(buffer), pltpu.make_async_copy(source, buffer, fetch_sem.at[i]))
+                for i, (source, buffer) in enumerate(zip(sources, buffers))
+            ],
+            [
+                (id(buffer), pltpu.make_async_copy(buffer, target, send_sem.at[i]))
+                for i, (buffer, target) in enumerate(zip(leaving, targets))
+            ],
+        )
+        kernel(moves, *given, *buffers, *results, *leaving, *own)
+        moves.finish()
+
+    out_shape = [jax.ShapeDtypeStruct(shape, dtype) for shape, dtype in tuple(scalar_outs) + tuple(outs)]
     moved = sum(a.size * a.dtype.itemsize for a in arrays)
     return pl.pallas_call(
         body,
         out_shape=out_shape,
-        in_specs=[SMEM] * len(scalars) + [VMEM] * len(arrays) + [ANYWHERE] * len(after),
-        out_specs=[SMEM] * len(scalar_outs) + [VMEM] * len(outs),
-        scratch_shapes=[
-            kind if dtype is None else pltpu.VMEM(kind, dtype) for kind, dtype in scratch
-        ],
+        in_specs=[SMEM] * len(scalars)
+        + [VMEM] * len(eager)
+        + [ANYWHERE] * (n_late + len(after)),
+        out_specs=[SMEM] * len(scalar_outs) + [VMEM] * first_out + [ANYWHERE] * n_sent,
+        scratch_shapes=scratch_shapes,
         compiler_params=pltpu.CompilerParams(vmem_limit_bytes=VMEM_BYTES),
         cost_estimate=pl.CostEstimate(flops=flops, bytes_accessed=moved, transcendentals=0),
         name=name,
-    )(*scalars, *arrays, *after)
+    )(*scalars, *eager, *late, *after)
 
 
 def gate(values, after):
     values, after = list(values), list(after)
-
-    def body(*refs):
-        del refs
-
-    return pl.pallas_call(
-        body,
-        out_shape=[jax.ShapeDtypeStruct(v.shape, v.dtype) for v in values],
-        in_specs=[ANYWHERE] * (len(values) + len(after)),
-        out_specs=[ANYWHERE] * len(values),
-        input_output_aliases={i: i for i in range(len(values))},
-        name="gate",
-    )(*values, *after)
+    return list(lax.optimization_barrier(tuple(values + after)))[: len(values)]
 
 
 def swap(values, axis):
@@ -1075,7 +1208,20 @@
     capacity = (2 * images_here + groups - 1) // groups
     slots = groups * capacity
     order = rank_order(lax.axis_index(RANKS), ranks)
-    place = jnp.stack([lax.axis_index("dp"), row, col, 2 * row + col, order]).astype(jnp.int32)
+    place = jnp.stack(
+        [
+            lax.axis_index("dp"),
+            row,
+            col,
+            2 * row + col,
+            order,
+            order // (ranks // 4),
+            order % (ranks // 4),
+        ]
+    ).astype(jnp.int32)
+    spots = [0] * ranks
+    for rank in range(ranks):
+        spots[rank_order(rank, ranks)] = rank
     quad = ((share, TILE, 8, width), BF)
     corners = corners.T
     masks = drop_masks.T
@@ -1106,13 +1252,13 @@
     conv_k = position_kernel.transpose(1, 2, 0, 3)
     tall = (rows, width)
     (
+        vec1,
         act_a,
         act_b,
         act_c,
         act_d,
         keep1,
         away1,
-        vec1,
         active0,
         slope0,
         win0,
@@ -1125,29 +1271,29 @@
         hidden1,
         grad1,
     ) = run(
-        first_kernel,
+        functools.partial(first_kernel, spots),
         [place, masks],
         [
             *mixed,
-            *cot,
             norm_gains,
             norm_shifts,
-            entry_weight,
             entry_bias,
             conv_k,
             position_bias,
+            exit_bias,
+            expand_bias,
+            shrink_bias,
+            entry_weight,
             exit_weight,
-            exit_bias,
             expand_weight,
-            expand_bias,
             shrink_weight,
-            shrink_bias,
+            *cot,
         ],
         [
+            ((7, 8, width), F32),
             *([quad] * 4),
             ((units, width), BF),
             ((units, width), BF),
-            ((7, 8, width), F32),
             ((rows, units), BF),
             ((rows, units), BF),
             ((4 * share, WIN, 3 * HALF), BF),
@@ -1171,41 +1317,40 @@
         ],
         flops=10 * rows * width * width * 120,
         name="first",
+        lazy=(12, 1),
     )
     sent1 = shards(added(keep1, swap(away1, "col")), ranks)
     pieces1 = lax.all_to_all(sent1, RANKS, split_axis=0, concat_axis=0, tiled=True)
-    act = deal([act_a, act_b, act_c, act_d])
-    keep2, away2, vec2, conv2, grad0, delta0 = run(
+    vec2, conv2, grad0, delta0, keep2, away2 = run(
         second_kernel,
         [place, masks],
         [
+            norm_gains,
+            norm_shifts,
+            conv_k,
             grad1,
-            hidden1,
-            stripe1,
+            exit_weight,
             win1,
             chance1,
+            hidden1,
+            entry_weight,
+            stripe1,
             mid0,
+            shrink_weight,
+            slope0,
+            expand_weight,
             active0,
-            slope0,
             stripe0,
-            norm_gains,
-            norm_shifts,
-            entry_weight,
-            conv_k,
-            exit_weight,
-            expand_weight,
-            shrink_weight,
         ],
         [
-            ((13 * width // 2, width), BF),
-            ((13 * width // 2, width), BF),
             ((15, 8, width), F32),
             ((9, 8, width), F32),
             (tall, F32),
             (tall, F32),
+            ((13 * width // 2, width), BF),
+            ((13 * width // 2, width), BF),
         ],
         [
-            (tall, F32),
             (tall, F32),
             (tall, BF),
             ((rows, 3 * width), F32),
@@ -1217,28 +1362,38 @@
         flops=6 * rows * width * width * 120,
         name="second",
         after=[sent1],
-    )
-    keep2, away2, grad0, delta0 = gate([keep2, away2, grad0, delta0], [pieces1, *act])
-    spread1 = spread_sum(pieces1)
+        lazy=(3, 2),
+    )
+    act = deal([act_a, act_b, act_c, act_d])
+    keep2, away2, grad0, delta0, *act = gate([keep2, away2, grad0, delta0, *act], [pieces1])
     steps = stages(ranks)
-    parts2 = scatter_send(added(keep2, swap(away2, "col")), ranks, steps[0])
+
+    def first_parts(keep, away):
+        other = swap(away, "col")
+        count = keep.shape[0] // 4
+        return [
+            added(keep[d * count : (d + 1) * count], other[d * count : (d + 1) * count])
+            for d in range(4)
+        ]
+
+    parts2 = first_parts(keep2, away2)
     moved2 = scatter_move(parts2, ranks, steps[0])
     *out_tiles, keep3, away3 = run(
         third_kernel,
         [place],
         [
-            grad0,
-            delta0,
-            *mixed,
-            win0,
-            chance0,
             norm_gains,
             norm_shifts,
-            entry_weight,
             conv_k,
             vec1,
             vec2,
             conv2,
+            delta0,
+            win0,
+            chance0,
+            *mixed,
+            entry_weight,
+            grad0,
         ],
         [quad] * 4 + [((2 * width, width), BF), ((2 * width, width), BF)],
         [
@@ -1253,9 +1408,9 @@
         flops=3 * rows * width * width * 120,
         name="third",
         after=parts2,
-    )
-    *held, keep3, away3 = gate([*moved2, keep3, away3], [])
-    moved2 = held
+        lazy=(6, 0),
+    )
+    *moved2, keep3, away3 = gate([*moved2, keep3, away3], out_tiles)
     gradient = deal(out_tiles)
     (parted,) = run(
         split_kernel,
@@ -1264,6 +1419,26 @@
         [((slots, TILE, 8, width), BF)],
         name="split",
     )
+    mine1 = jnp.sum(pieces1.astype(F32), axis=0).astype(BF)
+    mine2 = scatter_sum(moved2)
+    mine3 = scatter_sum(scatter_move(first_parts(keep3, away3), ranks, steps[0]))
+    cut = mine2.shape[0] * 4 // ranks
+    lot = mine3.shape[0] * 4 // ranks
+    joint = jnp.concatenate(
+        [
+            mine3.reshape(ranks // 4, lot, width),
+            mine2.reshape(ranks // 4, cut, width),
+        ],
+        axis=1,
+    ).reshape(-1, width)
+    for step in steps[1:]:
+        joint = scatter_sum(scatter_move(scatter_send(joint, ranks, step), ranks, step))
+    joint = jnp.concatenate([mine1, joint], axis=0)
+    counts = (mine1.shape[0], lot, cut)
+    for step in reversed(steps[1:]):
+        joint = gather(joint, ranks, step).reshape(-1, width)
+    joint = shards(joint, ranks // 4)
+    (parted,) = gate([parted], [joint])
     back = lax.all_to_all(parted, "dp", split_axis=0, concat_axis=0, tiled=True)
     (input_gradient,) = run(
         join_kernel,
@@ -1273,50 +1448,42 @@
         [((width // 128, (images_here + 1) * PAD, 128), F32)],
         name="join",
     )
-    full1 = lax.all_to_all(spread1, RANKS, split_axis=0, concat_axis=0, tiled=True)
-    mine2 = scatter_sum(moved2)
-    moved3 = scatter_move(
-        scatter_send(added(keep3, swap(away3, "col")), ranks, steps[0]), ranks, steps[0]
-    )
-    mine3 = scatter_sum(moved3)
-    cut = mine2.shape[0] * 4 // ranks
-    lot = mine3.shape[0] * 4 // ranks
-    joint = jnp.concatenate(
-        [
-            mine2.reshape(ranks // 4, cut, width),
-            mine3.reshape(ranks // 4, lot, width),
-        ],
-        axis=1,
-    ).reshape(-1, width)
-    for step in steps[1:]:
-        joint = scatter_sum(scatter_move(scatter_send(joint, ranks, step), ranks, step))
-    for step in reversed(steps):
-        joint = gather(joint, ranks, step).reshape(-1, width)
-    joint = shards(joint, ranks)
-    full = [full1, swap(full1, "col"), joint, swap(joint, "col")]
+    full = [joint] + [across(joint, RANKS, ranks, d) for d in (1, 2, 3)]
+    full += [swap(piece, "col") for piece in full]
+    full = gate(full, [input_gradient])
     (activations,) = run(
         lay_kernel, [place], act, [((TILE, TILE, images_here, width), BF)], [flat], name="lay"
     )
-    gains, shifts, entry, entry_b, conv, conv_b, exit_, exit_b, expand, expand_b, shrink, shrink_b = run(
-        unpack_kernel,
-        [place],
-        full,
-        [
-            ((2, 2, width), F32),
-            ((2, 2, width), F32),
-            ((2, width, 3 * width), F32),
-            ((2, 2 * width), F32),
-            ((3, 3, 2, width), F32),
-            ((2, width), F32),
-            ((2, width, width), F32),
-            ((2, width), F32),
-            ((2, width, units), F32),
-            ((2, units), F32),
-            ((2, units, width), F32),
-            ((2, width), F32),
-        ],
-        [((width // 2, width), F32)],
-        name="unpack",
+    shapes = [
+        (2, 2, width),
+        (2, 2, width),
+        (2, width, 3 * width),
+        (2, 2 * width),
+        (3, 3, 2, width),
+        (2, width),
+        (2, width, width),
+        (2, width),
+        (2, width, units),
+        (2, units),
+        (2, units, width),
+        (2, width),
+    ]
+    gains, shifts, entry, entry_b, conv, conv_b, exit_, exit_b, expand, expand_b, shrink, shrink_b = (
+        pl.pallas_call(
+            functools.partial(unpack_kernel, ranks, counts),
+            out_shape=[jax.ShapeDtypeStruct(shape, F32) for shape in shapes],
+            in_specs=[SMEM] + [ANYWHERE] * 8,
+            out_specs=[ANYWHERE] * 12,
+            scratch_shapes=[
+                pltpu.VMEM((width // 2, width), F32),
+                pltpu.VMEM((8,) + joint.shape, BF),
+                pltpu.SemaphoreType.DMA((8,)),
+            ]
+            + [pltpu.VMEM(shape, F32) for shape in shapes]
+            + [pltpu.SemaphoreType.DMA((12,))],
+            compiler_params=pltpu.CompilerParams(vmem_limit_bytes=VMEM_BYTES),
+            name="unpack",
+        )(place, *full)
     )
     return (
         activations.transpose(2, 0, 1, 3),

time: 229 us -> 206 us (0.90)
  Pallas kernels: 108 us -> 86.7 us
  starting transfers between devices: 50.4 us -> 44 us
  waiting for transfers between devices: 56.7 us -> 61.2 us
  local copies, waits for them, and re-layouts: 8.27 us -> 5.71 us
  other arithmetic: 3.88 us -> 6.27 us
    pallas_call x10 -> x9, Pallas kernels: 108 us -> 81.2 us  [run(): pl.pallas_call(body, out_shape=out_shape, in_specs=[SMEM] * len(scalars)...]
    all_to_all x1 -> x0, starting transfers between devices: 6.9 us -> none  [local(): lax.all_to_all(spread1, RANKS, split_axis=0, concat_axis=0, tiled=True)]
    pallas_call x2 -> x1, Pallas kernels: 0.01 us -> 5.5 us  [local(): pl.pallas_call(functools.partial(unpack_kernel, ranks, counts), out_shape...]
    ppermute x27, waiting for transfers between devices: 41.8 us -> 45 us  [across(): return lax.ppermute(values, axes, [(i, i ^ mask) for i in range(size)])]
    unnamed x66 -> x54, local copies, waits for them, and re-layouts: 6.02 us -> 5.02 us
  transfers between devices with their start and end apart: 36 -> 37, of which waited for: 13 -> 15; matrix products, arithmetic and copies ran while one was open for 1% -> 1% of each run, Pallas kernels for 23% -> 21%
where the time goes in v3:
time: 206 us; the launch traced here: 205 us
  Pallas kernels  86.7 us (42%)
  waiting for transfers between devices  61.2 us (30%)
  starting transfers between devices  44 us (21%)
  other arithmetic  6.27 us (3%)
  local copies, waits for them, and re-layouts  5.71 us (3%)
    pallas_call x9, Pallas kernels, run(): pl.pallas_call(body, out_shape=out_shape, in_specs=[SMEM] * len(scalars)...  81.2 us
    ppermute x27, waiting for transfers between devices, across(): return lax.ppermute(values, axes, [(i, i ^ mask) for i in range(size)])  45 us
    ppermute x27, starting transfers between devices, across(): return lax.ppermute(values, axes, [(i, i ^ mask) for i in range(size)])  27 us
    all_to_all x1, waiting for transfers between devices, local(): lax.all_to_all(outgoing, 'dp', split_axis=0, concat_axis=0, tiled=True)  12.5 us
    all_to_all x1, starting transfers between devices, local(): lax.all_to_all(outgoing, 'dp', split_axis=0, concat_axis=0, tiled=True)  7.29 us
    pallas_call x1, Pallas kernels, local(): pl.pallas_call(functools.partial(unpack_kernel, ranks, counts), out_shape...  5.5 us
    convert_element_type x3, other arithmetic, added(): return (values.astype(F32) + others.astype(F32)).astype(BF)  5.04 us
    unnamed x54, local copies, waits for them, and re-layouts  5.02 us
  transfers between devices with their start and end apart: 37, of which 15 were waited for; matrix products, arithmetic and copies ran while one was open for 1% of the time, Pallas kernels for 21%

profile of v3, /device:TPU:0, one launch (start us, length us, event | category | flops | bytes accessed | tf_op | source)
XLA Modules:
  0.0 205.1 jit_solution(13706134123587613731)
XLA Ops:
  1.4 3.9 %pick.1 = (s32[40]{0:T(128)}, s32[32]{0:T(128)}, bf16[32,7,8,256]{3,2,1,0:T(8,128)(2,1)}, bf16[16,7,8,256]{3,2,1,0:T(8,128)(2,1)}) custom-call(s32[7]{0:T(128)} %stack.46.refs_0_.place_ref, s32[128]{0:T(128)} %refs_1_.2, s32[128]{0:T(128)} %refs_2_.3, bf16[7,7,16,256]{3,2,1,0:T(8,128)(2,1)} %bitcast.39), custom_call_target="tpu_custom_call" | custom-call | bytes 401408 | tf_op jit(solution)/shard_map/pick/pallas_call | solution.py:1095
  5.2 7.3 %all-to-all-start = ((bf16[32,7,8,256]{3,2,1,0:T(8,128)(2,1)}), bf16[32,7,8,256]{3,2,1,0:T(8,128)(2,1)S(1)}, u32[]{:S(2)}, u32[]{:S(2)}) async-start(bf16[32,7,8,256]{3,2,1,0:T(8,128)(2,1)} %get-tuple-element.92), calls=%async_computation | async-start | bytes 1835008 | tf_op jit(solution)/shard_map/all_to_all | solution.py:1238
  12.5 2.7 %deal.1 = (bf16[4,7,8,256]{3,2,1,0:T(8,128)(2,1)}, bf16[4,7,8,256]{3,2,1,0:T(8,128)(2,1)}, bf16[4,7,8,256]{3,2,1,0:T(8,128)(2,1)}, bf16[4,7,8,256]{3,2,1,0:T(8,128)(2,1)}) custom-call(s32[7]{0:T(128)} %stack.46.refs_0_.place_ref, bf16[7,7,16,256]{3,2,1,0:T(8,128)(2,1)} %bitcast.40), custom_call_target="tpu_custom_call" | custom-call | bytes 401408 | tf_op jit(solution)/shard_map/deal/pallas_call | solution.py:1095
  17.1 4.3 %collective-permute-done.1.refs_8_.refs_20_ = bf16[4,7,8,256]{3,2,1,0:T(8,128)(2,1)S(1)} collective-permute-done((bf16[4,7,8,256]{3,2,1,0:T(8,128)(2,1)}, bf16[4,7,8,256]{3,2,1,0:T(8,128)(2,1)S(1)}, u32[]{:S(2)}, u32[]{:S(2)}) %collective-permute-start.1) | collective-permute-done | bytes 114720 | tf_op jit(solution)/shard_map/ppermute | solution.py:1132
  23.0 12.5 %all-to-all-done.refs_4_ = bf16[32,7,8,256]{3,2,1,0:T(8,128)(2,1)S(1)} async-done(((bf16[32,7,8,256]{3,2,1,0:T(8,128)(2,1)}), bf16[32,7,8,256]{3,2,1,0:T(8,128)(2,1)S(1)}, u32[]{:S(2)}, u32[]{:S(2)}) %all-to-all-start) | async-done | bytes 917536 | tf_op jit(solution)/shard_map/all_to_all | solution.py:1238
  36.5 2.7 %mix.1 = (bf16[4,7,8,256]{3,2,1,0:T(8,128)(2,1)}, bf16[4,7,8,256]{3,2,1,0:T(8,128)(2,1)}, bf16[4,7,8,256]{3,2,1,0:T(8,128)(2,1)}, bf16[4,7,8,256]{3,2,1,0:T(8,128)(2,1)}) custom-call(s32[7]{0:T(128)} %stack.46.refs_0_.place_ref, s32[32]{0:T(128)} %get-tuple-element.91.refs_1_, s32[4,16]{1,0:T(4,128)} %bitcast.45, f32[16]{0:T(128)} %refs_3_.7, ...), custom_call_target="tpu_custom_call" | custom-call | bytes 1376256 | tf_op jit(solution)/shard_map/mix/pallas_call | solution.py:1095
  41.0 4.3 %collective-permute-done.4.refs_4_.refs_12_ = bf16[4,7,8,256]{3,2,1,0:T(8,128)(2,1)S(1)} collective-permute-done((bf16[4,7,8,256]{3,2,1,0:T(8,128)(2,1)}, bf16[4,7,8,256]{3,2,1,0:T(8,128)(2,1)S(1)}, u32[]{:S(2)}, u32[]{:S(2)}) %collective-permute-start.4) | collective-permute-done | bytes 114720 | tf_op jit(solution)/shard_map/ppermute | solution.py:1132
  47.6 32.2 %first.1 = (f32[7,8,256]{2,1,0:T(8,128)}, bf16[4,7,8,256]{3,2,1,0:T(8,128)(2,1)}, bf16[4,7,8,256]{3,2,1,0:T(8,128)(2,1)}, bf16[4,7,8,256]{3,2,1,0:T(8,128)(2,1)}...) custom-call(s32[7]{0:T(128)} %stack.46.refs_0_.place_ref, ...), custom_call_target="tpu_custom_call" | custom-call | flops 70464307200 | bytes 4108288 | tf_op jit(solution)/shard_map/first/pallas_call | solution.py:1095
  84.0 4.6 %all-to-all-start.1 = ((bf16[16,64,256]{2,1,0:T(8,128)(2,1)}), bf16[16,64,256]{2,1,0:T(8,128)(2,1)S(1)}, u32[]{:S(2)}, u32[]{:S(2)}) async-start(bf16[16,64,256]{2,1,0:T(8,128)(2,1)} %bitcast.12.refs_18_), calls=%async_computation.1 | async-start | bytes 1048576 | tf_op jit(solution)/shard_map/all_to_all | solution.py:1323
  88.5 19.7 %second.1 = (f32[15,8,256]{2,1,0:T(8,128)}, f32[9,8,256]{2,1,0:T(8,128)}, f32[896,256]{1,0:T(8,128)}, f32[896,256]{1,0:T(8,128)}, bf16[1664,256]{1,0:T(8,128)(2,1)}, /*index=5*/bf16[1664,256]{1,0:T(8,128)(2,1)}) custom-call(s32[7]{0:T(128)} %stack.46.refs_0_.place_ref, s32[4,16]{1,0:T(4,128)} %bitcast.53, f32[2,2,256]{2,1,0:T(2,128)} %refs_1_.3, ...), custom_call_target="tpu_custom_call" | custom-call | flops 42278584320 | bytes 13723648 | tf_op jit(solution)/shard_map/second/pallas_call | solution.py:1095
  110.9 2.1 %add_convert_fusion.2 = (bf16[416,256]{1,0:T(8,128)(2,1)S(1)}, bf16[416,256]{1,0:T(8,128)(2,1)S(1)}, bf16[416,256]{1,0:T(8,128)(2,1)S(1)}, bf16[416,256]{1,0:T(8,128)(2,1)}) fusion(bf16[1664,256]{1,0:T(8,128)(2,1)S(1)} %collective-permute-done.10, bf16[1664,256]{1,0:T(8,128)(2,1)} %get-tuple-element.133), kind=kLoop, calls=%fused_computation.6 | loop fusion | flops 1703936 | bytes 2555904 | tf_op jit(solution)/shard_map/convert_element_type | solution.py:1119
  116.6 12.4 %third.1 = (bf16[4,7,8,256]{3,2,1,0:T(8,128)(2,1)}, bf16[4,7,8,256]{3,2,1,0:T(8,128)(2,1)}, bf16[4,7,8,256]{3,2,1,0:T(8,128)(2,1)}, bf16[4,7,8,256]{3,2,1,0:T(8,...) custom-call(s32[7]{0:T(128)} %stack.46.refs_0_.place_ref, f32[2,2,256]{2,1,0:T(2,128)} %refs_1_.3, ...), custom_call_target="tpu_custom_call" | custom-call | flops 21139292160 | bytes 6572032 | tf_op jit(solution)/shard_map/third/pallas_call | solution.py:1095
  131.8 2.0 collective-permute-start.18
  138.1 2.4 %collective-permute-done.20 = bf16[128,256]{1,0:T(8,128)(2,1)S(1)} collective-permute-done((bf16[128,256]{1,0:T(8,128)(2,1)S(1)}, bf16[128,256]{1,0:T(8,128)(2,1)S(1)}, u32[]{:S(2)}, u32[]{:S(2)}) %collective-permute-start.20) | collective-permute-done | bytes 65568 | tf_op jit(solution)/shard_map/ppermute | solution.py:1132
  142.9 2.4 %collective-permute-start.22 = (bf16[136,256]{1,0:T(8,128)(2,1)S(1)}, bf16[136,256]{1,0:T(8,128)(2,1)S(1)}, u32[]{:S(2)}, u32[]{:S(2)}) collective-permute-start(bf16[136,256]{1,0:T(8,128)(2,1)S(1)} %get-tuple-element.176), channel_id=1, source_target_pairs={{0,16},{2,18},{4,20},{6,22},{8,24},{10,26},{12,28},{14,30},{16,0},... | collective-permute-start | bytes 208904 | tf_op jit(solution)/shard_map/ppermute | solution.py:1132
  153.0 2.9 %collective-permute-start.26 = (bf16[200,256]{1,0:T(8,128)(2,1)S(1)}, bf16[200,256]{1,0:T(8,128)(2,1)S(1)}, u32[]{:S(2)}, u32[]{:S(2)}) collective-permute-start(bf16[200,256]{1,0:T(8,128)(2,1)S(1)} %get-tuple-element.179), channel_id=1, source_target_pairs={{0,24},{2,26},{4,28},{6,30},{8,16},{10,18},{12,20},{14,22},{16,8},... | collective-permute-start | bytes 307208 | tf_op jit(solution)/shard_map/ppermute | solution.py:1132
  157.2 2.5 %split.1 = bf16[32,7,8,256]{3,2,1,0:T(8,128)(2,1)} custom-call(s32[7]{0:T(128)} %stack.46.refs_0_.place_ref, s32[32]{0:T(128)} %get-tuple-element.91.refs_1_, s32[4,16]{1,0:T(4,128)} %bitcast.46, f32[16]{0:T(128)} %refs_3_.7, bf16[4,7,8,256]{3,2,1,0:T(8,128)(2,1)} %get-tuple-element.135.refs_4_, bf16[4,7,8,256]{3,2,1,0:T(8,128)(2,1)} %copy-done.4, ...), custom_call_target="tpu_custom_call" | custom-call | bytes 458752 | tf_op jit(solution)/shard_map/split/pallas_call | solution.py:1095
  160.5 3.9 %all-to-all-start.2 = ((bf16[32,7,8,256]{3,2,1,0:T(8,128)(2,1)}), bf16[32,7,8,256]{3,2,1,0:T(8,128)(2,1)S(1)}, u32[]{:S(2)}, u32[]{:S(2)}) async-start(bf16[32,7,8,256]{3,2,1,0:T(8,128)(2,1)} %split.1), calls=%async_computation.2 | async-start | bytes 1835008 | tf_op jit(solution)/shard_map/all_to_all | solution.py:1442
  165.0 2.0 collective-permute-start.28
  168.0 8.9 %collective-permute-done.27.refs_1_ = bf16[4,200,256]{2,1,0:T(8,128)(2,1)S(1)} collective-permute-done((bf16[4,200,256]{2,1,0:T(8,128)(2,1)S(1)}, bf16[4,200,256]{2,1,0:T(8,128)(2,1)S(1)}, u32[]{:S(2)}, u32[]{:S(2)}) %collective-permute-start.27) | collective-permute-done | bytes 409632 | tf_op jit(solution)/shard_map/ppermute | solution.py:1132
  176.9 14.9 %collective-permute-done.28.refs_2_ = bf16[4,200,256]{2,1,0:T(8,128)(2,1)S(1)} collective-permute-done((bf16[4,200,256]{2,1,0:T(8,128)(2,1)S(1)}, bf16[4,200,256]{2,1,0:T(8,128)(2,1)S(1)}, u32[]{:S(2)}, u32[]{:S(2)}) %collective-permute-start.28) | collective-permute-done | bytes 409632 | tf_op jit(solution)/shard_map/ppermute | solution.py:1132
  192.3 2.1 %lay.1 = bf16[7,7,16,256]{3,2,1,0:T(8,128)(2,1)} custom-call(s32[7]{0:T(128)} %stack.46.refs_0_.place_ref, bf16[4,7,8,256]{3,2,1,0:T(8,128)(2,1)} %get-tuple-element.121.refs_1_, bf16[4,7,8,256]{3,2,1,0:T(8,128)(2,1)} %copy-done.15, bf16[4,7,8,256]{3,2,1,0:T(8,128)(2,1)} %copy-done.16, bf16[4,7,8,256]{3,2,1,0:T(8,128)(2,1)} %copy-done.17), custom_call_target="tpu_custom_call" | custom-call | bytes 458752 | tf_op jit(solution)/shard_map/lay/pallas_call | solution.py:1095
  195.4 3.2 %join.1 = f32[7,7,16,256]{3,2,1,0:T(8,128)} custom-call(s32[7]{0:T(128)} %stack.46.refs_0_.place_ref, s32[40]{0:T(128)} %get-tuple-element.125.refs_1_, s32[4,16]{1,0:T(4,128)} %bitcast.47, f32[16]{0:T(128)} %refs_3_.7, bf16[4,7,8,256]{3,2,1,0:T(8,128)(2,1)} %get-tuple-element.135.refs_4_, bf16[4,7,8,256]{3,2,1,0:T(8,128)(2,1)} %copy-done.4, ...), custom_call_target="tpu_custom_call" | custom-call | bytes 1376256 | tf_op jit(solution)/shard_map/join/pallas_call | solution.py:1095
  199.5 5.5 %unpack.1 = (f32[2,2,256]{2,1,0:T(2,128)}, f32[2,2,256]{2,1,0:T(2,128)}, f32[2,256,768]{2,1,0:T(8,128)}, f32[2,512]{1,0:T(2,128)}, f32[3,3,2,256]{3,2,1,0:T(2,12...) custom-call(s32[7]{0:T(128)} %stack.46.refs_0_.place_ref, ...), custom_call_target="tpu_custom_call" | custom-call | tf_op jit(solution)/shard_map/unpack/pallas_call | solution.py:1472
  (125 shorter events, 42.7 us)
Async XLA Ops:
  5.2 30.3 %all-to-all-start = ((bf16[32,7,8,256]{3,2,1,0:T(8,128)(2,1)}), bf16[32,7,8,256]{3,2,1,0:T(8,128)(2,1)S(1)}, u32[]{:S(2)}, u32[]{:S(2)}) async-start(bf16[32,7,8,256]{3,2,1,0:T(8,128)(2,1)} %get-tuple-element.92), calls=%async_computation | async-start | bytes 1835008 | tf_op jit(solution)/shard_map/all_to_all | solution.py:1238
  16.7 6.3 %collective-permute-start.2 = (bf16[4,7,8,256]{3,2,1,0:T(8,128)(2,1)}, bf16[4,7,8,256]{3,2,1,0:T(8,128)(2,1)S(1)}, u32[]{:S(2)}, u32[]{:S(2)}) collective-permute-start(bf16[4,7,8,256]{3,2,1,0:T(8,128)(2,1)} %get-tuple-element.97), channel_id=1, source_target_pairs={{0,3},{1,2},{2,1},{3,0},{4,7},{5,6},{6,5},{7,4},{8,11},{9,10},{10,... | collective-permute-start | bytes 344072 | tf_op jit(solution)/shard_map/ppermute | solution.py:1132
  80.1 28.1 %collective-permute-start.7 = (bf16[4,7,8,256]{3,2,1,0:T(8,128)(2,1)}, bf16[4,7,8,256]{3,2,1,0:T(8,128)(2,1)S(1)}, u32[]{:S(2)}, u32[]{:S(2)}) collective-permute-start(bf16[4,7,8,256]{3,2,1,0:T(8,128)(2,1)} %get-tuple-element.118), channel_id=1, source_target_pairs={{0,1},{1,0},{2,3},{3,2},{4,5},{5,4},{6,7},{7,6},{8,9},{9,8},{10,11... | collective-permute-start | bytes 344072 | tf_op jit(solution)/shard_map/ppermute | solution.py:1132
  80.4 27.8 %collective-permute-start.8 = (bf16[4,7,8,256]{3,2,1,0:T(8,128)(2,1)}, bf16[4,7,8,256]{3,2,1,0:T(8,128)(2,1)S(1)}, u32[]{:S(2)}, u32[]{:S(2)}) collective-permute-start(bf16[4,7,8,256]{3,2,1,0:T(8,128)(2,1)} %get-tuple-element.119), channel_id=1, source_target_pairs={{0,2},{1,3},{2,0},{3,1},{4,6},{5,7},{6,4},{7,5},{8,10},{9,11},{10,... | collective-permute-start | bytes 344072 | tf_op jit(solution)/shard_map/ppermute | solution.py:1132
  81.9 26.4 %collective-permute-start.9 = (bf16[4,7,8,256]{3,2,1,0:T(8,128)(2,1)}, bf16[4,7,8,256]{3,2,1,0:T(8,128)(2,1)S(1)}, u32[]{:S(2)}, u32[]{:S(2)}) collective-permute-start(bf16[4,7,8,256]{3,2,1,0:T(8,128)(2,1)} %get-tuple-element.120), channel_id=1, source_target_pairs={{0,3},{1,2},{2,1},{3,0},{4,7},{5,6},{6,5},{7,4},{8,11},{9,10},{10,... | collective-permute-start | bytes 344072 | tf_op jit(solution)/shard_map/ppermute | solution.py:1132
  84.0 24.3 %all-to-all-start.1 = ((bf16[16,64,256]{2,1,0:T(8,128)(2,1)}), bf16[16,64,256]{2,1,0:T(8,128)(2,1)S(1)}, u32[]{:S(2)}, u32[]{:S(2)}) async-start(bf16[16,64,256]{2,1,0:T(8,128)(2,1)} %bitcast.12.refs_18_), calls=%async_computation.1 | async-start | bytes 1048576 | tf_op jit(solution)/shard_map/all_to_all | solution.py:1323
  113.1 16.0 %collective-permute-start.14 = (bf16[416,256]{1,0:T(8,128)(2,1)S(1)}, bf16[416,256]{1,0:T(8,128)(2,1)S(1)}, u32[]{:S(2)}, u32[]{:S(2)}) collective-permute-start(bf16[416,256]{1,0:T(8,128)(2,1)S(1)} %get-tuple-element.170.refs_17_), channel_id=1, source_target_pairs={{0,2},{2,0},{4,6},{6,4},{8,10},{10,8},{12,14},{14,12},{16,18},{18,... | collective-permute-start | bytes 638984 | tf_op jit(solution)/shard_map/ppermute | solution.py:1132
  115.0 14.0 %collective-permute-start.15 = (bf16[416,256]{1,0:T(8,128)(2,1)S(1)}, bf16[416,256]{1,0:T(8,128)(2,1)S(1)}, u32[]{:S(2)}, u32[]{:S(2)}) collective-permute-start(bf16[416,256]{1,0:T(8,128)(2,1)S(1)} %get-tuple-element.169.refs_18_), channel_id=1, source_target_pairs={{0,4},{2,6},{4,0},{6,2},{8,12},{10,14},{12,8},{14,10},{16,20},{18,... | collective-permute-start | bytes 638984 | tf_op jit(solution)/shard_map/ppermute | solution.py:1132
  116.5 12.6 %collective-permute-start.16 = (bf16[416,256]{1,0:T(8,128)(2,1)S(1)}, bf16[416,256]{1,0:T(8,128)(2,1)S(1)}, u32[]{:S(2)}, u32[]{:S(2)}) collective-permute-start(bf16[416,256]{1,0:T(8,128)(2,1)S(1)} %get-tuple-element.168.refs_19_), channel_id=1, source_target_pairs={{0,6},{2,4},{4,2},{6,0},{8,14},{10,12},{12,10},{14,8},{16,22},{18,... | collective-permute-start | bytes 638984 | tf_op jit(solution)/shard_map/ppermute | solution.py:1132
  142.9 6.7 %collective-permute-start.22 = (bf16[136,256]{1,0:T(8,128)(2,1)S(1)}, bf16[136,256]{1,0:T(8,128)(2,1)S(1)}, u32[]{:S(2)}, u32[]{:S(2)}) collective-permute-start(bf16[136,256]{1,0:T(8,128)(2,1)S(1)} %get-tuple-element.176), channel_id=1, source_target_pairs={{0,16},{2,18},{4,20},{6,22},{8,24},{10,26},{12,28},{14,30},{16,0},... | collective-permute-start | bytes 208904 | tf_op jit(solution)/shard_map/ppermute | solution.py:1132
  145.9 7.1 %collective-permute-start.11 = (bf16[4,7,8,256]{3,2,1,0:T(8,128)(2,1)S(1)}, bf16[4,7,8,256]{3,2,1,0:T(8,128)(2,1)S(1)}, u32[]{:S(2)}, u32[]{:S(2)}) collective-permute-start(bf16[4,7,8,256]{3,2,1,0:T(8,128)(2,1)S(1)} %copy-done.23), channel_id=1, source_target_pairs={{0,1},{1,0},{2,3},{3,2},{4,5},{5,4},{6,7},{7,6},{8,9},{9,8},{10,11... | collective-permute-start | bytes 344072 | tf_op jit(solution)/shard_map/ppermute | solution.py:1132
  146.0 9.9 %collective-permute-start.12 = (bf16[4,7,8,256]{3,2,1,0:T(8,128)(2,1)S(1)}, bf16[4,7,8,256]{3,2,1,0:T(8,128)(2,1)S(1)}, u32[]{:S(2)}, u32[]{:S(2)}) collective-permute-start(bf16[4,7,8,256]{3,2,1,0:T(8,128)(2,1)S(1)} %copy-done.22), channel_id=1, source_target_pairs={{0,2},{1,3},{2,0},{3,1},{4,6},{5,7},{6,4},{7,5},{8,10},{9,11},{10,... | collective-permute-start | bytes 344072 | tf_op jit(solution)/shard_map/ppermute | solution.py:1132
  146.6 9.3 %collective-permute-start.13 = (bf16[4,7,8,256]{3,2,1,0:T(8,128)(2,1)S(1)}, bf16[4,7,8,256]{3,2,1,0:T(8,128)(2,1)S(1)}, u32[]{:S(2)}, u32[]{:S(2)}) collective-permute-start(bf16[4,7,8,256]{3,2,1,0:T(8,128)(2,1)S(1)} %copy-done.21), channel_id=1, source_target_pairs={{0,3},{1,2},{2,1},{3,0},{4,7},{5,6},{6,5},{7,4},{8,11},{9,10},{10,... | collective-permute-start | bytes 344072 | tf_op jit(solution)/shard_map/ppermute | solution.py:1132
  151.4 8.2 %collective-permute-start.24 = (bf16[200,256]{1,0:T(8,128)(2,1)S(1)}, bf16[200,256]{1,0:T(8,128)(2,1)S(1)}, u32[]{:S(2)}, u32[]{:S(2)}) collective-permute-start(bf16[200,256]{1,0:T(8,128)(2,1)S(1)} %get-tuple-element.179), channel_id=1, source_target_pairs={{0,8},{2,10},{4,12},{6,14},{8,0},{10,2},{12,4},{14,6},{16,24},{18,... | collective-permute-start | bytes 307208 | tf_op jit(solution)/shard_map/ppermute | solution.py:1132
  151.5 8.9 %collective-permute-start.25 = (bf16[200,256]{1,0:T(8,128)(2,1)S(1)}, bf16[200,256]{1,0:T(8,128)(2,1)S(1)}, u32[]{:S(2)}, u32[]{:S(2)}) collective-permute-start(bf16[200,256]{1,0:T(8,128)(2,1)S(1)} %get-tuple-element.179), channel_id=1, source_target_pairs={{0,16},{2,18},{4,20},{6,22},{8,24},{10,26},{12,28},{14,30},{16,0},... | collective-permute-start | bytes 307208 | tf_op jit(solution)/shard_map/ppermute | solution.py:1132
  153.0 7.5 %collective-permute-start.26 = (bf16[200,256]{1,0:T(8,128)(2,1)S(1)}, bf16[200,256]{1,0:T(8,128)(2,1)S(1)}, u32[]{:S(2)}, u32[]{:S(2)}) collective-permute-start(bf16[200,256]{1,0:T(8,128)(2,1)S(1)} %get-tuple-element.179), channel_id=1, source_target_pairs={{0,24},{2,26},{4,28},{6,30},{8,16},{10,18},{12,20},{14,22},{16,8},... | collective-permute-start | bytes 307208 | tf_op jit(solution)/shard_map/ppermute | solution.py:1132
  160.5 33.9 %all-to-all-start.2 = ((bf16[32,7,8,256]{3,2,1,0:T(8,128)(2,1)}), bf16[32,7,8,256]{3,2,1,0:T(8,128)(2,1)S(1)}, u32[]{:S(2)}, u32[]{:S(2)}) async-start(bf16[32,7,8,256]{3,2,1,0:T(8,128)(2,1)} %split.1), calls=%async_computation.2 | async-start | bytes 1835008 | tf_op jit(solution)/shard_map/all_to_all | solution.py:1442
  164.5 12.4 %collective-permute-start.27 = (bf16[4,200,256]{2,1,0:T(8,128)(2,1)S(1)}, bf16[4,200,256]{2,1,0:T(8,128)(2,1)S(1)}, u32[]{:S(2)}, u32[]{:S(2)}) collective-permute-start(bf16[4,200,256]{2,1,0:T(8,128)(2,1)S(1)} %pad_maximum_fusion.refs_0_), channel_id=1, source_target_pairs={{0,2},{2,0},{4,6},{6,4},{8,10},{10,8},{12,14},{14,12},{16,18},{18,... | collective-permute-start | bytes 1228808 | tf_op jit(solution)/shard_map/ppermute | solution.py:1132
  165.0 26.7 %collective-permute-start.28 = (bf16[4,200,256]{2,1,0:T(8,128)(2,1)S(1)}, bf16[4,200,256]{2,1,0:T(8,128)(2,1)S(1)}, u32[]{:S(2)}, u32[]{:S(2)}) collective-permute-start(bf16[4,200,256]{2,1,0:T(8,128)(2,1)S(1)} %pad_maximum_fusion.refs_0_), channel_id=1, source_target_pairs={{0,4},{2,6},{4,0},{6,2},{8,12},{10,14},{12,8},{14,10},{16,20},{18,... | collective-permute-start | bytes 1228808 | tf_op jit(solution)/shard_map/ppermute | solution.py:1132
  167.1 24.7 %collective-permute-start.29 = (bf16[4,200,256]{2,1,0:T(8,128)(2,1)S(1)}, bf16[4,200,256]{2,1,0:T(8,128)(2,1)S(1)}, u32[]{:S(2)}, u32[]{:S(2)}) collective-permute-start(bf16[4,200,256]{2,1,0:T(8,128)(2,1)S(1)} %pad_maximum_fusion.refs_0_), channel_id=1, source_target_pairs={{0,6},{2,4},{4,2},{6,0},{8,14},{10,12},{12,10},{14,8},{16,22},{18,... | collective-permute-start | bytes 1228808 | tf_op jit(solution)/shard_map/ppermute | solution.py:1132
  168.0 30.6 %collective-permute-start.30 = (bf16[4,200,256]{2,1,0:T(8,128)(2,1)S(1)}, bf16[4,200,256]{2,1,0:T(8,128)(2,1)S(1)}, u32[]{:S(2)}, u32[]{:S(2)}) collective-permute-start(bf16[4,200,256]{2,1,0:T(8,128)(2,1)S(1)} %pad_maximum_fusion.refs_0_), channel_id=1, source_target_pairs={{0,1},{1,0},{2,3},{3,2},{4,5},{5,4},{6,7},{7,6},{8,9},{9,8},{10,11... | collective-permute-start | bytes 1228808 | tf_op jit(solution)/shard_map/ppermute | solution.py:1115
  176.9 21.7 %collective-permute-start.31 = (bf16[4,200,256]{2,1,0:T(8,128)(2,1)S(1)}, bf16[4,200,256]{2,1,0:T(8,128)(2,1)S(1)}, u32[]{:S(2)}, u32[]{:S(2)}) collective-permute-start(bf16[4,200,256]{2,1,0:T(8,128)(2,1)S(1)} %collective-permute-done.27.refs_1_), channel_id=1, source_target_pairs={{0,1},{1,0},{2,3},{3,2},{4,5},{5,4},{6,7},{7,6},{8,9},{9,8},{10,11... | collective-permute-start | bytes 1228808 | tf_op jit(solution)/shard_map/ppermute | solution.py:1115
  191.8 6.8 %collective-permute-start.32 = (bf16[4,200,256]{2,1,0:T(8,128)(2,1)S(1)}, bf16[4,200,256]{2,1,0:T(8,128)(2,1)}, u32[]{:S(2)}, u32[]{:S(2)}) collective-permute-start(bf16[4,200,256]{2,1,0:T(8,128)(2,1)S(1)} %collective-permute-done.28.refs_2_), channel_id=1, source_target_pairs={{0,1},{1,0},{2,3},{3,2},{4,5},{5,4},{6,7},{7,6},{8,9},{9,8},{10,11... | collective-permute-start | bytes 1228808 | tf_op jit(solution)/shard_map/ppermute | solution.py:1115
  191.8 6.8 %collective-permute-start.33 = (bf16[4,200,256]{2,1,0:T(8,128)(2,1)S(1)}, bf16[4,200,256]{2,1,0:T(8,128)(2,1)}, u32[]{:S(2)}, u32[]{:S(2)}) collective-permute-start(bf16[4,200,256]{2,1,0:T(8,128)(2,1)S(1)} %collective-permute-done.29.refs_3_), channel_id=1, source_target_pairs={{0,1},{1,0},{2,3},{3,2},{4,5},{5,4},{6,7},{7,6},{8,9},{9,8},{10,11... | collective-permute-start | bytes 1228808 | tf_op jit(solution)/shard_map/ppermute | solution.py:1115
  (40 other events, 291.9 us)

commit v4 on v3

--- a/solution.py
+++ b/solution.py
@@ -20,7 +20,6 @@
 EPS = 1e-05
 BF = jnp.bfloat16
 F32 = jnp.float32
-VMEM_BYTES = 60 * 1024 * 1024
 
 
 def dot_nn(a, b):
@@ -49,16 +48,9 @@
 
 
 def gelu_parts(values):
-    size = jnp.abs(values) * (0.5**0.5)
-    fall = jnp.exp(-(size * size))
-    step = 1.0 / (1.0 + 0.3275911 * size)
-    series = step * (
-        0.254829592
-        + step * (-0.284496736 + step * (1.421413741 + step * (-1.453152027 + step * 1.061405429)))
-    )
-    tail = 0.5 * series * fall
-    chance = jnp.where(values >= 0.0, 1.0 - tail, tail)
-    return chance, fall * 0.3989422804014327
+    chance = 0.5 + 0.5 * lax.erf(values * (0.5**0.5))
+    density = jnp.exp2(values * values * (-0.5 * LOG2E)) * 0.3989422804014327
+    return chance, density
 
 
 def row_sums(values):
@@ -245,6 +237,7 @@
 
 
 def attention_backward(
+    ready,
     block,
     win_in,
     chance_in,
@@ -255,6 +248,7 @@
 ):
     width = stripe_delta.shape[1]
     for direction in range(2):
+        ready(direction)
         across = direction == 0
         lane = direction * HALF
 
@@ -409,8 +403,10 @@
     hidden_units = expand_w.shape[2]
     bundle = Bundle(place_ref, keep_out, away_out, len(spots), lambda chunk: spots[chunk])
     vec_out[...] = jnp.zeros(vec_out.shape, F32)
+    moves.fetch(entry_w)
     load_tiles(place_ref, (mixed_a, mixed_b, mixed_c, mixed_d), hidden)
     moves.need(entry_w)
+    moves.fetch(exit_w, expand_w, shrink_w, cot_a, cot_b, cot_c, cot_d)
 
     for block in range(2):
         win_out, chance_out, stripe_out = (
@@ -563,10 +559,20 @@
     )
     vec_out[...] = jnp.zeros(vec_out.shape, F32)
     conv_out[...] = jnp.zeros(conv_out.shape, F32)
+    moves.fetch(grad_in, exit_w)
+    moves.fetch(win1, chance1, part=0)
     moves.need(grad_in, exit_w)
+    moves.fetch(win1, chance1, part=1)
     delta_rows(1, place_ref, mask_ref, exit_w, grad_in, stripe_delta, branch_delta, vec_out, 0)
-    moves.need(win1, chance1)
-    attention_backward(1, win1, chance1, conv_k, stripe_delta, wide, conv_out)
+
+    def ready(direction):
+        moves.need(win1, chance1, part=direction)
+        if direction == 0:
+            moves.fetch(hidden1, entry_w, stripe1)
+        else:
+            moves.fetch(mid0, shrink_w, slope0, expand_w, active0, stripe0)
+
+    attention_backward(ready, 1, win1, chance1, conv_k, stripe_delta, wide, conv_out)
 
     def emit(t, rows, values):
         grad[rows, :] = values
@@ -652,8 +658,17 @@
     )
     vec3[...] = jnp.zeros(vec3.shape, F32)
     conv3[...] = jnp.zeros(conv3.shape, F32)
-    moves.need(stripe_delta, win0, chance0)
-    attention_backward(0, win0, chance0, conv_k, stripe_delta, wide, conv3)
+    moves.fetch(stripe_delta)
+    moves.fetch(win0, chance0, part=0)
+    moves.need(stripe_delta)
+    moves.fetch(win0, chance0, part=1)
+
+    def ready(direction):
+        moves.need(win0, chance0, part=direction)
+        if direction == 0:
+            moves.fetch(mixed_a, mixed_b, mixed_c, mixed_d, entry_w, grad_in)
+
+    attention_backward(ready, 0, win0, chance0, conv_k, stripe_delta, wide, conv3)
 
     def emit(t, rows, values):
         store_tile(place_ref, (out_a, out_b, out_c, out_d), t, values)
@@ -1009,35 +1024,65 @@
 
 
 ANYWHERE = pl.BlockSpec(memory_space=pl.ANY)
+FAR = pl.BlockSpec(memory_space=pltpu.HBM)
+
+
+def far(values):
+    return pltpu.with_memory_space_constraint(values, pltpu.HBM)
 
 
 class Moves:
     def __init__(self, fetched, sent):
         self.fetched, self.sent = dict(fetched), dict(sent)
-        self.waited, self.started = [], []
-        for copy in self.fetched.values():
-            copy.start()
-
-    def need(self, *refs):
+        self.waited, self.started = set(), set()
+
+    def copies(self, ref, part):
+        copies = self.fetched[id(ref)]
+        return [
+            ((id(ref), i), copy)
+            for i, copy in enumerate(copies)
+            if part is None or len(copies) == 1 or i == part
+        ]
+
+    def fetch(self, *refs, part=None):
         for ref in refs:
-            if id(ref) in self.fetched and id(ref) not in self.waited:
-                self.fetched[id(ref)].wait()
-                self.waited.append(id(ref))
+            for key, copy in self.copies(ref, part):
+                if key not in self.started:
+                    copy.start()
+                    self.started.add(key)
+
+    def need(self, *refs, part=None):
+        self.fetch(*refs, part=part)
+        for ref in refs:
+            for key, copy in self.copies(ref, part):
+                if key not in self.waited:
+                    copy.wait()
+                    self.waited.add(key)
 
     def send(self, *refs):
         for ref in refs:
             self.sent[id(ref)].start()
-            self.started.append(id(ref))
+            self.started.add(id(ref))
 
     def finish(self):
-        for key, copy in self.fetched.items():
-            if key not in self.waited:
-                copy.wait()
+        for key, copies in self.fetched.items():
+            for i, copy in enumerate(copies):
+                if (key, i) not in self.started:
+                    copy.start()
+                if (key, i) not in self.waited:
+                    copy.wait()
         for key, copy in self.sent.items():
             if key not in self.started:
                 copy.start()
         for copy in self.sent.values():
             copy.wait()
+
+
+def halves(ref):
+    if ref.shape[-2] != WIN:
+        return [pl.ds(0, ref.shape[0])]
+    count = ref.shape[0] // 2
+    return [pl.ds(0, count), pl.ds(count, count)]
 
 
 def run(
@@ -1051,6 +1096,8 @@
     after=(),
     scalar_outs=(),
     lazy=None,
+    vmem=16,
+    near=((), ()),
 ):
     outs = list(outs)
     first_in, first_out = (len(arrays), len(outs)) if lazy is None else lazy
@@ -1064,7 +1111,7 @@
     if lazy is not None:
         scratch_shapes += [pltpu.VMEM(a.shape, a.dtype) for a in late]
         scratch_shapes += [pltpu.VMEM(*out) for out in outs[first_out:]]
-        scratch_shapes += [pltpu.SemaphoreType.DMA((n_late,)), pltpu.SemaphoreType.DMA((n_sent,))]
+        scratch_shapes += [pltpu.SemaphoreType.DMA((n_late, 2)), pltpu.SemaphoreType.DMA((n_sent,))]
 
     def body(*refs):
         given, refs = refs[:n_in], refs[n_in:]
@@ -1079,7 +1126,13 @@
         fetch_sem, send_sem = refs[n_late + n_sent :]
         moves = Moves(
             [
-                (id(buffer), pltpu.make_async_copy(source, buffer, fetch_sem.at[i]))
+                (
+                    id(buffer),
+                    [
+                        pltpu.make_async_copy(source.at[part], buffer.at[part], fetch_sem.at[i, j])
+                        for j, part in enumerate(halves(buffer))
+                    ],
+                )
                 for i, (source, buffer) in enumerate(zip(sources, buffers))
             ],
             [
@@ -1090,17 +1143,29 @@
         kernel(moves, *given, *buffers, *results, *leaving, *own)
         moves.finish()
 
-    out_shape = [jax.ShapeDtypeStruct(shape, dtype) for shape, dtype in tuple(scalar_outs) + tuple(outs)]
+    out_shape = [jax.ShapeDtypeStruct(shape, dtype) for shape, dtype in scalar_outs] + [
+        pltpu.HBM(shape, dtype)
+        if lazy is not None and i not in near[1]
+        else jax.ShapeDtypeStruct(shape, dtype)
+        for i, (shape, dtype) in enumerate(outs)
+    ]
+    late = [
+        a if i in near[0] else far(a)
+        for i, a in enumerate(late, first_in)
+    ]
     moved = sum(a.size * a.dtype.itemsize for a in arrays)
     return pl.pallas_call(
         body,
         out_shape=out_shape,
         in_specs=[SMEM] * len(scalars)
         + [VMEM] * len(eager)
-        + [ANYWHERE] * (n_late + len(after)),
-        out_specs=[SMEM] * len(scalar_outs) + [VMEM] * first_out + [ANYWHERE] * n_sent,
+        + [ANYWHERE if i in near[0] else FAR for i in range(first_in, len(arrays))]
+        + [ANYWHERE] * len(after),
+        out_specs=[SMEM] * len(scalar_outs)
+        + [VMEM] * first_out
+        + [ANYWHERE if i in near[1] else FAR for i in range(first_out, len(outs))],
         scratch_shapes=scratch_shapes,
-        compiler_params=pltpu.CompilerParams(vmem_limit_bytes=VMEM_BYTES),
+        compiler_params=pltpu.CompilerParams(vmem_limit_bytes=vmem * 1024 * 1024),
         cost_estimate=pl.CostEstimate(flops=flops, bytes_accessed=moved, transcendentals=0),
         name=name,
     )(*scalars, *eager, *late, *after)
@@ -1233,11 +1298,12 @@
         [((slots, TILE, 8, width), BF), ((images_here, TILE, 8, width), BF)],
         [flat, (pltpu.SMEM((groups,), jnp.int32), None)],
         name="pick",
+        vmem=60,
         scalar_outs=(((slots + 8,), jnp.int32), ((2 * images_here,), jnp.int32)),
     )
     arrived = lax.all_to_all(outgoing, "dp", split_axis=0, concat_axis=0, tiled=True)
     cot = deal(
-        run(deal_kernel, [place], [cotangent.transpose(1, 2, 0, 3)], [quad] * 4, [flat], name="deal")
+        run(deal_kernel, [place], [cotangent.transpose(1, 2, 0, 3)], [quad] * 4, [flat], name="deal", vmem=60)
     )
     mixed = deal(
         run(
@@ -1317,6 +1383,8 @@
         ],
         flops=10 * rows * width * width * 120,
         name="first",
+        vmem=46,
+        near=((16, 17, 18, 19), (5, 6)),
         lazy=(12, 1),
     )
     sent1 = shards(added(keep1, swap(away1, "col")), ranks)
@@ -1361,6 +1429,8 @@
         ],
         flops=6 * rows * width * width * 120,
         name="second",
+        vmem=42,
+        near=((), (4, 5)),
         after=[sent1],
         lazy=(3, 2),
     )
@@ -1407,6 +1477,8 @@
         ],
         flops=3 * rows * width * width * 120,
         name="third",
+        vmem=36,
+        near=((9, 10, 11, 12), range(6)),
         after=parts2,
         lazy=(6, 0),
     )
@@ -1419,9 +1491,13 @@
         [((slots, TILE, 8, width), BF)],
         name="split",
     )
+    (activations,) = run(
+        lay_kernel, [place], [far(a) for a in act], [((TILE, TILE, images_here, width), BF)], [flat], name="lay"
+    )
     mine1 = jnp.sum(pieces1.astype(F32), axis=0).astype(BF)
     mine2 = scatter_sum(moved2)
-    mine3 = scatter_sum(scatter_move(first_parts(keep3, away3), ranks, steps[0]))
+    moved3 = scatter_move(first_parts(keep3, away3), ranks, steps[0])
+    mine3 = scatter_sum(gate(moved3, [mine1]))
     cut = mine2.shape[0] * 4 // ranks
     lot = mine3.shape[0] * 4 // ranks
     joint = jnp.concatenate(
@@ -1440,6 +1516,7 @@
     joint = shards(joint, ranks // 4)
     (parted,) = gate([parted], [joint])
     back = lax.all_to_all(parted, "dp", split_axis=0, concat_axis=0, tiled=True)
+    (back,) = gate([back], [activations])
     (input_gradient,) = run(
         join_kernel,
         [place, index, corners, ratios],
@@ -1449,11 +1526,8 @@
         name="join",
     )
     full = [joint] + [across(joint, RANKS, ranks, d) for d in (1, 2, 3)]
+    full[2:] = gate(full[2:], [input_gradient])
     full += [swap(piece, "col") for piece in full]
-    full = gate(full, [input_gradient])
-    (activations,) = run(
-        lay_kernel, [place], act, [((TILE, TILE, images_here, width), BF)], [flat], name="lay"
-    )
     shapes = [
         (2, 2, width),
         (2, 2, width),
@@ -1481,7 +1555,7 @@
             ]
             + [pltpu.VMEM(shape, F32) for shape in shapes]
             + [pltpu.SemaphoreType.DMA((12,))],
-            compiler_params=pltpu.CompilerParams(vmem_limit_bytes=VMEM_BYTES),
+            compiler_params=pltpu.CompilerParams(vmem_limit_bytes=24 * 1024 * 1024),
             name="unpack",
         )(place, *full)
     )

time: 206 us -> 186 us (0.903)
  Pallas kernels: 86.7 us -> 77.6 us
  local copies, waits for them, and re-layouts: 5.71 us -> 1.61 us
  other arithmetic: 6.27 us -> 2.62 us
  waiting for transfers between devices: 61.2 us -> 58.5 us
    ppermute x27, waiting for transfers between devices: 45 us -> 32.7 us  [across(): return lax.ppermute(values, axes, [(i, i ^ mask) for i in range(size)])]
    pallas_call x9, Pallas kernels: 81.2 us -> 71.9 us  [run(): pl.pallas_call(body, out_shape=out_shape, in_specs=[SMEM] * len(scalars)...]
    all_to_all x1, waiting for transfers between devices: 0.01 us -> 7.89 us  [local(): back = lax.all_to_all(parted, 'dp', split_axis=0, concat_axis=0, tiled=True)]
    unnamed x54 -> x44, local copies, waits for them, and re-layouts: 5.02 us -> 1.01 us
    convert_element_type x3, other arithmetic: 5.04 us -> 1.21 us  [added(): return (values.astype(F32) + others.astype(F32)).astype(BF)]
  transfers between devices with their start and end apart: 37 -> 37, of which waited for: 15 -> 17; matrix products, arithmetic and copies ran while one was open for 1% -> 1% of each run, Pallas kernels for 21% -> 21%
where the time goes in v4:
time: 186 us
  Pallas kernels  77.6 us (42%)
  waiting for transfers between devices  58.5 us (31%)
  starting transfers between devices  44.1 us (24%)
  other arithmetic  2.62 us (1%)
    pallas_call x9, Pallas kernels, run(): pl.pallas_call(body, out_shape=out_shape, in_specs=[SMEM] * len(scalars)...  71.9 us
    ppermute x27, waiting for transfers between devices, across(): return lax.ppermute(values, axes, [(i, i ^ mask) for i in range(size)])  32.7 us
    ppermute x27, starting transfers between devices, across(): return lax.ppermute(values, axes, [(i, i ^ mask) for i in range(size)])  27 us
    all_to_all x1, waiting for transfers between devices, local(): lax.all_to_all(outgoing, 'dp', split_axis=0, concat_axis=0, tiled=True)  12.5 us
    all_to_all x1, waiting for transfers between devices, local(): back = lax.all_to_all(parted, 'dp', split_axis=0, concat_axis=0, tiled=True)  7.89 us
    all_to_all x1, starting transfers between devices, local(): lax.all_to_all(outgoing, 'dp', split_axis=0, concat_axis=0, tiled=True)  7.42 us
    pallas_call x1, Pallas kernels, local(): pl.pallas_call(functools.partial(unpack_kernel, ranks, counts), out_shape...  5.7 us
    ppermute x7, waiting for transfers between devices, swap(): return lax.ppermute(values, axis, [(0, 1), (1, 0)])  5.4 us
  transfers between devices with their start and end apart: 37, of which 17 were waited for; matrix products, arithmetic and copies ran while one was open for 1% of the time, Pallas kernels for 21%

profile of v4, /device:TPU:0, one launch (start us, length us, event | category | flops | bytes accessed | tf_op | source)
XLA Modules:
  0.0 185.8 jit_solution(15823340143626960808)
XLA Ops:
  1.3 3.9 %pick.1 = (s32[40]{0:T(128)}, s32[32]{0:T(128)}, bf16[32,7,8,256]{3,2,1,0:T(8,128)(2,1)}, bf16[16,7,8,256]{3,2,1,0:T(8,128)(2,1)}) custom-call(s32[7]{0:T(128)} %stack.46.refs_0_.place_ref, s32[128]{0:T(128)} %refs_1_.2, s32[128]{0:T(128)} %refs_2_.3, bf16[7,7,16,256]{3,2,1,0:T(8,128)(2,1)} %bitcast.47), custom_call_target="tpu_custom_call" | custom-call | bytes 401408 | tf_op jit(solution)/shard_map/pick/pallas_call | solution.py:1157
  5.3 7.4 %all-to-all-start = ((bf16[32,7,8,256]{3,2,1,0:T(8,128)(2,1)}), bf16[32,7,8,256]{3,2,1,0:T(8,128)(2,1)S(1)}, u32[]{:S(2)}, u32[]{:S(2)}) async-start(bf16[32,7,8,256]{3,2,1,0:T(8,128)(2,1)} %get-tuple-element.91), calls=%async_computation | async-start | bytes 1835008 | tf_op jit(solution)/shard_map/all_to_all | solution.py:1304
  12.8 2.7 %deal.1 = (bf16[4,7,8,256]{3,2,1,0:T(8,128)(2,1)}, bf16[4,7,8,256]{3,2,1,0:T(8,128)(2,1)}, bf16[4,7,8,256]{3,2,1,0:T(8,128)(2,1)}, bf16[4,7,8,256]{3,2,1,0:T(8,128)(2,1)}) custom-call(s32[7]{0:T(128)} %stack.46.refs_0_.place_ref, bf16[7,7,16,256]{3,2,1,0:T(8,128)(2,1)} %bitcast.48), custom_call_target="tpu_custom_call" | custom-call | bytes 401408 | tf_op jit(solution)/shard_map/deal/pallas_call | solution.py:1157
  17.3 4.3 %collective-permute-done.1.refs_8_.refs_20_ = bf16[4,7,8,256]{3,2,1,0:T(8,128)(2,1)S(1)} collective-permute-done((bf16[4,7,8,256]{3,2,1,0:T(8,128)(2,1)}, bf16[4,7,8,256]{3,2,1,0:T(8,128)(2,1)S(1)}, u32[]{:S(2)}, u32[]{:S(2)}) %collective-permute-start.1) | collective-permute-done | bytes 114720 | tf_op jit(solution)/shard_map/ppermute | solution.py:1197
  23.2 12.5 %all-to-all-done.refs_4_ = bf16[32,7,8,256]{3,2,1,0:T(8,128)(2,1)S(1)} async-done(((bf16[32,7,8,256]{3,2,1,0:T(8,128)(2,1)}), bf16[32,7,8,256]{3,2,1,0:T(8,128)(2,1)S(1)}, u32[]{:S(2)}, u32[]{:S(2)}) %all-to-all-start) | async-done | bytes 917536 | tf_op jit(solution)/shard_map/all_to_all | solution.py:1304
  39.9 4.1 %collective-permute-done.4.refs_4_.refs_12_ = bf16[4,7,8,256]{3,2,1,0:T(8,128)(2,1)S(1)} collective-permute-done((bf16[4,7,8,256]{3,2,1,0:T(8,128)(2,1)S(1)}, bf16[4,7,8,256]{3,2,1,0:T(8,128)(2,1)S(1)}, u32[]{:S(2)}, u32[]{:S(2)}) %collective-permute-start.4) | collective-permute-done | bytes 114720 | tf_op jit(solution)/shard_map/ppermute | solution.py:1197
  45.6 27.8 %first.1 = (f32[7,8,256]{2,1,0:T(8,128)}, bf16[4,7,8,256]{3,2,1,0:T(8,128)(2,1)}, bf16[4,7,8,256]{3,2,1,0:T(8,128)(2,1)}, bf16[4,7,8,256]{3,2,1,0:T(8,128)(2,1)}...) custom-call(s32[7]{0:T(128)S(1)} %copy-done.3, ...), custom_call_target="tpu_custom_call" | custom-call | flops 70464307200 | bytes 4108288 | tf_op jit(solution)/shard_map/first/pallas_call | solution.py:1157
  76.6 4.6 %all-to-all-start.1 = ((bf16[16,64,256]{2,1,0:T(8,128)(2,1)}), bf16[16,64,256]{2,1,0:T(8,128)(2,1)S(1)}, u32[]{:S(2)}, u32[]{:S(2)}) async-start(bf16[16,64,256]{2,1,0:T(8,128)(2,1)} %bitcast.12.refs_18_), calls=%async_computation.1 | async-start | bytes 1048576 | tf_op jit(solution)/shard_map/all_to_all | solution.py:1391
  81.1 18.2 %second.1 = (f32[15,8,256]{2,1,0:T(8,128)}, f32[9,8,256]{2,1,0:T(8,128)}, f32[896,256]{1,0:T(8,128)}, f32[896,256]{1,0:T(8,128)}, bf16[1664,256]{1,0:T(8,128)(2,1)S(1)}, /*index=5*/bf16[1664,256]{1,0:T(8,128)(2,1)S(1)}) custom-call(s32[7]{0:T(128)S(1)} %copy-done.3, s32[4,16]{1,0:T(4,128)S(1)} %bitcast.41, f32[2,2,256]{2,1,0:T(2,128)S(1)} %copy-done.11, ...), custom_call_target="tpu_custom_call" | custom-call | flops 42278584320 | bytes 13723648 | tf_op jit(solution)/shard_map/second/pallas_call | solution.py:1157
  99.8 2.2 %collective-permute-done.10 = bf16[1664,256]{1,0:T(8,128)(2,1)S(1)} collective-permute-done((bf16[1664,256]{1,0:T(8,128)(2,1)S(1)}, bf16[1664,256]{1,0:T(8,128)(2,1)S(1)}, u32[]{:S(2)}, u32[]{:S(2)}) %collective-permute-start.10) | collective-permute-done | bytes 852000 | tf_op jit(solution)/shard_map/ppermute | solution.py:1180
  102.1 2.0 %collective-permute-start.14 = (bf16[416,256]{1,0:T(8,128)(2,1)S(1)}, bf16[416,256]{1,0:T(8,128)(2,1)S(1)}, u32[]{:S(2)}, u32[]{:S(2)}) collective-permute-start(bf16[416,256]{1,0:T(8,128)(2,1)S(1)} %get-tuple-element.168.refs_17_), channel_id=1, source_target_pairs={{0,2},{2,0},{4,6},{6,4},{8,10},{10,8},{12,14},{14,12},{16,18},{18,... | collective-permute-start | bytes 638984 | tf_op jit(solution)/shard_map/ppermute | solution.py:1197
  105.7 11.8 %third.1 = (bf16[4,7,8,256]{3,2,1,0:T(8,128)(2,1)S(1)}, bf16[4,7,8,256]{3,2,1,0:T(8,128)(2,1)S(1)}, bf16[4,7,8,256]{3,2,1,0:T(8,128)(2,1)S(1)}, bf16[4,7,8,256]{...) custom-call(s32[7]{0:T(128)S(1)} %copy-done.3, f32[2,2,256]{2,1,0:T(2,128)S(1)} %copy-done.11, ...), custom_call_target="tpu_custom_call" | custom-call | flops 21139292160 | bytes 6572032 | tf_op jit(solution)/shard_map/third/pallas_call | solution.py:1157
  125.4 2.4 %collective-permute-done.20 = bf16[128,256]{1,0:T(8,128)(2,1)S(1)} collective-permute-done((bf16[128,256]{1,0:T(8,128)(2,1)S(1)}, bf16[128,256]{1,0:T(8,128)(2,1)S(1)}, u32[]{:S(2)}, u32[]{:S(2)}) %collective-permute-start.20) | collective-permute-done | bytes 65568 | tf_op jit(solution)/shard_map/ppermute | solution.py:1197
  129.4 2.4 %collective-permute-start.22 = (bf16[136,256]{1,0:T(8,128)(2,1)S(1)}, bf16[136,256]{1,0:T(8,128)(2,1)S(1)}, u32[]{:S(2)}, u32[]{:S(2)}) collective-permute-start(bf16[136,256]{1,0:T(8,128)(2,1)S(1)} %get-tuple-element.175), channel_id=1, source_target_pairs={{0,16},{2,18},{4,20},{6,22},{8,24},{10,26},{12,28},{14,30},{16,0},... | collective-permute-start | bytes 208904 | tf_op jit(solution)/shard_map/ppermute | solution.py:1197
  139.5 2.9 %collective-permute-start.26 = (bf16[200,256]{1,0:T(8,128)(2,1)S(1)}, bf16[200,256]{1,0:T(8,128)(2,1)S(1)}, u32[]{:S(2)}, u32[]{:S(2)}) collective-permute-start(bf16[200,256]{1,0:T(8,128)(2,1)S(1)} %get-tuple-element.178), channel_id=1, source_target_pairs={{0,24},{2,26},{4,28},{6,30},{8,16},{10,18},{12,20},{14,22},{16,8},... | collective-permute-start | bytes 307208 | tf_op jit(solution)/shard_map/ppermute | solution.py:1197
  144.4 2.4 %collective-permute-done.25 = bf16[200,256]{1,0:T(8,128)(2,1)S(1)} collective-permute-done((bf16[200,256]{1,0:T(8,128)(2,1)S(1)}, bf16[200,256]{1,0:T(8,128)(2,1)S(1)}, u32[]{:S(2)}, u32[]{:S(2)}) %collective-permute-start.25) | collective-permute-done | bytes 102432 | tf_op jit(solution)/shard_map/ppermute | solution.py:1197
  146.9 3.9 %all-to-all-start.2 = ((bf16[32,7,8,256]{3,2,1,0:T(8,128)(2,1)}), bf16[32,7,8,256]{3,2,1,0:T(8,128)(2,1)S(1)}, u32[]{:S(2)}, u32[]{:S(2)}) async-start(bf16[32,7,8,256]{3,2,1,0:T(8,128)(2,1)} %split.1), calls=%async_computation.2 | async-start | bytes 1835008 | tf_op jit(solution)/shard_map/all_to_all | solution.py:1518
  151.3 2.0 %collective-permute-start.28 = (bf16[4,200,256]{2,1,0:T(8,128)(2,1)S(1)}, bf16[4,200,256]{2,1,0:T(8,128)(2,1)S(1)}, u32[]{:S(2)}, u32[]{:S(2)}) collective-permute-start(bf16[4,200,256]{2,1,0:T(8,128)(2,1)S(1)} %pad_maximum_fusion.refs_0_), channel_id=1, source_target_pairs={{0,4},{2,6},{4,0},{6,2},{8,12},{10,14},{12,8},{14,10},{16,20},{18,... | collective-permute-start | bytes 1228808 | tf_op jit(solution)/shard_map/ppermute | solution.py:1197
  154.2 2.1 %lay.1 = bf16[7,7,16,256]{3,2,1,0:T(8,128)(2,1)} custom-call(s32[7]{0:T(128)S(1)} %copy-done.3, bf16[4,7,8,256]{3,2,1,0:T(8,128)(2,1)} %get-tuple-element.120.refs_1_, bf16[4,7,8,256]{3,2,1,0:T(8,128)(2,1)} %copy-done.20, bf16[4,7,8,256]{3,2,1,0:T(8,128)(2,1)} %copy-done.21, bf16[4,7,8,256]{3,2,1,0:T(8,128)(2,1)} %collective-permute-done.9.refs_4_), custom_call_target="tpu_custom_call" | custom-call | bytes 458752 | tf_op jit(solution)/shard_map/lay/pallas_call | solution.py:1157
  156.3 6.8 %collective-permute-done.27.refs_1_ = bf16[4,200,256]{2,1,0:T(8,128)(2,1)S(1)} collective-permute-done((bf16[4,200,256]{2,1,0:T(8,128)(2,1)S(1)}, bf16[4,200,256]{2,1,0:T(8,128)(2,1)S(1)}, u32[]{:S(2)}, u32[]{:S(2)}) %collective-permute-start.27) | collective-permute-done | bytes 409632 | tf_op jit(solution)/shard_map/ppermute | solution.py:1197
  163.1 7.9 %all-to-all-done.2.refs_8_ = bf16[32,7,8,256]{3,2,1,0:T(8,128)(2,1)S(1)} async-done(((bf16[32,7,8,256]{3,2,1,0:T(8,128)(2,1)}), bf16[32,7,8,256]{3,2,1,0:T(8,128)(2,1)S(1)}, u32[]{:S(2)}, u32[]{:S(2)}) %all-to-all-start.2) | async-done | bytes 917536 | tf_op jit(solution)/shard_map/all_to_all | solution.py:1518
  171.0 2.4 %join.1 = f32[7,7,16,256]{3,2,1,0:T(8,128)} custom-call(s32[7]{0:T(128)S(1)} %copy-done.3, s32[40]{0:T(128)S(1)} %copy-done.7, s32[4,16]{1,0:T(4,128)S(1)} %bitcast.36, f32[16]{0:T(128)S(1)} %copy-done.5, bf16[4,7,8,256]{3,2,1,0:T(8,128)(2,1)S(1)} %get-tuple-element.134.refs_4_, bf16[4,7,8,256]{3,2,1,0:T(8,128)(2,1)S(1)} %collective-permute-done.11.refs_5_, ...), custom_call_target="tpu_custom_call" | custom-call | bytes 1376256 | tf_op jit(solution)/shard_map/join/pallas_call | solution.py:1157
  173.4 4.1 %collective-permute-done.28.refs_2_ = bf16[4,200,256]{2,1,0:T(8,128)(2,1)S(1)} collective-permute-done((bf16[4,200,256]{2,1,0:T(8,128)(2,1)S(1)}, bf16[4,200,256]{2,1,0:T(8,128)(2,1)S(1)}, u32[]{:S(2)}, u32[]{:S(2)}) %collective-permute-start.28) | collective-permute-done | bytes 409632 | tf_op jit(solution)/shard_map/ppermute | solution.py:1197
  179.9 5.7 %unpack.1 = (f32[2,2,256]{2,1,0:T(2,128)}, f32[2,2,256]{2,1,0:T(2,128)}, f32[2,256,768]{2,1,0:T(8,128)}, f32[2,512]{1,0:T(2,128)}, f32[3,3,2,256]{3,2,1,0:T(2,12...) custom-call(s32[7]{0:T(128)S(1)} %copy-done.3, ...), custom_call_target="tpu_custom_call" | custom-call | tf_op jit(solution)/shard_map/unpack/pallas_call | solution.py:1546
  (115 shorter events, 38.1 us)
Async XLA Ops:
  5.3 30.5 %all-to-all-start = ((bf16[32,7,8,256]{3,2,1,0:T(8,128)(2,1)}), bf16[32,7,8,256]{3,2,1,0:T(8,128)(2,1)S(1)}, u32[]{:S(2)}, u32[]{:S(2)}) async-start(bf16[32,7,8,256]{3,2,1,0:T(8,128)(2,1)} %get-tuple-element.91), calls=%async_computation | async-start | bytes 1835008 | tf_op jit(solution)/shard_map/all_to_all | solution.py:1304
  15.4 6.2 %collective-permute-start.1 = (bf16[4,7,8,256]{3,2,1,0:T(8,128)(2,1)}, bf16[4,7,8,256]{3,2,1,0:T(8,128)(2,1)S(1)}, u32[]{:S(2)}, u32[]{:S(2)}) collective-permute-start(bf16[4,7,8,256]{3,2,1,0:T(8,128)(2,1)} %get-tuple-element.95), channel_id=1, source_target_pairs={{0,2},{1,3},{2,0},{3,1},{4,6},{5,7},{6,4},{7,5},{8,10},{9,11},{10,... | collective-permute-start | bytes 344072 | tf_op jit(solution)/shard_map/ppermute | solution.py:1197
  16.9 6.3 %collective-permute-start.2 = (bf16[4,7,8,256]{3,2,1,0:T(8,128)(2,1)}, bf16[4,7,8,256]{3,2,1,0:T(8,128)(2,1)S(1)}, u32[]{:S(2)}, u32[]{:S(2)}) collective-permute-start(bf16[4,7,8,256]{3,2,1,0:T(8,128)(2,1)} %get-tuple-element.96), channel_id=1, source_target_pairs={{0,3},{1,2},{2,1},{3,0},{4,7},{5,6},{6,5},{7,4},{8,11},{9,10},{10,... | collective-permute-start | bytes 344072 | tf_op jit(solution)/shard_map/ppermute | solution.py:1197
  73.8 25.6 %collective-permute-start.7 = (bf16[4,7,8,256]{3,2,1,0:T(8,128)(2,1)}, bf16[4,7,8,256]{3,2,1,0:T(8,128)(2,1)S(1)}, u32[]{:S(2)}, u32[]{:S(2)}) collective-permute-start(bf16[4,7,8,256]{3,2,1,0:T(8,128)(2,1)} %get-tuple-element.117), channel_id=1, source_target_pairs={{0,1},{1,0},{2,3},{3,2},{4,5},{5,4},{6,7},{7,6},{8,9},{9,8},{10,11... | collective-permute-start | bytes 344072 | tf_op jit(solution)/shard_map/ppermute | solution.py:1197
  74.0 25.4 %collective-permute-start.8 = (bf16[4,7,8,256]{3,2,1,0:T(8,128)(2,1)}, bf16[4,7,8,256]{3,2,1,0:T(8,128)(2,1)S(1)}, u32[]{:S(2)}, u32[]{:S(2)}) collective-permute-start(bf16[4,7,8,256]{3,2,1,0:T(8,128)(2,1)} %get-tuple-element.118), channel_id=1, source_target_pairs={{0,2},{1,3},{2,0},{3,1},{4,6},{5,7},{6,4},{7,5},{8,10},{9,11},{10,... | collective-permute-start | bytes 344072 | tf_op jit(solution)/shard_map/ppermute | solution.py:1197
  75.5 24.0 %collective-permute-start.9 = (bf16[4,7,8,256]{3,2,1,0:T(8,128)(2,1)}, bf16[4,7,8,256]{3,2,1,0:T(8,128)(2,1)}, u32[]{:S(2)}, u32[]{:S(2)}) collective-permute-start(bf16[4,7,8,256]{3,2,1,0:T(8,128)(2,1)} %get-tuple-element.119), channel_id=1, source_target_pairs={{0,3},{1,2},{2,1},{3,0},{4,7},{5,6},{6,5},{7,4},{8,11},{9,10},{10,... | collective-permute-start | bytes 344072 | tf_op jit(solution)/shard_map/ppermute | solution.py:1197
  76.6 22.9 %all-to-all-start.1 = ((bf16[16,64,256]{2,1,0:T(8,128)(2,1)}), bf16[16,64,256]{2,1,0:T(8,128)(2,1)S(1)}, u32[]{:S(2)}, u32[]{:S(2)}) async-start(bf16[16,64,256]{2,1,0:T(8,128)(2,1)} %bitcast.12.refs_18_), calls=%async_computation.1 | async-start | bytes 1048576 | tf_op jit(solution)/shard_map/all_to_all | solution.py:1391
  102.1 15.4 %collective-permute-start.14 = (bf16[416,256]{1,0:T(8,128)(2,1)S(1)}, bf16[416,256]{1,0:T(8,128)(2,1)S(1)}, u32[]{:S(2)}, u32[]{:S(2)}) collective-permute-start(bf16[416,256]{1,0:T(8,128)(2,1)S(1)} %get-tuple-element.168.refs_17_), channel_id=1, source_target_pairs={{0,2},{2,0},{4,6},{6,4},{8,10},{10,8},{12,14},{14,12},{16,18},{18,... | collective-permute-start | bytes 638984 | tf_op jit(solution)/shard_map/ppermute | solution.py:1197
  104.1 13.4 %collective-permute-start.15 = (bf16[416,256]{1,0:T(8,128)(2,1)S(1)}, bf16[416,256]{1,0:T(8,128)(2,1)}, u32[]{:S(2)}, u32[]{:S(2)}) collective-permute-start(bf16[416,256]{1,0:T(8,128)(2,1)S(1)} %get-tuple-element.167.refs_18_), channel_id=1, source_target_pairs={{0,4},{2,6},{4,0},{6,2},{8,12},{10,14},{12,8},{14,10},{16,20},{18,... | collective-permute-start | bytes 638984 | tf_op jit(solution)/shard_map/ppermute | solution.py:1197
  105.5 12.0 %collective-permute-start.16 = (bf16[416,256]{1,0:T(8,128)(2,1)S(1)}, bf16[416,256]{1,0:T(8,128)(2,1)}, u32[]{:S(2)}, u32[]{:S(2)}) collective-permute-start(bf16[416,256]{1,0:T(8,128)(2,1)S(1)} %get-tuple-element.166.refs_19_), channel_id=1, source_target_pairs={{0,6},{2,4},{4,2},{6,0},{8,14},{10,12},{12,10},{14,8},{16,22},{18,... | collective-permute-start | bytes 638984 | tf_op jit(solution)/shard_map/ppermute | solution.py:1197
  129.4 6.7 %collective-permute-start.22 = (bf16[136,256]{1,0:T(8,128)(2,1)S(1)}, bf16[136,256]{1,0:T(8,128)(2,1)S(1)}, u32[]{:S(2)}, u32[]{:S(2)}) collective-permute-start(bf16[136,256]{1,0:T(8,128)(2,1)S(1)} %get-tuple-element.175), channel_id=1, source_target_pairs={{0,16},{2,18},{4,20},{6,22},{8,24},{10,26},{12,28},{14,30},{16,0},... | collective-permute-start | bytes 208904 | tf_op jit(solution)/shard_map/ppermute | solution.py:1197
  131.7 6.1 %collective-permute-start.23 = (bf16[136,256]{1,0:T(8,128)(2,1)S(1)}, bf16[136,256]{1,0:T(8,128)(2,1)S(1)}, u32[]{:S(2)}, u32[]{:S(2)}) collective-permute-start(bf16[136,256]{1,0:T(8,128)(2,1)S(1)} %get-tuple-element.176), channel_id=1, source_target_pairs={{0,24},{2,26},{4,28},{6,30},{8,16},{10,18},{12,20},{14,22},{16,8},... | collective-permute-start | bytes 208904 | tf_op jit(solution)/shard_map/ppermute | solution.py:1197
  132.3 7.2 %collective-permute-start.11 = (bf16[4,7,8,256]{3,2,1,0:T(8,128)(2,1)S(1)}, bf16[4,7,8,256]{3,2,1,0:T(8,128)(2,1)S(1)}, u32[]{:S(2)}, u32[]{:S(2)}) collective-permute-start(bf16[4,7,8,256]{3,2,1,0:T(8,128)(2,1)S(1)} %get-tuple-element.135), channel_id=1, source_target_pairs={{0,1},{1,0},{2,3},{3,2},{4,5},{5,4},{6,7},{7,6},{8,9},{9,8},{10,11... | collective-permute-start | bytes 344072 | tf_op jit(solution)/shard_map/ppermute | solution.py:1197
  132.3 10.1 %collective-permute-start.12 = (bf16[4,7,8,256]{3,2,1,0:T(8,128)(2,1)S(1)}, bf16[4,7,8,256]{3,2,1,0:T(8,128)(2,1)S(1)}, u32[]{:S(2)}, u32[]{:S(2)}) collective-permute-start(bf16[4,7,8,256]{3,2,1,0:T(8,128)(2,1)S(1)} %get-tuple-element.136), channel_id=1, source_target_pairs={{0,2},{1,3},{2,0},{3,1},{4,6},{5,7},{6,4},{7,5},{8,10},{9,11},{10,... | collective-permute-start | bytes 344072 | tf_op jit(solution)/shard_map/ppermute | solution.py:1197
  132.9 9.5 %collective-permute-start.13 = (bf16[4,7,8,256]{3,2,1,0:T(8,128)(2,1)S(1)}, bf16[4,7,8,256]{3,2,1,0:T(8,128)(2,1)S(1)}, u32[]{:S(2)}, u32[]{:S(2)}) collective-permute-start(bf16[4,7,8,256]{3,2,1,0:T(8,128)(2,1)S(1)} %get-tuple-element.137), channel_id=1, source_target_pairs={{0,3},{1,2},{2,1},{3,0},{4,7},{5,6},{6,5},{7,4},{8,11},{9,10},{10,... | collective-permute-start | bytes 344072 | tf_op jit(solution)/shard_map/ppermute | solution.py:1197
  137.9 6.4 %collective-permute-start.24 = (bf16[200,256]{1,0:T(8,128)(2,1)S(1)}, bf16[200,256]{1,0:T(8,128)(2,1)S(1)}, u32[]{:S(2)}, u32[]{:S(2)}) collective-permute-start(bf16[200,256]{1,0:T(8,128)(2,1)S(1)} %get-tuple-element.178), channel_id=1, source_target_pairs={{0,8},{2,10},{4,12},{6,14},{8,0},{10,2},{12,4},{14,6},{16,24},{18,... | collective-permute-start | bytes 307208 | tf_op jit(solution)/shard_map/ppermute | solution.py:1197
  138.0 8.8 %collective-permute-start.25 = (bf16[200,256]{1,0:T(8,128)(2,1)S(1)}, bf16[200,256]{1,0:T(8,128)(2,1)S(1)}, u32[]{:S(2)}, u32[]{:S(2)}) collective-permute-start(bf16[200,256]{1,0:T(8,128)(2,1)S(1)} %get-tuple-element.178), channel_id=1, source_target_pairs={{0,16},{2,18},{4,20},{6,22},{8,24},{10,26},{12,28},{14,30},{16,0},... | collective-permute-start | bytes 307208 | tf_op jit(solution)/shard_map/ppermute | solution.py:1197
  139.5 7.3 %collective-permute-start.26 = (bf16[200,256]{1,0:T(8,128)(2,1)S(1)}, bf16[200,256]{1,0:T(8,128)(2,1)S(1)}, u32[]{:S(2)}, u32[]{:S(2)}) collective-permute-start(bf16[200,256]{1,0:T(8,128)(2,1)S(1)} %get-tuple-element.178), channel_id=1, source_target_pairs={{0,24},{2,26},{4,28},{6,30},{8,16},{10,18},{12,20},{14,22},{16,8},... | collective-permute-start | bytes 307208 | tf_op jit(solution)/shard_map/ppermute | solution.py:1197
  146.9 24.2 %all-to-all-start.2 = ((bf16[32,7,8,256]{3,2,1,0:T(8,128)(2,1)}), bf16[32,7,8,256]{3,2,1,0:T(8,128)(2,1)S(1)}, u32[]{:S(2)}, u32[]{:S(2)}) async-start(bf16[32,7,8,256]{3,2,1,0:T(8,128)(2,1)} %split.1), calls=%async_computation.2 | async-start | bytes 1835008 | tf_op jit(solution)/shard_map/all_to_all | solution.py:1518
  150.7 12.4 %collective-permute-start.27 = (bf16[4,200,256]{2,1,0:T(8,128)(2,1)S(1)}, bf16[4,200,256]{2,1,0:T(8,128)(2,1)S(1)}, u32[]{:S(2)}, u32[]{:S(2)}) collective-permute-start(bf16[4,200,256]{2,1,0:T(8,128)(2,1)S(1)} %pad_maximum_fusion.refs_0_), channel_id=1, source_target_pairs={{0,2},{2,0},{4,6},{6,4},{8,10},{10,8},{12,14},{14,12},{16,18},{18,... | collective-permute-start | bytes 1228808 | tf_op jit(solution)/shard_map/ppermute | solution.py:1197
  151.3 26.3 %collective-permute-start.28 = (bf16[4,200,256]{2,1,0:T(8,128)(2,1)S(1)}, bf16[4,200,256]{2,1,0:T(8,128)(2,1)S(1)}, u32[]{:S(2)}, u32[]{:S(2)}) collective-permute-start(bf16[4,200,256]{2,1,0:T(8,128)(2,1)S(1)} %pad_maximum_fusion.refs_0_), channel_id=1, source_target_pairs={{0,4},{2,6},{4,0},{6,2},{8,12},{10,14},{12,8},{14,10},{16,20},{18,... | collective-permute-start | bytes 1228808 | tf_op jit(solution)/shard_map/ppermute | solution.py:1197
  153.3 24.2 %collective-permute-start.29 = (bf16[4,200,256]{2,1,0:T(8,128)(2,1)S(1)}, bf16[4,200,256]{2,1,0:T(8,128)(2,1)S(1)}, u32[]{:S(2)}, u32[]{:S(2)}) collective-permute-start(bf16[4,200,256]{2,1,0:T(8,128)(2,1)S(1)} %pad_maximum_fusion.refs_0_), channel_id=1, source_target_pairs={{0,6},{2,4},{4,2},{6,0},{8,14},{10,12},{12,10},{14,8},{16,22},{18,... | collective-permute-start | bytes 1228808 | tf_op jit(solution)/shard_map/ppermute | solution.py:1197
  156.3 21.7 %collective-permute-start.30 = (bf16[4,200,256]{2,1,0:T(8,128)(2,1)S(1)}, bf16[4,200,256]{2,1,0:T(8,128)(2,1)S(1)}, u32[]{:S(2)}, u32[]{:S(2)}) collective-permute-start(bf16[4,200,256]{2,1,0:T(8,128)(2,1)S(1)} %pad_maximum_fusion.refs_0_), channel_id=1, source_target_pairs={{0,1},{1,0},{2,3},{3,2},{4,5},{5,4},{6,7},{7,6},{8,9},{9,8},{10,11... | collective-permute-start | bytes 1228808 | tf_op jit(solution)/shard_map/ppermute | solution.py:1180
  163.1 14.9 %collective-permute-start.31 = (bf16[4,200,256]{2,1,0:T(8,128)(2,1)S(1)}, bf16[4,200,256]{2,1,0:T(8,128)(2,1)}, u32[]{:S(2)}, u32[]{:S(2)}) collective-permute-start(bf16[4,200,256]{2,1,0:T(8,128)(2,1)S(1)} %collective-permute-done.27.refs_1_), channel_id=1, source_target_pairs={{0,1},{1,0},{2,3},{3,2},{4,5},{5,4},{6,7},{7,6},{8,9},{9,8},{10,11... | collective-permute-start | bytes 1228808 | tf_op jit(solution)/shard_map/ppermute | solution.py:1180
  (35 other events, 665.7 us)
